TPU v7x, 512 devices: a whole 4x8x8 slice. The times are simulated.
512 devices in a mesh: chan: 16 (over y, z_hi), tm: 32 (over x, z_lo, core).
Axes of the slice: x: 4, y: 8, z: 8 (z_hi: 2, z_lo: 4; z = z_hi * 4 + z_lo), core: 2. Of those that a mesh axis runs over, the one named last changes fastest.
Arguments:
- voltage: bfloat16 [24576, 2, 16, 1024], P('tm', None, 'chan'), may hold values from -8 to 8, as said below
- taps: float32 [256], replicated, may hold values from -0.375 to 0.375
Outputs:
- visibility: float32 [16, 2, 1024, 8192], P('chan', None, None, 'tm')
Inputs may be any that keep to these rules, and one draw needn't show every extreme that they name: `voltage`: real and imaginary parts of sampled antenna voltages.
All inputs are finite; a program needn't handle non-finite values.
Results may differ from a plain program's by a relative error of at most 0.00068.
Values may be sent and summed in bfloat16 or wider, within the bound.
No kernel may reach another device: no remote copies, remote signals or barrier semaphores. Data moves between devices by JAX's collectives and lax.ppermute only.
A program may use at most 128 MiB of HBM per device.

v0:
```python
import jax
import jax.numpy as jnp
from jax import lax
from jax.sharding import PartitionSpec as P

FINE = 16
FOUT = 8
TAPS = 16


def shifted(array, axis, by):
    peers = lax.axis_size(axis)
    pairs = [(i, i + by) for i in range(peers) if 0 <= i + by < peers]
    return lax.ppermute(array, axis, pairs)


def swapped(block, axis, distance):
    count = lax.axis_size(axis)
    route = []
    for low in range(count):
        high = low | 1 << distance
        if high != low and high < count:
            route += [(low, high), (high, low)]
    return lax.ppermute(block, axis, route)


def coefficients(taps):
    fine_out = jnp.arange(FOUT, dtype=jnp.int32)
    fine_in = jnp.arange(FINE, dtype=jnp.int32)
    phase = (fine_out[:, None] * fine_in[None, :] % FINE).astype(jnp.float32) * (
        2.0 * jnp.pi / FINE
    )
    cosine = jnp.cos(phase)[:, :, None]
    sine_table = jnp.sin(phase)[:, :, None]
    tap_table = jnp.transpose(taps.reshape(TAPS, FINE))[None, :, :]
    real_row = jnp.stack([tap_table * cosine, tap_table * sine_table], 2)
    imag_row = jnp.stack([-tap_table * sine_table, tap_table * cosine], 2)
    coeff_table = jnp.stack([real_row, imag_row], 0)
    return coeff_table.reshape(2 * FOUT, FINE * 2, TAPS).astype(jnp.bfloat16)


def shards(voltage, taps):
    samples_here, _, chan_count, signals = voltage.shape
    frames_here = samples_here // FINE
    kernel = coefficients(taps)
    tail_rows = voltage[samples_here - (TAPS - 1) * FINE :]
    prior_rows = shifted(tail_rows, "tm", 1)
    padded = jnp.concatenate([prior_rows, voltage], 0)
    frame_input = padded.reshape(frames_here + TAPS - 1, FINE * 2, chan_count * signals)
    filtered = lax.conv_general_dilated(
        frame_input,
        kernel,
        (1,),
        "VALID",
        dimension_numbers=("WCN", "OIW", "WCN"),
        preferred_element_type=jnp.float32,
    )
    spectra = filtered.astype(jnp.bfloat16).reshape(frames_here, 2, FOUT, chan_count, signals)
    spectra = jnp.transpose(spectra, (0, 1, 3, 2, 4))
    devices = lax.axis_size("tm")
    group_size = devices // FOUT
    flat_spectra = spectra.reshape(frames_here, 2, chan_count, FOUT * signals)
    columns = lax.all_to_all(flat_spectra, "tm", split_axis=3, concat_axis=0, tiled=True)
    row_spectra = columns
    tm_place = lax.axis_index("tm")
    for bit_number in range(group_size.bit_length() - 1):
        partner = swapped(row_spectra, "tm", bit_number)
        upper_half = tm_place // (1 << bit_number) % 2 == 1
        row_spectra = jnp.where(
            upper_half,
            jnp.concatenate([partner, row_spectra], 3),
            jnp.concatenate([row_spectra, partner], 3),
        )
    rotated = jnp.stack([row_spectra, jnp.stack([-row_spectra[:, 1], row_spectra[:, 0]], 1)], 0)
    visibility_block = jnp.einsum(
        "pfrcj,frcs->cpjs", rotated, columns, preferred_element_type=jnp.float32
    )
    return visibility_block * (1.0 / (frames_here * devices))


def solution(mesh):
    in_specs = (P("tm", None, "chan", None), P())
    out_specs = P("chan", None, None, "tm")
    return jax.shard_map(shards, mesh=mesh, in_specs=in_specs, out_specs=out_specs, check_vma=False)
```

profile of v0, /device:TPU:1, one launch (start us, length us, event | category | flops | bytes accessed | tf_op | source)
XLA Modules:
  0.0 231.3 jit_solution(12469172421130486138)
XLA Ops:
  0.0 1.9 slice.9
  1.9 5.4 %collective-permute-start = (bf16[240,2,1,1024]{3,1,2,0:T(2,128)(2,1)S(1)}, bf16[240,2,1,1024]{3,1,2,0:T(2,128)(2,1)S(1)}, u32[]{:S(2)}, u32[]{:S(2)}) collective-permute-start(bf16[240,2,1,1024]{3,1,2,0:T(2,128)(2,1)S(1)} %slice.9), channel_id=1, source_target_pairs={{0,1},{1,2},{2,3},{3,4},{4,5},{5,6},{6,7},{7,8},{8,9},{9,10},{10,1... | collective-permute-start | bytes 2949128 | tf_op jit(solution)/shard_map/ppermute | solution.py:14
  7.3 0.8 reshape.374
  8.0 0.1 copy.23
  8.1 0.1 copy.24
  8.2 0.1 fusion.12
  8.3 0.1 multiply_convert_fusion.1
  8.4 0.2 copy.26
  8.6 9.7 %collective-permute-done = bf16[240,2,1,1024]{3,1,2,0:T(2,128)(2,1)S(1)} collective-permute-done((bf16[240,2,1,1024]{3,1,2,0:T(2,128)(2,1)S(1)}, bf16[240,2,1,1024]{3,1,2,0:T(2,128)(2,1)S(1)}, u32[]{:S(2)}, u32[]{:S(2)}) %collective-permute-start) | collective-permute-done | bytes 983072 | tf_op jit(solution)/shard_map/ppermute | solution.py:14
  18.3 9.1 %pad_maximum_fusion = bf16[1008,2,1,1024]{3,1,2,0:T(2,128)(2,1)} fusion(bf16[768,2,1,1024]{3,1,2,0:T(2,128)(2,1)} %param.2, bf16[240,2,1,1024]{3,1,2,0:T(2,128)(2,1)S(1)} %collective-permute-done), kind=kLoop, calls=%fused_computation.7 | loop fusion | flops 2064384 | bytes 8257536 | tf_op jit(solution)/shard_map/concatenate | solution.py:48
  27.4 9.5 %reshape.373 = bf16[63,32,1024]{2,1,0:T(8,128)(2,1)} reshape(bf16[1008,2,1,1024]{3,1,2,0:T(2,128)(2,1)} %pad_maximum_fusion) | data formatting | bytes 8257536 | tf_op jit(solution)/shard_map/reshape | solution.py:49
  36.9 8.5 %convolution_convert_fusion = bf16[48,16,1024]{2,1,0:T(8,128)(2,1)S(1)} fusion(bf16[63,32,1024]{2,1,0:T(8,128)(2,1)} %reshape.373, bf16[16,32,16]{1,0,2:T(8,128)(2,1)S(1)} %copy.26), kind=kOutput, calls=%fused_computation.13 | convolution fusion | flops 806092800 | bytes 5718016 | tf_op jit(solution)/shard_map/conv_general_dilated | solution.py:50
  45.4 1.2 reshape_transpose_reshape.3
  46.6 7.5 %copy.27 = bf16[48,2,1,8192]{0,1,2,3:T(2,128)(2,1)} copy(bf16[48,2,1,8192]{3,1,0,2:T(2,128)(2,1)S(1)} %reshape_transpose_reshape.3) | data formatting | bytes 3145728 | tf_op jit(solution)/shard_map/reshape;transpose;reshape | solution.py:62
  54.1 15.4 %reshape.378 = bf16[32,2,12288]{2,1,0:T(2,128)(2,1)S(1)} reshape(bf16[8192,1,2,48]{3,2,1,0:T(2,128)(2,1)} %bitcast.44) | data formatting | bytes 3145728
  69.4 49.5 %all_to_all.18 = bf16[32,2,12288]{2,1,0:T(2,128)(2,1)S(1)} all-to-all(bf16[32,2,12288]{2,1,0:T(2,128)(2,1)S(1)} %reshape.378), channel_id=1, replica_groups=mesh['chan'=16,'tm'=32] {'tm'}, dimensions={0} | all-to-all | bytes 3145728 | tf_op jit(solution)/shard_map/all_to_all | solution.py:63
  118.9 5.2 %reshape.379 = bf16[8192,1,2,48]{3,2,1,0:T(2,128)(2,1)} reshape(bf16[32,2,12288]{2,1,0:T(2,128)(2,1)S(1)} %all_to_all.18) | data formatting | bytes 3145728
  124.1 8.7 %copy.28 = bf16[48,2,1,32,256]{4,0,3,1,2:T(8,128)(2,1)S(1)} copy(bf16[48,2,1,32,256]{0,1,4,3,2:T(2,128)(2,1)} %bitcast.45) | data formatting | bytes 3145728 | tf_op jit(solution)/shard_map/all_to_all | solution.py:63
  132.8 2.1 collective-permute-start.1
  134.9 3.2 %collective-permute-done.1 = bf16[1536,2,1,256]{3,0,1,2:T(8,128)(2,1)S(1)} collective-permute-done((bf16[1536,2,1,256]{3,0,1,2:T(8,128)(2,1)S(1)}, bf16[1536,2,1,256]{3,0,1,2:T(8,128)(2,1)S(1)}, u32[]{:S(2)}, u32[]{:S(2)}) %collective-permute-start.1) | collective-permute-done | bytes 1572896 | tf_op jit(solution)/shard_map/ppermute | solution.py:24
  138.1 2.0 maximum_select_fusion.2
  140.1 1.9 collective-permute-start.2
  142.0 1.0 fusion.5
  143.0 68.8 %collective-permute-done.2 = bf16[1536,2,1,512]{3,0,1,2:T(8,128)(2,1)} collective-permute-done((bf16[1536,2,1,512]{3,0,1,2:T(8,128)(2,1)}, bf16[1536,2,1,512]{3,0,1,2:T(8,128)(2,1)}, u32[]{:S(2)}, u32[]{:S(2)}) %collective-permute-start.2) | collective-permute-done | bytes 3145760 | tf_op jit(solution)/shard_map/ppermute | solution.py:24
  211.8 4.6 %maximum_select_fusion.1 = bf16[1536,2,1,1024]{3,0,1,2:T(8,128)(2,1)S(1)} fusion(bf16[1536,2,1,512]{3,0,1,2:T(8,128)(2,1)S(1)} %get-tuple-element.8, bf16[1536,2,1,512]{3,0,1,2:T(8,128)(2,1)} %collective-permute-done.2, pred[]{:T(512)S(6)} %eq.11), kind=kLoop, calls=%fused_computation.5 | loop fusion | flops 28311552 | bytes 12582913 | tf_op jit(solution)/shard_map/jit(_where)/select_n | solution.py:69
  216.4 0.4 slice_negate_fusion
  216.8 4.6 %maximum_select_fusion = bf16[1,1536,2,1,1024]{4,1,2,3,0:T(8,128)(2,1)S(1)} fusion(bf16[1,1536,2,1,512]{4,1,2,3,0:T(8,128)(2,1)S(1)} %get-tuple-element.7, bf16[1,1536,2,1,512]{4,1,2,3,0:T(8,128)(2,1)} %bitcast.9, pred[]{:T(512)S(6)} %eq.11), kind=kLoop, calls=%fused_computation.4 | loop fusion | flops 28311552 | bytes 12582913 | tf_op jit(solution)/shard_map/jit(_where)/select_n | solution.py:69
  221.4 3.2 %maximum_bitcast_fusion.2 = bf16[1,1536,2,1,1024]{4,1,2,3,0:T(8,128)(2,1)} fusion(bf16[1536,1,1,1024]{3,0,1,2:T(8,128)(2,1)S(1)} %get-tuple-element.6, bf16[1536,1,1,1024]{3,0,1,2:T(8,128)(2,1)S(1)} %get-tuple-element.5), kind=kLoop, calls=%fused_computation.6 | loop fusion | flops 3145728 | bytes 12582912 | tf_op jit(solution)/shard_map/stack | solution.py:74
  224.6 6.7 %fusion.3 = f32[1,2,1024,256]{3,2,1,0:T(8,128)} fusion(bf16[1536,2,256,1]{2,0,1,3:T(8,128)(2,1)S(1)} %bitcast.49, bf16[1,1536,2,1,1024]{4,1,2,3,0:T(8,128)(2,1)} %maximum_bitcast_fusion.2, bf16[1,1536,2,1,1024]{4,1,2,3,0:T(8,128)(2,1)S(1)} %maximum_select_fusion), kind=kOutput, calls=%fused_computation.12 | convolution fusion | flops 3228041216 | bytes 16252928 | tf_op jit(solution)/shard_map/pfrcj,frcs->cpjs/dot_general | solution.py:75
  (3 shorter events, 0.1 us)
Async XLA Ops:
  1.9 16.4 %collective-permute-start = (bf16[240,2,1,1024]{3,1,2,0:T(2,128)(2,1)S(1)}, bf16[240,2,1,1024]{3,1,2,0:T(2,128)(2,1)S(1)}, u32[]{:S(2)}, u32[]{:S(2)}) collective-permute-start(bf16[240,2,1,1024]{3,1,2,0:T(2,128)(2,1)S(1)} %slice.9), channel_id=1, source_target_pairs={{0,1},{1,2},{2,3},{3,4},{4,5},{5,6},{6,7},{7,8},{8,9},{9,10},{10,1... | collective-permute-start | bytes 2949128 | tf_op jit(solution)/shard_map/ppermute | solution.py:14
  132.8 5.3 %collective-permute-start.1 = (bf16[1536,2,1,256]{3,0,1,2:T(8,128)(2,1)S(1)}, bf16[1536,2,1,256]{3,0,1,2:T(8,128)(2,1)S(1)}, u32[]{:S(2)}, u32[]{:S(2)}) collective-permute-start(bf16[1536,2,1,256]{3,0,1,2:T(8,128)(2,1)S(1)} %bitcast.46), channel_id=1, source_target_pairs={{0,1},{1,0},{2,3},{3,2},{4,5},{5,4},{6,7},{7,6},{8,9},{9,8},{10,11... | collective-permute-start | bytes 4718600 | tf_op jit(solution)/shard_map/ppermute | solution.py:24
  140.1 71.7 %collective-permute-start.2 = (bf16[1536,2,1,512]{3,0,1,2:T(8,128)(2,1)}, bf16[1536,2,1,512]{3,0,1,2:T(8,128)(2,1)}, u32[]{:S(2)}, u32[]{:S(2)}) collective-permute-start(bf16[1536,2,1,512]{3,0,1,2:T(8,128)(2,1)} %maximum_select_fusion.2), channel_id=1, source_target_pairs={{0,2},{2,0},{1,3},{3,1},{4,6},{6,4},{5,7},{7,5},{8,10},{10,8},{9,1... | collective-permute-start | bytes 9437192 | tf_op jit(solution)/shard_map/ppermute | solution.py:24
where the time goes:
time: 232 us; the launch traced here: 231 us
  waiting for transfers between devices  81.7 us (35%)
  local copies, waits for them, and re-layouts  50.3 us (22%)
  blocking collectives  49.5 us (21%)
  other arithmetic  25.1 us (11%)
  matrix products  15.2 us (7%)
  starting transfers between devices  9.36 us (4%)
    ppermute x2, waiting for transfers between devices, swapped(): return lax.ppermute(block, axis, route)  72 us
    all_to_all x1, blocking collectives, shards(): lax.all_to_all(flat_spectra, 'tm', split_axis=3, concat_axis=0, tiled=True)  49.5 us
    unnamed x2, local copies, waits for them, and re-layouts  20.5 us
    select_n x3, other arithmetic, shards(): jnp.where(upper_half, jnp.concatenate([partner, row_spectra], 3), jnp.con...  11.1 us
    ppermute x1, waiting for transfers between devices, shifted(): return lax.ppermute(array, axis, pairs)  9.67 us
    reshape x1, local copies, waits for them, and re-layouts, shards(): padded.reshape(frames_here + TAPS - 1, FINE * 2, chan_count * signals)  9.51 us
    concatenate x1, other arithmetic, shards(): padded = jnp.concatenate([prior_rows, voltage], 0)  9.12 us
    all_to_all x1, local copies, waits for them, and re-layouts, shards(): lax.all_to_all(flat_spectra, 'tm', split_axis=3, concat_axis=0, tiled=True)  8.69 us
  transfers between devices with their start and end apart: 3, of which 3 were waited for; matrix products, arithmetic and copies ran while one was open for 1% of the time, Pallas kernels for 0%

commit v1 on v0

v1 whole, which is shorter than its diff:
```python
import functools

import jax
import jax.numpy as jnp
import numpy as np
from jax import lax
from jax.experimental import pallas as pl
from jax.experimental.pallas import tpu as pltpu
from jax.sharding import PartitionSpec as P

FINE = 16
FOUT = 8
TAPS = 16
S = 1024
XS, ZS, CORES = 4, 4, 2
BLOCK = 16
ROWS = 2 * BLOCK
WINDOW = 2 * BLOCK * FINE
VMEM = pltpu.VMEM
F32 = jnp.float32
BF16 = jnp.bfloat16


def place(x, z, c):
    return (x * ZS + z) * CORES + c


def moves(rule):
    out = []
    for x in range(XS):
        for z in range(ZS):
            for c in range(CORES):
                out.append((place(x, z, c), place(*rule(x, z, c))))
    return out


def move(array, rule):
    return lax.ppermute(array, "tm", moves(rule))


def along_x(distance):
    return lambda x, z, c: ((x + distance) % XS, z, c)


def far_z(x, z, c):
    return x, z ^ 2, c


def near_z(x, z, c):
    return x, z ^ 1, c


def other_core(x, z, c):
    return x, z, 1 - c


def halo_of(tail):
    pairs = [(i, i + 1) for i in range(XS * ZS * CORES - 1)]
    return lax.ppermute(tail, "tm", pairs)


def trig_table():
    k = np.arange(FOUT)[:, None]
    n = np.arange(FINE)[None, :]
    phase = (k * n % FINE) * (2.0 * np.pi / FINE)
    c, s = np.cos(phase), np.sin(phase)
    real_row = np.stack([c, s], -1).reshape(FOUT, 2 * FINE)
    imag_row = np.stack([-s, c], -1).reshape(FOUT, 2 * FINE)
    rows = np.stack([real_row, imag_row], 1).reshape(2 * FOUT, 2 * FINE)
    return np.tile(rows.astype(np.float32), (1, 2 * BLOCK))


def spec(n):
    return [pl.BlockSpec(memory_space=VMEM)] * n


def shape(*dims, kind=BF16):
    return jax.ShapeDtypeStruct(dims, kind)


def band_matrix(taps_ref, trig_ref, band_ref):
    me = lax.axis_index("tm")
    x = me // (ZS * CORES)
    odd = me // 4 % 2
    width = 2 * WINDOW
    taps_len = TAPS * FINE
    row = lax.broadcasted_iota(jnp.int32, (taps_len, width), 0)
    col = lax.broadcasted_iota(jnp.int32, (taps_len, width), 1)
    pick = (col // 2 == row).astype(F32)
    taps = jnp.broadcast_to(taps_ref[...], (BLOCK, taps_len))
    twice = lax.dot_general(
        taps, pick, (((1,), (0,)), ((), ())), precision=lax.Precision.HIGHEST, preferred_element_type=F32
    )
    frame = lax.broadcasted_iota(jnp.int32, (BLOCK, width), 0)
    shifted = jnp.zeros((BLOCK, width), F32)
    for f in range(BLOCK):
        shifted = jnp.where(frame == f, pltpu.roll(twice, 2 * FINE * (f + 1) % width, 1), shifted)
    for d in range(XS):
        for other in range(2):
            k = (x + d) % XS * 2 + (odd + other) % 2
            for ro in range(2):
                at = ((d * 2 + other) * 2 + ro) * BLOCK
                wave = trig_ref[pl.ds(k * 2 + ro, 1), :]
                band_ref[at : at + BLOCK, :] = (shifted * wave).astype(BF16)


def filter_late(taps_ref, trig_ref, volt_ref, band_ref, m0, m1, m2, m3, t_ref):
    band_matrix(taps_ref, trig_ref, band_ref)
    mine = (m0, m1, m2, m3)
    for i in range(2):
        start = i * BLOCK * FINE
        window = volt_ref[start : start + WINDOW].reshape(2 * WINDOW, S)
        out = jnp.dot(band_ref[...], window, preferred_element_type=F32).astype(BF16)
        rows = slice(i * ROWS, (i + 1) * ROWS)
        for d in range(XS):
            mine[d][rows, :] = out[2 * d * ROWS : (2 * d + 1) * ROWS]
            t_ref[d, rows, :] = out[(2 * d + 1) * ROWS : (2 * d + 2) * ROWS]


def filter_first(halo_ref, volt_ref, band_ref, m_ref, t_ref):
    here = BLOCK * FINE
    own = volt_ref[0:here].reshape(2 * here, S)
    prior = halo_ref[...].reshape(2 * here - 2 * FINE, S)
    band = band_ref[...]
    out = jnp.dot(band[:, 2 * here :], own, preferred_element_type=F32)
    out += jnp.dot(band[:, 2 * FINE : 2 * here], prior, preferred_element_type=F32)
    out = out.astype(BF16)
    for d in range(XS):
        m_ref[d] = out[2 * d * ROWS : (2 * d + 1) * ROWS]
        t_ref[d] = out[(2 * d + 1) * ROWS : (2 * d + 2) * ROWS]


def products(n_pieces, scale, *refs):
    pieces, rest = refs[:n_pieces], refs[n_pieces:]
    out_ref = rest[-1]
    j = pl.program_id(0)
    quarter = lax.axis_index("tm") % 4
    cols = pl.ds(pl.multiple_of(quarter * 256, 256), 256)
    rows = pl.ds(pl.multiple_of(j * 256, 256), 256)
    total = None
    for piece in pieces:
        n = piece.shape[0]
        here = piece[:, cols]
        halves = here.reshape(n // ROWS, 2, BLOCK, 256)
        turned = jnp.stack([halves[:, 1], -halves[:, 0]], 1).reshape(n, 256)
        both = jnp.concatenate([here, turned], 1)
        part = lax.dot_general(
            piece[:, rows], both, (((0,), (0,)), ((), ())), preferred_element_type=F32
        )
        total = part if total is None else total + part
    real, imag = total[:, :256], total[:, 256:]
    if len(rest) > 1:
        real += rest[0][0]
        imag += rest[0][1]
    if scale is not None:
        real, imag = real * scale, imag * scale
    out_ref[0] = real
    out_ref[1] = imag


def correlate(pieces, acc, scale=None):
    frames = sum(p.shape[0] for p in pieces)
    block = pl.BlockSpec((2, 256, 256), lambda j: (0, j, 0))
    more = [] if acc is None else [acc]
    return pl.pallas_call(
        functools.partial(products, len(pieces), scale),
        grid=(4,),
        out_shape=shape(2, S, 256, kind=F32),
        in_specs=[pl.BlockSpec(p.shape, lambda j: (0, 0), memory_space=VMEM, pipeline_mode=pl.Buffered(1)) for p in pieces]
        + [block] * len(more),
        out_specs=block,
        compiler_params=pltpu.CompilerParams(vmem_limit_bytes=40 << 20),
        cost_estimate=pl.CostEstimate(flops=2 * frames * S * 512, bytes_accessed=4 << 20, transcendentals=0),
    )(*pieces, *more)


def shards(voltage, taps):
    samples_here = voltage.shape[0]
    late = 2 * BLOCK
    volt = voltage.reshape(samples_here, 2, S)
    halo = halo_of(volt[samples_here - (TAPS - 1) * FINE :])
    params = pltpu.CompilerParams(vmem_limit_bytes=40 << 20)
    band, ma0, ma1, ma2, ma3, ta = pl.pallas_call(
        filter_late,
        out_shape=(
            shape(4 * FOUT * BLOCK // 2, 2 * WINDOW),
            *[shape(2 * late, S)] * 4,
            shape(XS, 2 * late, S),
        ),
        in_specs=spec(3),
        out_specs=spec(6),
        compiler_params=params,
        cost_estimate=pl.CostEstimate(flops=2 << 29, bytes_accessed=6 << 20, transcendentals=0),
    )(taps.reshape(1, -1), jnp.asarray(trig_table()), volt)
    ta = move(ta, far_z)
    ma = [ma0] + [move(m, along_x(d)) for d, m in ((1, ma1), (2, ma2), (3, ma3))]
    mb, tb = pl.pallas_call(
        filter_first,
        out_shape=(shape(XS, ROWS, S), shape(XS, ROWS, S)),
        in_specs=spec(3),
        out_specs=spec(2),
        compiler_params=params,
        cost_estimate=pl.CostEstimate(flops=1 << 29, bytes_accessed=3 << 20, transcendentals=0),
    )(halo, volt, band)
    tb = move(tb, far_z)
    ma = jnp.concatenate(ma, 0)
    ma = jnp.concatenate([ma, move(ma, near_z)], 0)
    second = [jnp.concatenate([ta[d], mb[d]], 0) for d in range(XS)]
    second = [second[0]] + [move(second[d], along_x(d)) for d in range(1, XS)]
    second = jnp.concatenate(second, 0)
    third = [tb[0]] + [move(tb[d], along_x(d)) for d in range(1, XS)]
    third = jnp.concatenate(third, 0)
    second = jnp.concatenate([second, move(second, near_z)], 0)
    third_near = move(third, near_z)
    acc = correlate([ma, move(ma, other_core)], None)
    acc = correlate([second, move(second, other_core)], acc)
    pieces = [third, move(third, other_core), third_near, move(third_near, other_core)]
    frames = samples_here // FINE * XS * ZS * CORES
    return correlate(pieces, acc, 1.0 / frames)[None]


def solution(mesh):
    in_specs = (P("tm", None, "chan", None), P())
    out_specs = P("chan", None, None, "tm")
    return jax.shard_map(shards, mesh=mesh, in_specs=in_specs, out_specs=out_specs, check_vma=False)
```

time: 232 us -> 147 us (0.63)
  starting transfers between devices: 9.36 us -> 73.3 us
  blocking collectives: 49.5 us -> 0 us
  local copies, waits for them, and re-layouts: 50.3 us -> 4.42 us
  other arithmetic: 25.1 us -> 0.1 us
  waiting for transfers between devices: 81.7 us -> 57.5 us
  matrix products: 15.2 us -> 0 us
  Pallas kernels: 0 us -> 10.4 us
    ppermute x3 -> x19, starting transfers between devices: 9.36 us -> 73.3 us  [the longest x18 68.4 us: move(): return lax.ppermute(array, 'tm', moves(rule))]
    all_to_all x1 -> x0, blocking collectives: 49.5 us -> none  [shards(): lax.all_to_all(flat_spectra, 'tm', split_axis=3, concat_axis=0, tiled=True)]
    ppermute x3 -> x19, waiting for transfers between devices: 81.7 us -> 57.5 us  [the longest x18 57.5 us: move(): return lax.ppermute(array, 'tm', moves(rule))]
    unnamed x2 -> x16, local copies, waits for them, and re-layouts: 20.5 us -> 3.56 us
    select_n x3 -> x0, other arithmetic: 11.1 us -> none  [shards(): jnp.where(upper_half, jnp.concatenate([partner, row_spectra], 3), jnp.con...]
    pallas_call x0 -> x5, Pallas kernels: none -> 10.4 us  [the longest x3 7.92 us: correlate(): pl.pallas_call(functools.partial(products, len(pieces), scale), grid=(4,)...]
    reshape x2 -> x0, local copies, waits for them, and re-layouts: 10.3 us -> none  [the longest x1 9.51 us: shards(): padded.reshape(frames_here + TAPS - 1, FINE * 2, chan_count * signals)]
    concatenate x2 -> x5, other arithmetic: 10.1 us -> 0.1 us  [the longest x3 0.05 us: shards(): second = [jnp.concatenate([ta[d], mb[d]], 0) for d in range(XS)]]
  transfers between devices with their start and end apart: 3 -> 19, of which waited for: 3 -> 11; matrix products, arithmetic and copies ran while one was open for 1% -> 1% of each run, Pallas kernels for 0% -> 3%
where the time goes in v1:
time: 147 us; the launch traced here: 146 us
  starting transfers between devices  73.3 us (50%)
  waiting for transfers between devices  57.5 us (39%)
  Pallas kernels  10.4 us (7%)
  local copies, waits for them, and re-layouts  4.42 us (3%)
    ppermute x18, starting transfers between devices, move(): return lax.ppermute(array, 'tm', moves(rule))  68.4 us
    ppermute x18, waiting for transfers between devices, move(): return lax.ppermute(array, 'tm', moves(rule))  57.5 us
    pallas_call x3, Pallas kernels, correlate(): pl.pallas_call(functools.partial(products, len(pieces), scale), grid=(4,)...  7.92 us
    ppermute x1, starting transfers between devices, halo_of(): return lax.ppermute(tail, 'tm', pairs)  4.97 us
    unnamed x16, local copies, waits for them, and re-layouts  3.56 us
  transfers between devices with their start and end apart: 19, of which 11 were waited for; matrix products, arithmetic and copies ran while one was open for 1% of the time, Pallas kernels for 3%

profile of v1, /device:TPU:1, one launch (start us, length us, event | category | flops | bytes accessed | tf_op | source)
XLA Modules:
  0.0 146.2 jit_solution(7453677986053078560)
XLA Ops:
  0.0 1.9 %copy-done = bf16[768,2,1,1024]{3,1,2,0:T(2,128)(2,1)S(1)} copy-done((bf16[768,2,1,1024]{3,1,2,0:T(2,128)(2,1)S(1)}, bf16[768,2,1,1024]{3,1,2,0:T(2,128)(2,1)}, u32[]{:S(2)}) %copy-start) | copy-done | bytes 3145752
  1.9 0.7 copy-done.2
  2.6 0.8 copy-done.3
  3.4 1.7 %shard_map.37 = (bf16[256,1024]{1,0:T(8,128)(2,1)S(1)}, bf16[64,1024]{1,0:T(8,128)(2,1)S(1)}, bf16[64,1024]{1,0:T(8,128)(2,1)S(1)}, bf16[64,1024]{1,0:T(8,128)(2...) custom-call(f32[1,256]{1,0:T(1,128)S(1)} %bitcast.38, f32[16,1024]{1,0:T(8,128)S(1)} %copy-done.3, ...), custom_call_target="tpu_custom_call" | custom-call | flops 1073741824 | bytes 6291456 | tf_op jit(solution)/shard_map/pallas_call | solution.py:183
  5.2 6.6 %collective-permute-start.8 = (bf16[4,64,1024]{2,1,0:T(8,128)(2,1)S(1)}, bf16[4,64,1024]{2,1,0:T(8,128)(2,1)S(1)}, u32[]{:S(2)}, u32[]{:S(2)}) collective-permute-start(bf16[4,64,1024]{2,1,0:T(8,128)(2,1)S(1)} %get-tuple-element.15), channel_id=1, source_target_pairs={{0,4},{1,5},{2,6},{3,7},{4,0},{5,1},{6,2},{7,3},{8,12},{9,13},{10,... | collective-permute-start | bytes 1572872 | tf_op jit(solution)/shard_map/ppermute | solution.py:38
  11.8 0.0 copy-start.1
  11.8 0.7 slice_bitcast_fusion
  12.5 5.0 %collective-permute-start = (bf16[240,2,1024]{2,1,0:T(2,128)(2,1)S(1)}, bf16[240,2,1024]{2,1,0:T(2,128)(2,1)S(1)}, u32[]{:S(2)}, u32[]{:S(2)}) collective-permute-start(bf16[240,2,1024]{2,1,0:T(2,128)(2,1)S(1)} %slice_bitcast_fusion), channel_id=1, source_target_pairs={{0,1},{1,2},{2,3},{3,4},{4,5},{5,6},{6,7},{7,8},{8,9},{9,10},{10,1... | collective-permute-start | bytes 2949128 | tf_op jit(solution)/shard_map/ppermute | solution.py:59
  17.5 26.6 %collective-permute-done.8 = bf16[4,64,1024]{2,1,0:T(8,128)(2,1)S(1)} collective-permute-done((bf16[4,64,1024]{2,1,0:T(8,128)(2,1)S(1)}, bf16[4,64,1024]{2,1,0:T(8,128)(2,1)S(1)}, u32[]{:S(2)}, u32[]{:S(2)}) %collective-permute-start.8) | collective-permute-done | bytes 524320 | tf_op jit(solution)/shard_map/ppermute | solution.py:38
  44.1 0.0 collective-permute-done.halo_ref
  44.2 0.8 shard_map.38
  45.0 4.3 %collective-permute-start.9 = (bf16[96,1024]{1,0:T(8,128)(2,1)S(1)}, bf16[96,1024]{1,0:T(8,128)(2,1)S(1)}, u32[]{:S(2)}, u32[]{:S(2)}) collective-permute-start(bf16[96,1024]{1,0:T(8,128)(2,1)S(1)} %pad_maximum_fusion.2), channel_id=1, source_target_pairs={{0,8},{1,9},{2,10},{3,11},{4,12},{5,13},{6,14},{7,15},{8,16},{9,17... | collective-permute-start | bytes 589832 | tf_op jit(solution)/shard_map/ppermute | solution.py:38
  49.3 3.5 %collective-permute-start.10 = (bf16[96,1024]{1,0:T(8,128)(2,1)S(1)}, bf16[96,1024]{1,0:T(8,128)(2,1)S(1)}, u32[]{:S(2)}, u32[]{:S(2)}) collective-permute-start(bf16[96,1024]{1,0:T(8,128)(2,1)S(1)} %pad_maximum_fusion.3), channel_id=1, source_target_pairs={{0,16},{1,17},{2,18},{3,19},{4,20},{5,21},{6,22},{7,23},{8,24},{9,... | collective-permute-start | bytes 589832 | tf_op jit(solution)/shard_map/ppermute | solution.py:38
  52.7 4.0 %collective-permute-start.11 = (bf16[96,1024]{1,0:T(8,128)(2,1)S(1)}, bf16[96,1024]{1,0:T(8,128)(2,1)S(1)}, u32[]{:S(2)}, u32[]{:S(2)}) collective-permute-start(bf16[96,1024]{1,0:T(8,128)(2,1)S(1)} %pad_maximum_fusion.4), channel_id=1, source_target_pairs={{0,24},{1,25},{2,26},{3,27},{4,28},{5,29},{6,30},{7,31},{8,0},{9,1... | collective-permute-start | bytes 589832 | tf_op jit(solution)/shard_map/ppermute | solution.py:38
  56.7 0.0 collective-permute-done.9
  56.8 2.4 %collective-permute-done.10 = bf16[96,1024]{1,0:T(8,128)(2,1)S(1)} collective-permute-done((bf16[96,1024]{1,0:T(8,128)(2,1)S(1)}, bf16[96,1024]{1,0:T(8,128)(2,1)S(1)}, u32[]{:S(2)}, u32[]{:S(2)}) %collective-permute-start.10) | collective-permute-done | bytes 196640 | tf_op jit(solution)/shard_map/ppermute | solution.py:38
  59.3 2.3 %collective-permute-done.11 = bf16[96,1024]{1,0:T(8,128)(2,1)S(1)} collective-permute-done((bf16[96,1024]{1,0:T(8,128)(2,1)S(1)}, bf16[96,1024]{1,0:T(8,128)(2,1)S(1)}, u32[]{:S(2)}, u32[]{:S(2)}) %collective-permute-start.11) | collective-permute-done | bytes 196640 | tf_op jit(solution)/shard_map/ppermute | solution.py:38
  61.6 1.9 %collective-permute-start.12 = (bf16[384,1024]{1,0:T(8,128)(2,1)S(1)}, bf16[384,1024]{1,0:T(8,128)(2,1)S(1)}, u32[]{:S(2)}, u32[]{:S(2)}) collective-permute-start(bf16[384,1024]{1,0:T(8,128)(2,1)S(1)} %get-tuple-element.35), channel_id=1, source_target_pairs={{0,2},{1,3},{2,0},{3,1},{4,6},{5,7},{6,4},{7,5},{8,10},{9,11},{10,... | collective-permute-start | bytes 2359304 | tf_op jit(solution)/shard_map/ppermute | solution.py:38
  63.5 4.6 %collective-permute-start.14 = (bf16[64,1024]{1,0:T(8,128)(2,1)S(1)}, bf16[64,1024]{1,0:T(8,128)(2,1)S(1)}, u32[]{:S(2)}, u32[]{:S(2)}) collective-permute-start(bf16[64,1024]{1,0:T(8,128)(2,1)S(1)} %get-tuple-element.18), channel_id=1, source_target_pairs={{0,8},{1,9},{2,10},{3,11},{4,12},{5,13},{6,14},{7,15},{8,16},{9,17... | collective-permute-start | bytes 393224 | tf_op jit(solution)/shard_map/ppermute | solution.py:38
  68.1 2.8 %collective-permute-start.15 = (bf16[64,1024]{1,0:T(8,128)(2,1)S(1)}, bf16[64,1024]{1,0:T(8,128)(2,1)S(1)}, u32[]{:S(2)}, u32[]{:S(2)}) collective-permute-start(bf16[64,1024]{1,0:T(8,128)(2,1)S(1)} %get-tuple-element.19), channel_id=1, source_target_pairs={{0,16},{1,17},{2,18},{3,19},{4,20},{5,21},{6,22},{7,23},{8,24},{9,... | collective-permute-start | bytes 393224 | tf_op jit(solution)/shard_map/ppermute | solution.py:38
  71.0 3.4 %collective-permute-start.16 = (bf16[64,1024]{1,0:T(8,128)(2,1)S(1)}, bf16[64,1024]{1,0:T(8,128)(2,1)S(1)}, u32[]{:S(2)}, u32[]{:S(2)}) collective-permute-start(bf16[64,1024]{1,0:T(8,128)(2,1)S(1)} %get-tuple-element.20), channel_id=1, source_target_pairs={{0,24},{1,25},{2,26},{3,27},{4,28},{5,29},{6,30},{7,31},{8,0},{9,1... | collective-permute-start | bytes 393224 | tf_op jit(solution)/shard_map/ppermute | solution.py:38
  74.4 0.0 collective-permute-done.14
  74.4 1.0 collective-permute-done.15
  75.4 1.6 %collective-permute-done.16 = bf16[64,1024]{1,0:T(8,128)(2,1)S(1)} collective-permute-done((bf16[64,1024]{1,0:T(8,128)(2,1)S(1)}, bf16[64,1024]{1,0:T(8,128)(2,1)S(1)}, u32[]{:S(2)}, u32[]{:S(2)}) %collective-permute-start.16) | collective-permute-done | bytes 131104 | tf_op jit(solution)/shard_map/ppermute | solution.py:38
  77.0 3.6 %collective-permute-start.17 = (bf16[256,1024]{1,0:T(8,128)(2,1)S(1)}, bf16[256,1024]{1,0:T(8,128)(2,1)S(1)}, u32[]{:S(2)}, u32[]{:S(2)}) collective-permute-start(bf16[256,1024]{1,0:T(8,128)(2,1)S(1)} %pad_maximum_fusion), channel_id=1, source_target_pairs={{0,2},{1,3},{2,0},{3,1},{4,6},{5,7},{6,4},{7,5},{8,10},{9,11},{10,... | collective-permute-start | bytes 1572872 | tf_op jit(solution)/shard_map/ppermute | solution.py:38
  80.7 0.3 collective-permute-done.12
  80.9 0.1 constant_dynamic-update-slice_fusion.3.refs_0_
  81.0 5.5 %collective-permute-start.13 = (bf16[768,1024]{1,0:T(8,128)(2,1)S(1)}, bf16[768,1024]{1,0:T(8,128)(2,1)S(1)}, u32[]{:S(2)}, u32[]{:S(2)}) collective-permute-start(bf16[768,1024]{1,0:T(8,128)(2,1)S(1)} %constant_dynamic-update-slice_fusion.3.refs_0_), channel_id=1, source_target_pairs={{0,1},{1,0},{2,3},{3,2},{4,5},{5,4},{6,7},{7,6},{8,9},{9,8},{10,11... | collective-permute-start | bytes 4718600 | tf_op jit(solution)/shard_map/ppermute | solution.py:38
  86.6 5.2 %collective-permute-done.17 = bf16[256,1024]{1,0:T(8,128)(2,1)S(1)} collective-permute-done((bf16[256,1024]{1,0:T(8,128)(2,1)S(1)}, bf16[256,1024]{1,0:T(8,128)(2,1)S(1)}, u32[]{:S(2)}, u32[]{:S(2)}) %collective-permute-start.17) | collective-permute-done | bytes 524320 | tf_op jit(solution)/shard_map/ppermute | solution.py:38
  91.8 4.8 %collective-permute-start.18 = (bf16[512,1024]{1,0:T(8,128)(2,1)S(1)}, bf16[512,1024]{1,0:T(8,128)(2,1)S(1)}, u32[]{:S(2)}, u32[]{:S(2)}) collective-permute-start(bf16[512,1024]{1,0:T(8,128)(2,1)S(1)} %constant_dynamic-update-slice_fusion.7.refs_0_), channel_id=1, source_target_pairs={{0,1},{1,0},{2,3},{3,2},{4,5},{5,4},{6,7},{7,6},{8,9},{9,8},{10,11... | collective-permute-start | bytes 3145736 | tf_op jit(solution)/shard_map/ppermute | solution.py:38
  96.6 1.9 %collective-permute-start.1 = (bf16[4,32,1024]{2,1,0:T(8,128)(2,1)S(1)}, bf16[4,32,1024]{2,1,0:T(8,128)(2,1)S(1)}, u32[]{:S(2)}, u32[]{:S(2)}) collective-permute-start(bf16[4,32,1024]{2,1,0:T(8,128)(2,1)S(1)} %get-tuple-element.14), channel_id=1, source_target_pairs={{0,4},{1,5},{2,6},{3,7},{4,0},{5,1},{6,2},{7,3},{8,12},{9,13},{10,... | collective-permute-start | bytes 786440 | tf_op jit(solution)/shard_map/ppermute | solution.py:38
  98.6 14.7 %collective-permute-done.1 = bf16[4,32,1024]{2,1,0:T(8,128)(2,1)S(1)} collective-permute-done((bf16[4,32,1024]{2,1,0:T(8,128)(2,1)S(1)}, bf16[4,32,1024]{2,1,0:T(8,128)(2,1)S(1)}, u32[]{:S(2)}, u32[]{:S(2)}) %collective-permute-start.1) | collective-permute-done | bytes 262176 | tf_op jit(solution)/shard_map/ppermute | solution.py:38
  113.3 4.4 %collective-permute-start.2 = (bf16[32,1024]{1,0:T(8,128)(2,1)S(1)}, bf16[32,1024]{1,0:T(8,128)(2,1)S(1)}, u32[]{:S(2)}, u32[]{:S(2)}) collective-permute-start(bf16[32,1024]{1,0:T(8,128)(2,1)S(1)} %get-tuple-element.34), channel_id=1, source_target_pairs={{0,8},{1,9},{2,10},{3,11},{4,12},{5,13},{6,14},{7,15},{8,16},{9,17... | collective-permute-start | bytes 196616 | tf_op jit(solution)/shard_map/ppermute | solution.py:38
  117.7 2.9 %collective-permute-start.3 = (bf16[32,1024]{1,0:T(8,128)(2,1)S(1)}, bf16[32,1024]{1,0:T(8,128)(2,1)S(1)}, u32[]{:S(2)}, u32[]{:S(2)}) collective-permute-start(bf16[32,1024]{1,0:T(8,128)(2,1)S(1)} %get-tuple-element.33), channel_id=1, source_target_pairs={{0,16},{1,17},{2,18},{3,19},{4,20},{5,21},{6,22},{7,23},{8,24},{9,... | collective-permute-start | bytes 196616 | tf_op jit(solution)/shard_map/ppermute | solution.py:38
  120.6 3.3 %collective-permute-start.4 = (bf16[32,1024]{1,0:T(8,128)(2,1)S(1)}, bf16[32,1024]{1,0:T(8,128)(2,1)S(1)}, u32[]{:S(2)}, u32[]{:S(2)}) collective-permute-start(bf16[32,1024]{1,0:T(8,128)(2,1)S(1)} %get-tuple-element.32), channel_id=1, source_target_pairs={{0,24},{1,25},{2,26},{3,27},{4,28},{5,29},{6,30},{7,31},{8,0},{9,1... | collective-permute-start | bytes 196616 | tf_op jit(solution)/shard_map/ppermute | solution.py:38
  123.9 0.0 collective-permute-done.2
  123.9 0.3 collective-permute-done.3
  124.2 1.5 %collective-permute-done.4 = bf16[32,1024]{1,0:T(8,128)(2,1)S(1)} collective-permute-done((bf16[32,1024]{1,0:T(8,128)(2,1)S(1)}, bf16[32,1024]{1,0:T(8,128)(2,1)S(1)}, u32[]{:S(2)}, u32[]{:S(2)}) %collective-permute-start.4) | collective-permute-done | bytes 65568 | tf_op jit(solution)/shard_map/ppermute | solution.py:38
  125.7 1.9 %collective-permute-start.6 = (bf16[128,1024]{1,0:T(8,128)(2,1)S(1)}, bf16[128,1024]{1,0:T(8,128)(2,1)S(1)}, u32[]{:S(2)}, u32[]{:S(2)}) collective-permute-start(bf16[128,1024]{1,0:T(8,128)(2,1)S(1)} %pad_maximum_fusion.1.refs_0_), channel_id=1, source_target_pairs={{0,2},{1,3},{2,0},{3,1},{4,6},{5,7},{6,4},{7,5},{8,10},{9,11},{10,... | collective-permute-start | bytes 786440 | tf_op jit(solution)/shard_map/ppermute | solution.py:38
  127.6 4.0 %collective-permute-start.5 = (bf16[128,1024]{1,0:T(8,128)(2,1)S(1)}, bf16[128,1024]{1,0:T(8,128)(2,1)S(1)}, u32[]{:S(2)}, u32[]{:S(2)}) collective-permute-start(bf16[128,1024]{1,0:T(8,128)(2,1)S(1)} %pad_maximum_fusion.1.refs_0_), channel_id=1, source_target_pairs={{0,1},{1,0},{2,3},{3,2},{4,5},{5,4},{6,7},{7,6},{8,9},{9,8},{10,11... | collective-permute-start | bytes 786440 | tf_op jit(solution)/shard_map/ppermute | solution.py:38
  131.6 1.7 %collective-permute-done.6.refs_2_ = bf16[128,1024]{1,0:T(8,128)(2,1)S(1)} collective-permute-done((bf16[128,1024]{1,0:T(8,128)(2,1)S(1)}, bf16[128,1024]{1,0:T(8,128)(2,1)S(1)}, u32[]{:S(2)}, u32[]{:S(2)}) %collective-permute-start.6) | collective-permute-done | bytes 262176 | tf_op jit(solution)/shard_map/ppermute | solution.py:38
  133.3 4.9 %collective-permute-start.7 = (bf16[128,1024]{1,0:T(8,128)(2,1)S(1)}, bf16[128,1024]{1,0:T(8,128)(2,1)S(1)}, u32[]{:S(2)}, u32[]{:S(2)}) collective-permute-start(bf16[128,1024]{1,0:T(8,128)(2,1)S(1)} %collective-permute-done.6.refs_2_), channel_id=1, source_target_pairs={{0,1},{1,0},{2,3},{3,2},{4,5},{5,4},{6,7},{7,6},{8,9},{9,8},{10,11... | collective-permute-start | bytes 786440 | tf_op jit(solution)/shard_map/ppermute | solution.py:38
  138.2 0.0 collective-permute-done.18.refs_1_
  138.2 2.0 %shard_map.39.refs_2_ = f32[2,1024,256]{2,1,0:T(8,128)S(1)} custom-call(bf16[512,1024]{1,0:T(8,128)(2,1)S(1)} %constant_dynamic-update-slice_fusion.7.refs_0_, bf16[512,1024]{1,0:T(8,128)(2,1)S(1)} %collective-permute-done.18.refs_1_), custom_call_target="tpu_custom_call" | custom-call | flops 1073741824 | bytes 4194304 | tf_op jit(solution)/shard_map/pallas_call | solution.py:165
  140.3 2.8 %shard_map.40.refs_4_ = f32[2,1024,256]{2,1,0:T(8,128)S(1)} custom-call(bf16[768,1024]{1,0:T(8,128)(2,1)S(1)} %constant_dynamic-update-slice_fusion.3.refs_0_, bf16[768,1024]{1,0:T(8,128)(2,1)S(1)} %collective-permute-done.13.refs_1_, f32[2,1024,256]{2,1,0:T(8,128)S(1)} %shard_map.39.refs_2_), custom_call_target="tpu_custom_call" | custom-call | flops 1610612736 | bytes 4194304 | tf_op jit(solution)/shard_map/pallas_call | solution.py:165
  143.1 0.0 collective-permute-done.5.refs_1_
  143.1 0.0 collective-permute-done.7.refs_3_
  143.1 3.1 %shard_map.41 = f32[2,1024,256]{2,1,0:T(8,128)} custom-call(bf16[128,1024]{1,0:T(8,128)(2,1)S(1)} %pad_maximum_fusion.1.refs_0_, bf16[128,1024]{1,0:T(8,128)(2,1)S(1)} %collective-permute-done.5.refs_1_, bf16[128,1024]{1,0:T(8,128)(2,1)S(1)} %collective-permute-done.6.refs_2_, bf16[128,1024]{1,0:T(8,128)(2,1)S(1)} %collective-permute-done.7.refs_3_, ...), custom_call_target="tpu_custom_call" | custom-call | flops 536870912 | bytes 4194304 | tf_op jit(solution)/shard_map/pallas_call | solution.py:165
  (23 shorter events, 0.4 us)
Async XLA Ops:
  0.0 1.9 %copy-start = (bf16[768,2,1,1024]{3,1,2,0:T(2,128)(2,1)S(1)}, bf16[768,2,1,1024]{3,1,2,0:T(2,128)(2,1)}, u32[]{:S(2)}) copy-start(bf16[768,2,1,1024]{3,1,2,0:T(2,128)(2,1)} %param.3) | copy-start | bytes 9437188
  1.9 0.7 copy-start.2
  2.6 0.8 copy-start.3
  5.2 38.9 %collective-permute-start.8 = (bf16[4,64,1024]{2,1,0:T(8,128)(2,1)S(1)}, bf16[4,64,1024]{2,1,0:T(8,128)(2,1)S(1)}, u32[]{:S(2)}, u32[]{:S(2)}) collective-permute-start(bf16[4,64,1024]{2,1,0:T(8,128)(2,1)S(1)} %get-tuple-element.15), channel_id=1, source_target_pairs={{0,4},{1,5},{2,6},{3,7},{4,0},{5,1},{6,2},{7,3},{8,12},{9,13},{10,... | collective-permute-start | bytes 1572872 | tf_op jit(solution)/shard_map/ppermute | solution.py:38
  11.8 32.3 %copy-start.1 = (bf16[768,2,1,1024]{3,1,2,0:T(2,128)(2,1)S(1)}, bf16[768,2,1,1024]{3,1,2,0:T(2,128)(2,1)}, u32[]{:S(2)}) copy-start(bf16[768,2,1,1024]{3,1,2,0:T(2,128)(2,1)} %param.3) | copy-start | bytes 9437188
  12.5 31.6 %collective-permute-start = (bf16[240,2,1024]{2,1,0:T(2,128)(2,1)S(1)}, bf16[240,2,1024]{2,1,0:T(2,128)(2,1)S(1)}, u32[]{:S(2)}, u32[]{:S(2)}) collective-permute-start(bf16[240,2,1024]{2,1,0:T(2,128)(2,1)S(1)} %slice_bitcast_fusion), channel_id=1, source_target_pairs={{0,1},{1,2},{2,3},{3,4},{4,5},{5,6},{6,7},{7,8},{8,9},{9,10},{10,1... | collective-permute-start | bytes 2949128 | tf_op jit(solution)/shard_map/ppermute | solution.py:59
  45.0 11.8 %collective-permute-start.9 = (bf16[96,1024]{1,0:T(8,128)(2,1)S(1)}, bf16[96,1024]{1,0:T(8,128)(2,1)S(1)}, u32[]{:S(2)}, u32[]{:S(2)}) collective-permute-start(bf16[96,1024]{1,0:T(8,128)(2,1)S(1)} %pad_maximum_fusion.2), channel_id=1, source_target_pairs={{0,8},{1,9},{2,10},{3,11},{4,12},{5,13},{6,14},{7,15},{8,16},{9,17... | collective-permute-start | bytes 589832 | tf_op jit(solution)/shard_map/ppermute | solution.py:38
  49.3 10.0 %collective-permute-start.10 = (bf16[96,1024]{1,0:T(8,128)(2,1)S(1)}, bf16[96,1024]{1,0:T(8,128)(2,1)S(1)}, u32[]{:S(2)}, u32[]{:S(2)}) collective-permute-start(bf16[96,1024]{1,0:T(8,128)(2,1)S(1)} %pad_maximum_fusion.3), channel_id=1, source_target_pairs={{0,16},{1,17},{2,18},{3,19},{4,20},{5,21},{6,22},{7,23},{8,24},{9,... | collective-permute-start | bytes 589832 | tf_op jit(solution)/shard_map/ppermute | solution.py:38
  52.7 8.8 %collective-permute-start.11 = (bf16[96,1024]{1,0:T(8,128)(2,1)S(1)}, bf16[96,1024]{1,0:T(8,128)(2,1)S(1)}, u32[]{:S(2)}, u32[]{:S(2)}) collective-permute-start(bf16[96,1024]{1,0:T(8,128)(2,1)S(1)} %pad_maximum_fusion.4), channel_id=1, source_target_pairs={{0,24},{1,25},{2,26},{3,27},{4,28},{5,29},{6,30},{7,31},{8,0},{9,1... | collective-permute-start | bytes 589832 | tf_op jit(solution)/shard_map/ppermute | solution.py:38
  61.6 19.3 %collective-permute-start.12 = (bf16[384,1024]{1,0:T(8,128)(2,1)S(1)}, bf16[384,1024]{1,0:T(8,128)(2,1)S(1)}, u32[]{:S(2)}, u32[]{:S(2)}) collective-permute-start(bf16[384,1024]{1,0:T(8,128)(2,1)S(1)} %get-tuple-element.35), channel_id=1, source_target_pairs={{0,2},{1,3},{2,0},{3,1},{4,6},{5,7},{6,4},{7,5},{8,10},{9,11},{10,... | collective-permute-start | bytes 2359304 | tf_op jit(solution)/shard_map/ppermute | solution.py:38
  63.5 10.9 %collective-permute-start.14 = (bf16[64,1024]{1,0:T(8,128)(2,1)S(1)}, bf16[64,1024]{1,0:T(8,128)(2,1)S(1)}, u32[]{:S(2)}, u32[]{:S(2)}) collective-permute-start(bf16[64,1024]{1,0:T(8,128)(2,1)S(1)} %get-tuple-element.18), channel_id=1, source_target_pairs={{0,8},{1,9},{2,10},{3,11},{4,12},{5,13},{6,14},{7,15},{8,16},{9,17... | collective-permute-start | bytes 393224 | tf_op jit(solution)/shard_map/ppermute | solution.py:38
  68.1 7.2 %collective-permute-start.15 = (bf16[64,1024]{1,0:T(8,128)(2,1)S(1)}, bf16[64,1024]{1,0:T(8,128)(2,1)S(1)}, u32[]{:S(2)}, u32[]{:S(2)}) collective-permute-start(bf16[64,1024]{1,0:T(8,128)(2,1)S(1)} %get-tuple-element.19), channel_id=1, source_target_pairs={{0,16},{1,17},{2,18},{3,19},{4,20},{5,21},{6,22},{7,23},{8,24},{9,... | collective-permute-start | bytes 393224 | tf_op jit(solution)/shard_map/ppermute | solution.py:38
  71.0 6.0 %collective-permute-start.16 = (bf16[64,1024]{1,0:T(8,128)(2,1)S(1)}, bf16[64,1024]{1,0:T(8,128)(2,1)S(1)}, u32[]{:S(2)}, u32[]{:S(2)}) collective-permute-start(bf16[64,1024]{1,0:T(8,128)(2,1)S(1)} %get-tuple-element.20), channel_id=1, source_target_pairs={{0,24},{1,25},{2,26},{3,27},{4,28},{5,29},{6,30},{7,31},{8,0},{9,1... | collective-permute-start | bytes 393224 | tf_op jit(solution)/shard_map/ppermute | solution.py:38
  77.0 14.8 %collective-permute-start.17 = (bf16[256,1024]{1,0:T(8,128)(2,1)S(1)}, bf16[256,1024]{1,0:T(8,128)(2,1)S(1)}, u32[]{:S(2)}, u32[]{:S(2)}) collective-permute-start(bf16[256,1024]{1,0:T(8,128)(2,1)S(1)} %pad_maximum_fusion), channel_id=1, source_target_pairs={{0,2},{1,3},{2,0},{3,1},{4,6},{5,7},{6,4},{7,5},{8,10},{9,11},{10,... | collective-permute-start | bytes 1572872 | tf_op jit(solution)/shard_map/ppermute | solution.py:38
  81.0 59.3 %collective-permute-start.13 = (bf16[768,1024]{1,0:T(8,128)(2,1)S(1)}, bf16[768,1024]{1,0:T(8,128)(2,1)S(1)}, u32[]{:S(2)}, u32[]{:S(2)}) collective-permute-start(bf16[768,1024]{1,0:T(8,128)(2,1)S(1)} %constant_dynamic-update-slice_fusion.3.refs_0_), channel_id=1, source_target_pairs={{0,1},{1,0},{2,3},{3,2},{4,5},{5,4},{6,7},{7,6},{8,9},{9,8},{10,11... | collective-permute-start | bytes 4718600 | tf_op jit(solution)/shard_map/ppermute | solution.py:38
  91.8 46.4 %collective-permute-start.18 = (bf16[512,1024]{1,0:T(8,128)(2,1)S(1)}, bf16[512,1024]{1,0:T(8,128)(2,1)S(1)}, u32[]{:S(2)}, u32[]{:S(2)}) collective-permute-start(bf16[512,1024]{1,0:T(8,128)(2,1)S(1)} %constant_dynamic-update-slice_fusion.7.refs_0_), channel_id=1, source_target_pairs={{0,1},{1,0},{2,3},{3,2},{4,5},{5,4},{6,7},{7,6},{8,9},{9,8},{10,11... | collective-permute-start | bytes 3145736 | tf_op jit(solution)/shard_map/ppermute | solution.py:38
  96.6 16.6 %collective-permute-start.1 = (bf16[4,32,1024]{2,1,0:T(8,128)(2,1)S(1)}, bf16[4,32,1024]{2,1,0:T(8,128)(2,1)S(1)}, u32[]{:S(2)}, u32[]{:S(2)}) collective-permute-start(bf16[4,32,1024]{2,1,0:T(8,128)(2,1)S(1)} %get-tuple-element.14), channel_id=1, source_target_pairs={{0,4},{1,5},{2,6},{3,7},{4,0},{5,1},{6,2},{7,3},{8,12},{9,13},{10,... | collective-permute-start | bytes 786440 | tf_op jit(solution)/shard_map/ppermute | solution.py:38
  113.3 10.7 %collective-permute-start.2 = (bf16[32,1024]{1,0:T(8,128)(2,1)S(1)}, bf16[32,1024]{1,0:T(8,128)(2,1)S(1)}, u32[]{:S(2)}, u32[]{:S(2)}) collective-permute-start(bf16[32,1024]{1,0:T(8,128)(2,1)S(1)} %get-tuple-element.34), channel_id=1, source_target_pairs={{0,8},{1,9},{2,10},{3,11},{4,12},{5,13},{6,14},{7,15},{8,16},{9,17... | collective-permute-start | bytes 196616 | tf_op jit(solution)/shard_map/ppermute | solution.py:38
  117.7 6.5 %collective-permute-start.3 = (bf16[32,1024]{1,0:T(8,128)(2,1)S(1)}, bf16[32,1024]{1,0:T(8,128)(2,1)S(1)}, u32[]{:S(2)}, u32[]{:S(2)}) collective-permute-start(bf16[32,1024]{1,0:T(8,128)(2,1)S(1)} %get-tuple-element.33), channel_id=1, source_target_pairs={{0,16},{1,17},{2,18},{3,19},{4,20},{5,21},{6,22},{7,23},{8,24},{9,... | collective-permute-start | bytes 196616 | tf_op jit(solution)/shard_map/ppermute | solution.py:38
  120.6 5.1 %collective-permute-start.4 = (bf16[32,1024]{1,0:T(8,128)(2,1)S(1)}, bf16[32,1024]{1,0:T(8,128)(2,1)S(1)}, u32[]{:S(2)}, u32[]{:S(2)}) collective-permute-start(bf16[32,1024]{1,0:T(8,128)(2,1)S(1)} %get-tuple-element.32), channel_id=1, source_target_pairs={{0,24},{1,25},{2,26},{3,27},{4,28},{5,29},{6,30},{7,31},{8,0},{9,1... | collective-permute-start | bytes 196616 | tf_op jit(solution)/shard_map/ppermute | solution.py:38
  125.7 7.6 %collective-permute-start.6 = (bf16[128,1024]{1,0:T(8,128)(2,1)S(1)}, bf16[128,1024]{1,0:T(8,128)(2,1)S(1)}, u32[]{:S(2)}, u32[]{:S(2)}) collective-permute-start(bf16[128,1024]{1,0:T(8,128)(2,1)S(1)} %pad_maximum_fusion.1.refs_0_), channel_id=1, source_target_pairs={{0,2},{1,3},{2,0},{3,1},{4,6},{5,7},{6,4},{7,5},{8,10},{9,11},{10,... | collective-permute-start | bytes 786440 | tf_op jit(solution)/shard_map/ppermute | solution.py:38
  127.6 15.5 %collective-permute-start.5 = (bf16[128,1024]{1,0:T(8,128)(2,1)S(1)}, bf16[128,1024]{1,0:T(8,128)(2,1)S(1)}, u32[]{:S(2)}, u32[]{:S(2)}) collective-permute-start(bf16[128,1024]{1,0:T(8,128)(2,1)S(1)} %pad_maximum_fusion.1.refs_0_), channel_id=1, source_target_pairs={{0,1},{1,0},{2,3},{3,2},{4,5},{5,4},{6,7},{7,6},{8,9},{9,8},{10,11... | collective-permute-start | bytes 786440 | tf_op jit(solution)/shard_map/ppermute | solution.py:38
  133.3 9.8 %collective-permute-start.7 = (bf16[128,1024]{1,0:T(8,128)(2,1)S(1)}, bf16[128,1024]{1,0:T(8,128)(2,1)S(1)}, u32[]{:S(2)}, u32[]{:S(2)}) collective-permute-start(bf16[128,1024]{1,0:T(8,128)(2,1)S(1)} %collective-permute-done.6.refs_2_), channel_id=1, source_target_pairs={{0,1},{1,0},{2,3},{3,2},{4,5},{5,4},{6,7},{7,6},{8,9},{9,8},{10,11... | collective-permute-start | bytes 786440 | tf_op jit(solution)/shard_map/ppermute | solution.py:38

commit v2 on v1

--- a/solution.py
+++ b/solution.py
@@ -104,20 +104,19 @@
                 band_ref[at : at + BLOCK, :] = (shifted * wave).astype(BF16)
 
 
-def filter_late(taps_ref, trig_ref, volt_ref, band_ref, m0, m1, m2, m3, t_ref):
+def filter_late(taps_ref, trig_ref, volt_ref, band_ref, *out_refs):
     band_matrix(taps_ref, trig_ref, band_ref)
-    mine = (m0, m1, m2, m3)
     for i in range(2):
         start = i * BLOCK * FINE
         window = volt_ref[start : start + WINDOW].reshape(2 * WINDOW, S)
         out = jnp.dot(band_ref[...], window, preferred_element_type=F32).astype(BF16)
-        rows = slice(i * ROWS, (i + 1) * ROWS)
         for d in range(XS):
-            mine[d][rows, :] = out[2 * d * ROWS : (2 * d + 1) * ROWS]
-            t_ref[d, rows, :] = out[(2 * d + 1) * ROWS : (2 * d + 2) * ROWS]
-
-
-def filter_first(halo_ref, volt_ref, band_ref, m_ref, t_ref):
+            for other in range(2):
+                at = (2 * other + i) * ROWS
+                out_refs[d][at : at + ROWS, :] = out[(2 * d + other) * ROWS : (2 * d + other + 1) * ROWS]
+
+
+def filter_first(halo_ref, volt_ref, band_ref, *out_refs):
     here = BLOCK * FINE
     own = volt_ref[0:here].reshape(2 * here, S)
     prior = halo_ref[...].reshape(2 * here - 2 * FINE, S)
@@ -126,8 +125,7 @@
     out += jnp.dot(band[:, 2 * FINE : 2 * here], prior, preferred_element_type=F32)
     out = out.astype(BF16)
     for d in range(XS):
-        m_ref[d] = out[2 * d * ROWS : (2 * d + 1) * ROWS]
-        t_ref[d] = out[(2 * d + 1) * ROWS : (2 * d + 2) * ROWS]
+        out_refs[d][...] = out[2 * d * ROWS : 2 * (d + 1) * ROWS]
 
 
 def products(n_pieces, scale, *refs):
@@ -174,47 +172,53 @@
     )(*pieces, *more)
 
 
+def spread(slabs):
+    return [slabs[0]] + [move(slabs[d], along_x(d)) for d in range(1, XS)]
+
+
+def part(slabs, other):
+    half = slabs[0].shape[0] // 2
+    return jnp.concatenate([slab[other * half : (other + 1) * half] for slab in slabs], 0)
+
+
 def shards(voltage, taps):
     samples_here = voltage.shape[0]
-    late = 2 * BLOCK
     volt = voltage.reshape(samples_here, 2, S)
     halo = halo_of(volt[samples_here - (TAPS - 1) * FINE :])
     params = pltpu.CompilerParams(vmem_limit_bytes=40 << 20)
-    band, ma0, ma1, ma2, ma3, ta = pl.pallas_call(
+    band, *late_out = pl.pallas_call(
         filter_late,
-        out_shape=(
-            shape(4 * FOUT * BLOCK // 2, 2 * WINDOW),
-            *[shape(2 * late, S)] * 4,
-            shape(XS, 2 * late, S),
-        ),
+        out_shape=(shape(4 * FOUT * BLOCK // 2, 2 * WINDOW), *[shape(4 * ROWS, S)] * XS),
         in_specs=spec(3),
-        out_specs=spec(6),
+        out_specs=spec(1 + XS),
         compiler_params=params,
         cost_estimate=pl.CostEstimate(flops=2 << 29, bytes_accessed=6 << 20, transcendentals=0),
     )(taps.reshape(1, -1), jnp.asarray(trig_table()), volt)
-    ta = move(ta, far_z)
-    ma = [ma0] + [move(m, along_x(d)) for d, m in ((1, ma1), (2, ma2), (3, ma3))]
-    mb, tb = pl.pallas_call(
+    late_all = spread(late_out)
+    halo, *late_all = lax.optimization_barrier((halo, *late_all))
+    first_out = pl.pallas_call(
         filter_first,
-        out_shape=(shape(XS, ROWS, S), shape(XS, ROWS, S)),
+        out_shape=[shape(2 * ROWS, S)] * XS,
         in_specs=spec(3),
-        out_specs=spec(2),
+        out_specs=spec(XS),
         compiler_params=params,
         cost_estimate=pl.CostEstimate(flops=1 << 29, bytes_accessed=3 << 20, transcendentals=0),
     )(halo, volt, band)
-    tb = move(tb, far_z)
-    ma = jnp.concatenate(ma, 0)
-    ma = jnp.concatenate([ma, move(ma, near_z)], 0)
-    second = [jnp.concatenate([ta[d], mb[d]], 0) for d in range(XS)]
-    second = [second[0]] + [move(second[d], along_x(d)) for d in range(1, XS)]
-    second = jnp.concatenate(second, 0)
-    third = [tb[0]] + [move(tb[d], along_x(d)) for d in range(1, XS)]
-    third = jnp.concatenate(third, 0)
-    second = jnp.concatenate([second, move(second, near_z)], 0)
-    third_near = move(third, near_z)
+    ta = move(part(late_all, 1), far_z)
+    ma = part(late_all, 0)
+    ma_near = move(ma, near_z)
+    first_all = spread(first_out)
+    ta, ma_near, *first_all = lax.optimization_barrier((ta, ma_near, *first_all))
+    tb = move(part(first_all, 1), far_z)
+    second = jnp.concatenate([ta, part(first_all, 0)], 0)
+    second_near = move(second, near_z)
+    tb_near = move(tb, near_z)
+    ma = jnp.concatenate([ma, ma_near], 0)
     acc = correlate([ma, move(ma, other_core)], None)
-    acc = correlate([second, move(second, other_core)], acc)
-    pieces = [third, move(third, other_core), third_near, move(third_near, other_core)]
+    own = jnp.concatenate([second, tb], 0)
+    acc = correlate([own, move(own, other_core)], acc)
+    near = jnp.concatenate(lax.optimization_barrier((second_near, tb_near)), 0)
+    pieces = [near, move(near, other_core)]
     frames = samples_here // FINE * XS * ZS * CORES
     return correlate(pieces, acc, 1.0 / frames)[None]
 

time: 147 us -> 110 us (0.75)
  starting transfers between devices: 73.3 us -> 48.2 us
  waiting for transfers between devices: 57.5 us -> 45.5 us
    ppermute x18 -> x14, starting transfers between devices: 68.4 us -> 42.9 us  [move(): return lax.ppermute(array, 'tm', moves(rule))]
    ppermute x18 -> x14, waiting for transfers between devices: 57.5 us -> 45.5 us  [move(): return lax.ppermute(array, 'tm', moves(rule))]
    unnamed x16 -> x18, local copies, waits for them, and re-layouts: 3.56 us -> 3.75 us
  transfers between devices with their start and end apart: 19 -> 15, of which waited for: 11 -> 7; matrix products, arithmetic and copies ran while one was open for 1% -> 0% of each run, Pallas kernels for 3% -> 6%
where the time goes in v2:
time: 110 us
  starting transfers between devices  48.2 us (44%)
  waiting for transfers between devices  45.5 us (41%)
  Pallas kernels  9.96 us (9%)
  local copies, waits for them, and re-layouts  5.7 us (5%)
    ppermute x14, waiting for transfers between devices, move(): return lax.ppermute(array, 'tm', moves(rule))  45.5 us
    ppermute x14, starting transfers between devices, move(): return lax.ppermute(array, 'tm', moves(rule))  42.9 us
    pallas_call x3, Pallas kernels, correlate(): pl.pallas_call(functools.partial(products, len(pieces), scale), grid=(4,)...  7.45 us
    ppermute x1, starting transfers between devices, halo_of(): return lax.ppermute(tail, 'tm', pairs)  5.39 us
    unnamed x18, local copies, waits for them, and re-layouts  3.75 us
  transfers between devices with their start and end apart: 15, of which 7 were waited for; matrix products, arithmetic and copies ran while one was open for 0% of the time, Pallas kernels for 6%

profile of v2, /device:TPU:1, one launch (start us, length us, event | category | flops | bytes accessed | tf_op | source)
XLA Modules:
  0.0 109.8 jit_solution(10185643115657246040)
XLA Ops:
  0.0 1.9 %slice_bitcast_fusion = bf16[240,2,1024]{2,1,0:T(2,128)(2,1)S(1)} fusion(bf16[768,2,1,1024]{3,1,0,2:T(2,128)(2,1)} %bitcast.6), kind=kLoop, calls=%fused_computation | loop fusion | bytes 1966080 | tf_op jit(solution)/shard_map/slice | solution.py:187
  1.9 5.4 %collective-permute-start = (bf16[240,2,1024]{2,1,0:T(2,128)(2,1)S(1)}, bf16[240,2,1024]{2,1,0:T(2,128)(2,1)S(1)}, u32[]{:S(2)}, u32[]{:S(2)}) collective-permute-start(bf16[240,2,1024]{2,1,0:T(2,128)(2,1)S(1)} %slice_bitcast_fusion), channel_id=1, source_target_pairs={{0,1},{1,2},{2,3},{3,4},{4,5},{5,6},{6,7},{7,8},{8,9},{9,10},{10,1... | collective-permute-start | bytes 2949128 | tf_op jit(solution)/shard_map/ppermute | solution.py:59
  7.3 0.0 copy-start
  7.3 1.9 %copy-done = bf16[768,2,1,1024]{3,1,2,0:T(2,128)(2,1)S(1)} copy-done((bf16[768,2,1,1024]{3,1,2,0:T(2,128)(2,1)S(1)}, bf16[768,2,1,1024]{3,1,2,0:T(2,128)(2,1)}, u32[]{:S(2)}) %copy-start) | copy-done | bytes 3145752
  9.2 0.0 copy-start.2
  9.2 0.7 copy-done.2
  9.9 0.0 copy-start.3
  9.9 0.8 copy-done.3
  10.7 1.7 %shard_map.37 = (bf16[256,1024]{1,0:T(8,128)(2,1)S(1)}, bf16[128,1024]{1,0:T(8,128)(2,1)S(1)}, bf16[128,1024]{1,0:T(8,128)(2,1)S(1)}, bf16[128,1024]{1,0:T(8,128)(2,1)S(1)}, bf16[128,1024]{1,0:T(8,128)(2,1)S(1)}) custom-call(f32[1,256]{1,0:T(1,128)S(1)} %bitcast.9, f32[16,1024]{1,0:T(8,128)S(1)} %copy-done.3, bf16[768,2,1024]{2,1,0:T(2,128)(2,1)S(1)} %bitcast.7), custom_call_target="tpu_custom_call" | custom-call | flops 1073741824 | bytes 6291456 | tf_op jit(solution)/shard_map/pallas_call | solution.py:189
  12.4 3.1 %collective-permute-start.1 = (bf16[128,1024]{1,0:T(8,128)(2,1)S(1)}, bf16[128,1024]{1,0:T(8,128)(2,1)S(1)}, u32[]{:S(2)}, u32[]{:S(2)}) collective-permute-start(bf16[128,1024]{1,0:T(8,128)(2,1)S(1)} %get-tuple-element.28), channel_id=1, source_target_pairs={{0,8},{1,9},{2,10},{3,11},{4,12},{5,13},{6,14},{7,15},{8,16},{9,17... | collective-permute-start | bytes 786440 | tf_op jit(solution)/shard_map/ppermute | solution.py:38
  15.6 4.4 %collective-permute-start.2 = (bf16[128,1024]{1,0:T(8,128)(2,1)S(1)}, bf16[128,1024]{1,0:T(8,128)(2,1)S(1)}, u32[]{:S(2)}, u32[]{:S(2)}) collective-permute-start(bf16[128,1024]{1,0:T(8,128)(2,1)S(1)} %get-tuple-element.29), channel_id=1, source_target_pairs={{0,16},{1,17},{2,18},{3,19},{4,20},{5,21},{6,22},{7,23},{8,24},{9,... | collective-permute-start | bytes 786440 | tf_op jit(solution)/shard_map/ppermute | solution.py:38
  19.9 3.1 %collective-permute-start.3 = (bf16[128,1024]{1,0:T(8,128)(2,1)S(1)}, bf16[128,1024]{1,0:T(8,128)(2,1)S(1)}, u32[]{:S(2)}, u32[]{:S(2)}) collective-permute-start(bf16[128,1024]{1,0:T(8,128)(2,1)S(1)} %get-tuple-element.30), channel_id=1, source_target_pairs={{0,24},{1,25},{2,26},{3,27},{4,28},{5,29},{6,30},{7,31},{8,0},{9,1... | collective-permute-start | bytes 786440 | tf_op jit(solution)/shard_map/ppermute | solution.py:38
  23.0 3.6 %collective-permute-done.1 = bf16[128,1024]{1,0:T(8,128)(2,1)S(1)} collective-permute-done((bf16[128,1024]{1,0:T(8,128)(2,1)S(1)}, bf16[128,1024]{1,0:T(8,128)(2,1)S(1)}, u32[]{:S(2)}, u32[]{:S(2)}) %collective-permute-start.1) | collective-permute-done | bytes 262176 | tf_op jit(solution)/shard_map/ppermute | solution.py:38
  26.6 9.1 %collective-permute-done.2 = bf16[128,1024]{1,0:T(8,128)(2,1)S(1)} collective-permute-done((bf16[128,1024]{1,0:T(8,128)(2,1)S(1)}, bf16[128,1024]{1,0:T(8,128)(2,1)S(1)}, u32[]{:S(2)}, u32[]{:S(2)}) %collective-permute-start.2) | collective-permute-done | bytes 262176 | tf_op jit(solution)/shard_map/ppermute | solution.py:38
  35.7 0.0 collective-permute-done.3
  35.7 0.0 collective-permute-done.halo_ref
  35.7 0.0 copy-start.1
  35.9 2.2 %collective-permute-start.5 = (bf16[256,1024]{1,0:T(8,128)(2,1)S(1)}, bf16[256,1024]{1,0:T(8,128)(2,1)S(1)}, u32[]{:S(2)}, u32[]{:S(2)}) collective-permute-start(bf16[256,1024]{1,0:T(8,128)(2,1)S(1)} %pad_maximum_fusion.1), channel_id=1, source_target_pairs={{0,2},{1,3},{2,0},{3,1},{4,6},{5,7},{6,4},{7,5},{8,10},{9,11},{10,... | collective-permute-start | bytes 1572872 | tf_op jit(solution)/shard_map/ppermute | solution.py:38
  38.1 1.9 %collective-permute-start.4 = (bf16[256,1024]{1,0:T(8,128)(2,1)S(1)}, bf16[256,1024]{1,0:T(8,128)(2,1)S(1)}, u32[]{:S(2)}, u32[]{:S(2)}) collective-permute-start(bf16[256,1024]{1,0:T(8,128)(2,1)S(1)} %pad_maximum_fusion), channel_id=1, source_target_pairs={{0,4},{1,5},{2,6},{3,7},{4,0},{5,1},{6,2},{7,3},{8,12},{9,13},{10,... | collective-permute-start | bytes 1572872 | tf_op jit(solution)/shard_map/ppermute | solution.py:38
  40.1 0.0 copy-done.1
  40.1 0.8 shard_map.38
  40.8 3.6 %collective-permute-start.6 = (bf16[64,1024]{1,0:T(8,128)(2,1)S(1)}, bf16[64,1024]{1,0:T(8,128)(2,1)S(1)}, u32[]{:S(2)}, u32[]{:S(2)}) collective-permute-start(bf16[64,1024]{1,0:T(8,128)(2,1)S(1)} %get-tuple-element.38), channel_id=1, source_target_pairs={{0,8},{1,9},{2,10},{3,11},{4,12},{5,13},{6,14},{7,15},{8,16},{9,17... | collective-permute-start | bytes 393224 | tf_op jit(solution)/shard_map/ppermute | solution.py:38
  44.4 2.7 %collective-permute-start.7 = (bf16[64,1024]{1,0:T(8,128)(2,1)S(1)}, bf16[64,1024]{1,0:T(8,128)(2,1)S(1)}, u32[]{:S(2)}, u32[]{:S(2)}) collective-permute-start(bf16[64,1024]{1,0:T(8,128)(2,1)S(1)} %get-tuple-element.39), channel_id=1, source_target_pairs={{0,16},{1,17},{2,18},{3,19},{4,20},{5,21},{6,22},{7,23},{8,24},{9,... | collective-permute-start | bytes 393224 | tf_op jit(solution)/shard_map/ppermute | solution.py:38
  47.1 3.5 %collective-permute-start.8 = (bf16[64,1024]{1,0:T(8,128)(2,1)S(1)}, bf16[64,1024]{1,0:T(8,128)(2,1)S(1)}, u32[]{:S(2)}, u32[]{:S(2)}) collective-permute-start(bf16[64,1024]{1,0:T(8,128)(2,1)S(1)} %get-tuple-element.40), channel_id=1, source_target_pairs={{0,24},{1,25},{2,26},{3,27},{4,28},{5,29},{6,30},{7,31},{8,0},{9,1... | collective-permute-start | bytes 393224 | tf_op jit(solution)/shard_map/ppermute | solution.py:38
  50.7 0.0 collective-permute-done.6
  50.7 1.0 collective-permute-done.7
  51.6 1.7 %collective-permute-done.8 = bf16[64,1024]{1,0:T(8,128)(2,1)S(1)} collective-permute-done((bf16[64,1024]{1,0:T(8,128)(2,1)S(1)}, bf16[64,1024]{1,0:T(8,128)(2,1)S(1)}, u32[]{:S(2)}, u32[]{:S(2)}) %collective-permute-start.8) | collective-permute-done | bytes 131104 | tf_op jit(solution)/shard_map/ppermute | solution.py:38
  53.4 4.6 %collective-permute-done.5 = bf16[256,1024]{1,0:T(8,128)(2,1)S(1)} collective-permute-done((bf16[256,1024]{1,0:T(8,128)(2,1)S(1)}, bf16[256,1024]{1,0:T(8,128)(2,1)S(1)}, u32[]{:S(2)}, u32[]{:S(2)}) %collective-permute-start.5) | collective-permute-done | bytes 524320 | tf_op jit(solution)/shard_map/ppermute | solution.py:38
  58.0 7.3 %collective-permute-done.4 = bf16[256,1024]{1,0:T(8,128)(2,1)S(1)} collective-permute-done((bf16[256,1024]{1,0:T(8,128)(2,1)S(1)}, bf16[256,1024]{1,0:T(8,128)(2,1)S(1)}, u32[]{:S(2)}, u32[]{:S(2)}) %collective-permute-start.4) | collective-permute-done | bytes 524320 | tf_op jit(solution)/shard_map/ppermute | solution.py:38
  65.3 0.1 constant_dynamic-update-slice_fusion.4
  65.5 1.9 %collective-permute-start.9 = (bf16[384,1024]{1,0:T(8,128)(2,1)S(1)}, bf16[384,1024]{1,0:T(8,128)(2,1)S(1)}, u32[]{:S(2)}, u32[]{:S(2)}) collective-permute-start(bf16[384,1024]{1,0:T(8,128)(2,1)S(1)} %get-tuple-element.65), channel_id=1, source_target_pairs={{0,2},{1,3},{2,0},{3,1},{4,6},{5,7},{6,4},{7,5},{8,10},{9,11},{10,... | collective-permute-start | bytes 2359304 | tf_op jit(solution)/shard_map/ppermute | solution.py:38
  67.5 3.4 %collective-permute-start.10 = (bf16[128,1024]{1,0:T(8,128)(2,1)S(1)}, bf16[128,1024]{1,0:T(8,128)(2,1)S(1)}, u32[]{:S(2)}, u32[]{:S(2)}) collective-permute-start(bf16[128,1024]{1,0:T(8,128)(2,1)S(1)} %pad_maximum_fusion.2), channel_id=1, source_target_pairs={{0,4},{1,5},{2,6},{3,7},{4,0},{5,1},{6,2},{7,3},{8,12},{9,13},{10,... | collective-permute-start | bytes 786440 | tf_op jit(solution)/shard_map/ppermute | solution.py:38
  70.9 18.1 %collective-permute-done.10 = bf16[128,1024]{1,0:T(8,128)(2,1)S(1)} collective-permute-done((bf16[128,1024]{1,0:T(8,128)(2,1)S(1)}, bf16[128,1024]{1,0:T(8,128)(2,1)S(1)}, u32[]{:S(2)}, u32[]{:S(2)}) %collective-permute-start.10) | collective-permute-done | bytes 262176 | tf_op jit(solution)/shard_map/ppermute | solution.py:38
  89.0 4.1 %collective-permute-start.11 = (bf16[128,1024]{1,0:T(8,128)(2,1)S(1)}, bf16[128,1024]{1,0:T(8,128)(2,1)S(1)}, u32[]{:S(2)}, u32[]{:S(2)}) collective-permute-start(bf16[128,1024]{1,0:T(8,128)(2,1)S(1)} %collective-permute-done.10), channel_id=1, source_target_pairs={{0,2},{1,3},{2,0},{3,1},{4,6},{5,7},{6,4},{7,5},{8,10},{9,11},{10,... | collective-permute-start | bytes 786440 | tf_op jit(solution)/shard_map/ppermute | solution.py:38
  93.1 4.0 %collective-permute-start.14 = (bf16[512,1024]{1,0:T(8,128)(2,1)S(1)}, bf16[512,1024]{1,0:T(8,128)(2,1)S(1)}, u32[]{:S(2)}, u32[]{:S(2)}) collective-permute-start(bf16[512,1024]{1,0:T(8,128)(2,1)S(1)} %constant_dynamic-update-slice_fusion.5.refs_0_), channel_id=1, source_target_pairs={{0,1},{1,0},{2,3},{3,2},{4,5},{5,4},{6,7},{7,6},{8,9},{9,8},{10,11... | collective-permute-start | bytes 3145736 | tf_op jit(solution)/shard_map/ppermute | solution.py:38
  97.2 1.9 %collective-permute-start.13 = (bf16[512,1024]{1,0:T(8,128)(2,1)S(1)}, bf16[512,1024]{1,0:T(8,128)(2,1)S(1)}, u32[]{:S(2)}, u32[]{:S(2)}) collective-permute-start(bf16[512,1024]{1,0:T(8,128)(2,1)S(1)} %constant_dynamic-update-slice_fusion.3.refs_0_), channel_id=1, source_target_pairs={{0,1},{1,0},{2,3},{3,2},{4,5},{5,4},{6,7},{7,6},{8,9},{9,8},{10,11... | collective-permute-start | bytes 3145736 | tf_op jit(solution)/shard_map/ppermute | solution.py:38
  99.1 0.0 collective-permute-done.11
  99.1 0.0 collective-permute-done.9
  99.1 0.1 constant_dynamic-update-slice_fusion.2
  99.2 3.1 %collective-permute-start.12 = (bf16[512,1024]{1,0:T(8,128)(2,1)S(1)}, bf16[512,1024]{1,0:T(8,128)(2,1)S(1)}, u32[]{:S(2)}, u32[]{:S(2)}) collective-permute-start(bf16[512,1024]{1,0:T(8,128)(2,1)S(1)} %constant_dynamic-update-slice_fusion.1.refs_0_), channel_id=1, source_target_pairs={{0,1},{1,0},{2,3},{3,2},{4,5},{5,4},{6,7},{7,6},{8,9},{9,8},{10,11... | collective-permute-start | bytes 3145736 | tf_op jit(solution)/shard_map/ppermute | solution.py:38
  102.3 0.0 collective-permute-done.14.refs_1_
  102.3 2.0 %shard_map.39.refs_2_ = f32[2,1024,256]{2,1,0:T(8,128)S(1)} custom-call(bf16[512,1024]{1,0:T(8,128)(2,1)S(1)} %constant_dynamic-update-slice_fusion.5.refs_0_, bf16[512,1024]{1,0:T(8,128)(2,1)S(1)} %collective-permute-done.14.refs_1_), custom_call_target="tpu_custom_call" | custom-call | flops 1073741824 | bytes 4194304 | tf_op jit(solution)/shard_map/pallas_call | solution.py:163
  104.4 0.0 collective-permute-done.13.refs_1_
  104.4 2.2 %shard_map.40.refs_2_ = f32[2,1024,256]{2,1,0:T(8,128)S(1)} custom-call(bf16[512,1024]{1,0:T(8,128)(2,1)S(1)} %constant_dynamic-update-slice_fusion.3.refs_0_, bf16[512,1024]{1,0:T(8,128)(2,1)S(1)} %collective-permute-done.13.refs_1_, f32[2,1024,256]{2,1,0:T(8,128)S(1)} %shard_map.39.refs_2_), custom_call_target="tpu_custom_call" | custom-call | flops 1073741824 | bytes 4194304 | tf_op jit(solution)/shard_map/pallas_call | solution.py:163
  106.6 0.0 collective-permute-done.12.refs_1_
  106.6 3.2 %shard_map.41 = f32[2,1024,256]{2,1,0:T(8,128)} custom-call(bf16[512,1024]{1,0:T(8,128)(2,1)S(1)} %constant_dynamic-update-slice_fusion.1.refs_0_, bf16[512,1024]{1,0:T(8,128)(2,1)S(1)} %collective-permute-done.12.refs_1_, f32[2,1024,256]{2,1,0:T(8,128)S(1)} %shard_map.40.refs_2_), custom_call_target="tpu_custom_call" | custom-call | flops 1073741824 | bytes 4194304 | tf_op jit(solution)/shard_map/pallas_call | solution.py:163
  (14 shorter events, 0.3 us)
Async XLA Ops:
  1.9 33.8 %collective-permute-start = (bf16[240,2,1024]{2,1,0:T(2,128)(2,1)S(1)}, bf16[240,2,1024]{2,1,0:T(2,128)(2,1)S(1)}, u32[]{:S(2)}, u32[]{:S(2)}) collective-permute-start(bf16[240,2,1024]{2,1,0:T(2,128)(2,1)S(1)} %slice_bitcast_fusion), channel_id=1, source_target_pairs={{0,1},{1,2},{2,3},{3,4},{4,5},{5,6},{6,7},{7,8},{8,9},{9,10},{10,1... | collective-permute-start | bytes 2949128 | tf_op jit(solution)/shard_map/ppermute | solution.py:59
  7.3 1.9 %copy-start = (bf16[768,2,1,1024]{3,1,2,0:T(2,128)(2,1)S(1)}, bf16[768,2,1,1024]{3,1,2,0:T(2,128)(2,1)}, u32[]{:S(2)}) copy-start(bf16[768,2,1,1024]{3,1,2,0:T(2,128)(2,1)} %param.3) | copy-start | bytes 9437188
  9.2 0.7 copy-start.2
  9.9 0.8 copy-start.3
  12.4 14.2 %collective-permute-start.1 = (bf16[128,1024]{1,0:T(8,128)(2,1)S(1)}, bf16[128,1024]{1,0:T(8,128)(2,1)S(1)}, u32[]{:S(2)}, u32[]{:S(2)}) collective-permute-start(bf16[128,1024]{1,0:T(8,128)(2,1)S(1)} %get-tuple-element.28), channel_id=1, source_target_pairs={{0,8},{1,9},{2,10},{3,11},{4,12},{5,13},{6,14},{7,15},{8,16},{9,17... | collective-permute-start | bytes 786440 | tf_op jit(solution)/shard_map/ppermute | solution.py:38
  15.6 20.1 %collective-permute-start.2 = (bf16[128,1024]{1,0:T(8,128)(2,1)S(1)}, bf16[128,1024]{1,0:T(8,128)(2,1)S(1)}, u32[]{:S(2)}, u32[]{:S(2)}) collective-permute-start(bf16[128,1024]{1,0:T(8,128)(2,1)S(1)} %get-tuple-element.29), channel_id=1, source_target_pairs={{0,16},{1,17},{2,18},{3,19},{4,20},{5,21},{6,22},{7,23},{8,24},{9,... | collective-permute-start | bytes 786440 | tf_op jit(solution)/shard_map/ppermute | solution.py:38
  19.9 15.8 %collective-permute-start.3 = (bf16[128,1024]{1,0:T(8,128)(2,1)S(1)}, bf16[128,1024]{1,0:T(8,128)(2,1)S(1)}, u32[]{:S(2)}, u32[]{:S(2)}) collective-permute-start(bf16[128,1024]{1,0:T(8,128)(2,1)S(1)} %get-tuple-element.30), channel_id=1, source_target_pairs={{0,24},{1,25},{2,26},{3,27},{4,28},{5,29},{6,30},{7,31},{8,0},{9,1... | collective-permute-start | bytes 786440 | tf_op jit(solution)/shard_map/ppermute | solution.py:38
  35.7 4.3 %copy-start.1 = (bf16[768,2,1,1024]{3,1,2,0:T(2,128)(2,1)S(1)}, bf16[768,2,1,1024]{3,1,2,0:T(2,128)(2,1)}, u32[]{:S(2)}) copy-start(bf16[768,2,1,1024]{3,1,2,0:T(2,128)(2,1)} %param.3) | copy-start | bytes 9437188
  35.9 22.1 %collective-permute-start.5 = (bf16[256,1024]{1,0:T(8,128)(2,1)S(1)}, bf16[256,1024]{1,0:T(8,128)(2,1)S(1)}, u32[]{:S(2)}, u32[]{:S(2)}) collective-permute-start(bf16[256,1024]{1,0:T(8,128)(2,1)S(1)} %pad_maximum_fusion.1), channel_id=1, source_target_pairs={{0,2},{1,3},{2,0},{3,1},{4,6},{5,7},{6,4},{7,5},{8,10},{9,11},{10,... | collective-permute-start | bytes 1572872 | tf_op jit(solution)/shard_map/ppermute | solution.py:38
  38.1 27.2 %collective-permute-start.4 = (bf16[256,1024]{1,0:T(8,128)(2,1)S(1)}, bf16[256,1024]{1,0:T(8,128)(2,1)S(1)}, u32[]{:S(2)}, u32[]{:S(2)}) collective-permute-start(bf16[256,1024]{1,0:T(8,128)(2,1)S(1)} %pad_maximum_fusion), channel_id=1, source_target_pairs={{0,4},{1,5},{2,6},{3,7},{4,0},{5,1},{6,2},{7,3},{8,12},{9,13},{10,... | collective-permute-start | bytes 1572872 | tf_op jit(solution)/shard_map/ppermute | solution.py:38
  40.8 9.8 %collective-permute-start.6 = (bf16[64,1024]{1,0:T(8,128)(2,1)S(1)}, bf16[64,1024]{1,0:T(8,128)(2,1)S(1)}, u32[]{:S(2)}, u32[]{:S(2)}) collective-permute-start(bf16[64,1024]{1,0:T(8,128)(2,1)S(1)} %get-tuple-element.38), channel_id=1, source_target_pairs={{0,8},{1,9},{2,10},{3,11},{4,12},{5,13},{6,14},{7,15},{8,16},{9,17... | collective-permute-start | bytes 393224 | tf_op jit(solution)/shard_map/ppermute | solution.py:38
  44.4 7.2 %collective-permute-start.7 = (bf16[64,1024]{1,0:T(8,128)(2,1)S(1)}, bf16[64,1024]{1,0:T(8,128)(2,1)S(1)}, u32[]{:S(2)}, u32[]{:S(2)}) collective-permute-start(bf16[64,1024]{1,0:T(8,128)(2,1)S(1)} %get-tuple-element.39), channel_id=1, source_target_pairs={{0,16},{1,17},{2,18},{3,19},{4,20},{5,21},{6,22},{7,23},{8,24},{9,... | collective-permute-start | bytes 393224 | tf_op jit(solution)/shard_map/ppermute | solution.py:38
  47.1 6.2 %collective-permute-start.8 = (bf16[64,1024]{1,0:T(8,128)(2,1)S(1)}, bf16[64,1024]{1,0:T(8,128)(2,1)S(1)}, u32[]{:S(2)}, u32[]{:S(2)}) collective-permute-start(bf16[64,1024]{1,0:T(8,128)(2,1)S(1)} %get-tuple-element.40), channel_id=1, source_target_pairs={{0,24},{1,25},{2,26},{3,27},{4,28},{5,29},{6,30},{7,31},{8,0},{9,1... | collective-permute-start | bytes 393224 | tf_op jit(solution)/shard_map/ppermute | solution.py:38
  65.5 33.6 %collective-permute-start.9 = (bf16[384,1024]{1,0:T(8,128)(2,1)S(1)}, bf16[384,1024]{1,0:T(8,128)(2,1)S(1)}, u32[]{:S(2)}, u32[]{:S(2)}) collective-permute-start(bf16[384,1024]{1,0:T(8,128)(2,1)S(1)} %get-tuple-element.65), channel_id=1, source_target_pairs={{0,2},{1,3},{2,0},{3,1},{4,6},{5,7},{6,4},{7,5},{8,10},{9,11},{10,... | collective-permute-start | bytes 2359304 | tf_op jit(solution)/shard_map/ppermute | solution.py:38
  67.5 21.5 %collective-permute-start.10 = (bf16[128,1024]{1,0:T(8,128)(2,1)S(1)}, bf16[128,1024]{1,0:T(8,128)(2,1)S(1)}, u32[]{:S(2)}, u32[]{:S(2)}) collective-permute-start(bf16[128,1024]{1,0:T(8,128)(2,1)S(1)} %pad_maximum_fusion.2), channel_id=1, source_target_pairs={{0,4},{1,5},{2,6},{3,7},{4,0},{5,1},{6,2},{7,3},{8,12},{9,13},{10,... | collective-permute-start | bytes 786440 | tf_op jit(solution)/shard_map/ppermute | solution.py:38
  89.0 10.2 %collective-permute-start.11 = (bf16[128,1024]{1,0:T(8,128)(2,1)S(1)}, bf16[128,1024]{1,0:T(8,128)(2,1)S(1)}, u32[]{:S(2)}, u32[]{:S(2)}) collective-permute-start(bf16[128,1024]{1,0:T(8,128)(2,1)S(1)} %collective-permute-done.10), channel_id=1, source_target_pairs={{0,2},{1,3},{2,0},{3,1},{4,6},{5,7},{6,4},{7,5},{8,10},{9,11},{10,... | collective-permute-start | bytes 786440 | tf_op jit(solution)/shard_map/ppermute | solution.py:38
  93.1 9.2 %collective-permute-start.14 = (bf16[512,1024]{1,0:T(8,128)(2,1)S(1)}, bf16[512,1024]{1,0:T(8,128)(2,1)S(1)}, u32[]{:S(2)}, u32[]{:S(2)}) collective-permute-start(bf16[512,1024]{1,0:T(8,128)(2,1)S(1)} %constant_dynamic-update-slice_fusion.5.refs_0_), channel_id=1, source_target_pairs={{0,1},{1,0},{2,3},{3,2},{4,5},{5,4},{6,7},{7,6},{8,9},{9,8},{10,11... | collective-permute-start | bytes 3145736 | tf_op jit(solution)/shard_map/ppermute | solution.py:38
  97.2 7.2 %collective-permute-start.13 = (bf16[512,1024]{1,0:T(8,128)(2,1)S(1)}, bf16[512,1024]{1,0:T(8,128)(2,1)S(1)}, u32[]{:S(2)}, u32[]{:S(2)}) collective-permute-start(bf16[512,1024]{1,0:T(8,128)(2,1)S(1)} %constant_dynamic-update-slice_fusion.3.refs_0_), channel_id=1, source_target_pairs={{0,1},{1,0},{2,3},{3,2},{4,5},{5,4},{6,7},{7,6},{8,9},{9,8},{10,11... | collective-permute-start | bytes 3145736 | tf_op jit(solution)/shard_map/ppermute | solution.py:38
  99.2 7.4 %collective-permute-start.12 = (bf16[512,1024]{1,0:T(8,128)(2,1)S(1)}, bf16[512,1024]{1,0:T(8,128)(2,1)S(1)}, u32[]{:S(2)}, u32[]{:S(2)}) collective-permute-start(bf16[512,1024]{1,0:T(8,128)(2,1)S(1)} %constant_dynamic-update-slice_fusion.1.refs_0_), channel_id=1, source_target_pairs={{0,1},{1,0},{2,3},{3,2},{4,5},{5,4},{6,7},{7,6},{8,9},{9,8},{10,11... | collective-permute-start | bytes 3145736 | tf_op jit(solution)/shard_map/ppermute | solution.py:38

commit v3 on v1

--- a/solution.py
+++ b/solution.py
@@ -104,16 +104,15 @@
                 band_ref[at : at + BLOCK, :] = (shifted * wave).astype(BF16)
 
 
-def filter_late(taps_ref, trig_ref, volt_ref, band_ref, m0, m1, m2, m3, t_ref):
+def filter_late(taps_ref, trig_ref, volt_ref, m0, m1, m2, m3, t_ref, band_ref):
     band_matrix(taps_ref, trig_ref, band_ref)
-    mine = (m0, m1, m2, m3)
     for i in range(2):
         start = i * BLOCK * FINE
         window = volt_ref[start : start + WINDOW].reshape(2 * WINDOW, S)
         out = jnp.dot(band_ref[...], window, preferred_element_type=F32).astype(BF16)
         rows = slice(i * ROWS, (i + 1) * ROWS)
-        for d in range(XS):
-            mine[d][rows, :] = out[2 * d * ROWS : (2 * d + 1) * ROWS]
+        for d, m_ref in enumerate((m0, m1, m2, m3)):
+            m_ref[rows, :] = out[2 * d * ROWS : (2 * d + 1) * ROWS]
             t_ref[d, rows, :] = out[(2 * d + 1) * ROWS : (2 * d + 2) * ROWS]
 
 
@@ -170,51 +169,56 @@
         + [block] * len(more),
         out_specs=block,
         compiler_params=pltpu.CompilerParams(vmem_limit_bytes=40 << 20),
-        cost_estimate=pl.CostEstimate(flops=2 * frames * S * 512, bytes_accessed=4 << 20, transcendentals=0),
+        cost_estimate=pl.CostEstimate(flops=16 * frames * S * 512, bytes_accessed=4 << 20, transcendentals=0),
     )(*pieces, *more)
+
+
+def spread(slabs):
+    return [slabs[0]] + [move(slabs[d], along_x(d)) for d in range(1, XS)]
 
 
 def shards(voltage, taps):
     samples_here = voltage.shape[0]
-    late = 2 * BLOCK
     volt = voltage.reshape(samples_here, 2, S)
     halo = halo_of(volt[samples_here - (TAPS - 1) * FINE :])
     params = pltpu.CompilerParams(vmem_limit_bytes=40 << 20)
-    band, ma0, ma1, ma2, ma3, ta = pl.pallas_call(
+    *late_out, band = pl.pallas_call(
         filter_late,
-        out_shape=(
-            shape(4 * FOUT * BLOCK // 2, 2 * WINDOW),
-            *[shape(2 * late, S)] * 4,
-            shape(XS, 2 * late, S),
-        ),
+        out_shape=(*[shape(2 * ROWS, S)] * XS, shape(XS, 2 * ROWS, S), shape(16 * BLOCK, 2 * WINDOW)),
         in_specs=spec(3),
-        out_specs=spec(6),
+        out_specs=spec(XS + 2),
         compiler_params=params,
         cost_estimate=pl.CostEstimate(flops=2 << 29, bytes_accessed=6 << 20, transcendentals=0),
     )(taps.reshape(1, -1), jnp.asarray(trig_table()), volt)
-    ta = move(ta, far_z)
-    ma = [ma0] + [move(m, along_x(d)) for d, m in ((1, ma1), (2, ma2), (3, ma3))]
-    mb, tb = pl.pallas_call(
+    ma = spread(late_out[:XS])
+    halo, *ma = lax.optimization_barrier((halo, *ma))
+    ma = jnp.concatenate(ma, 0)
+    ma_near = move(ma, near_z)
+    ta = move(late_out[XS], far_z)
+    first_out = pl.pallas_call(
         filter_first,
-        out_shape=(shape(XS, ROWS, S), shape(XS, ROWS, S)),
+        out_shape=[shape(XS, ROWS, S)] * 2,
         in_specs=spec(3),
         out_specs=spec(2),
         compiler_params=params,
         cost_estimate=pl.CostEstimate(flops=1 << 29, bytes_accessed=3 << 20, transcendentals=0),
     )(halo, volt, band)
+    mb, tb = first_out
+    mb_near = move(mb, near_z)
     tb = move(tb, far_z)
-    ma = jnp.concatenate(ma, 0)
-    ma = jnp.concatenate([ma, move(ma, near_z)], 0)
-    second = [jnp.concatenate([ta[d], mb[d]], 0) for d in range(XS)]
-    second = [second[0]] + [move(second[d], along_x(d)) for d in range(1, XS)]
-    second = jnp.concatenate(second, 0)
-    third = [tb[0]] + [move(tb[d], along_x(d)) for d in range(1, XS)]
-    third = jnp.concatenate(third, 0)
-    second = jnp.concatenate([second, move(second, near_z)], 0)
-    third_near = move(third, near_z)
-    acc = correlate([ma, move(ma, other_core)], None)
-    acc = correlate([second, move(second, other_core)], acc)
-    pieces = [third, move(third, other_core), third_near, move(third_near, other_core)]
+    ta, ma_near = lax.optimization_barrier((ta, ma_near))
+    second = spread([jnp.concatenate([ta[d], mb[d]], 0) for d in range(XS)])
+    tb, mb_near, *second = lax.optimization_barrier((tb, mb_near, *second))
+    ta = jnp.concatenate([slab[: 2 * ROWS] for slab in second], 0)
+    ta_near = move(ta, near_z)
+    third = spread([jnp.concatenate([tb[d], mb_near[d]], 0) for d in range(XS)])
+    tb_near = move(jnp.concatenate([slab[:ROWS] for slab in third], 0), near_z)
+    second, third = jnp.concatenate(second, 0), jnp.concatenate(third, 0)
+    ma = jnp.concatenate([ma, ma_near], 0)
+    acc = correlate([ma, move(ma, other_core), second, move(second, other_core), ta_near], None)
+    acc, ta_near, tb_near = lax.optimization_barrier((acc, ta_near, tb_near))
+    near = move(jnp.concatenate([ta_near, tb_near], 0), other_core)
+    pieces = [third, move(third, other_core), tb_near, near]
     frames = samples_here // FINE * XS * ZS * CORES
     return correlate(pieces, acc, 1.0 / frames)[None]
 

time: 147 us -> 119 us (0.81)
  waiting for transfers between devices: 57.5 us -> 39.8 us
  starting transfers between devices: 73.3 us -> 63.3 us
    ppermute x18 -> x19, waiting for transfers between devices: 57.5 us -> 39.7 us  [move(): return lax.ppermute(array, 'tm', moves(rule))]
    ppermute x18 -> x19, starting transfers between devices: 68.4 us -> 57.9 us  [move(): return lax.ppermute(array, 'tm', moves(rule))]
    pallas_call x3 -> x2, Pallas kernels: 7.92 us -> 6.71 us  [correlate(): pl.pallas_call(functools.partial(products, len(pieces), scale), grid=(4,)...]
    unnamed x16 -> x19, local copies, waits for them, and re-layouts: 3.56 us -> 3.53 us
  transfers between devices with their start and end apart: 19 -> 20, of which waited for: 11 -> 8; matrix products, arithmetic and copies ran while one was open for 1% -> 0% of each run, Pallas kernels for 3% -> 5%
where the time goes in v3:
time: 119 us
  starting transfers between devices  63.3 us (53%)
  waiting for transfers between devices  39.8 us (33%)
  Pallas kernels  9.21 us (8%)
  local copies, waits for them, and re-layouts  5.62 us (5%)
    ppermute x19, starting transfers between devices, move(): return lax.ppermute(array, 'tm', moves(rule))  57.9 us
    ppermute x19, waiting for transfers between devices, move(): return lax.ppermute(array, 'tm', moves(rule))  39.7 us
    pallas_call x2, Pallas kernels, correlate(): pl.pallas_call(functools.partial(products, len(pieces), scale), grid=(4,)...  6.71 us
    ppermute x1, starting transfers between devices, halo_of(): return lax.ppermute(tail, 'tm', pairs)  5.39 us
    unnamed x19, local copies, waits for them, and re-layouts  3.53 us
  transfers between devices with their start and end apart: 20, of which 8 were waited for; matrix products, arithmetic and copies ran while one was open for 0% of the time, Pallas kernels for 5%

profile of v3, /device:TPU:1, one launch (start us, length us, event | category | flops | bytes accessed | tf_op | source)
XLA Modules:
  0.0 118.6 jit_solution(3802843048242854579)
XLA Ops:
  0.0 1.9 %slice_bitcast_fusion = bf16[240,2,1024]{2,1,0:T(2,128)(2,1)S(1)} fusion(bf16[768,2,1,1024]{3,1,0,2:T(2,128)(2,1)} %bitcast.40), kind=kLoop, calls=%fused_computation | loop fusion | bytes 1966080 | tf_op jit(solution)/shard_map/slice | solution.py:183
  1.9 5.4 %collective-permute-start = (bf16[240,2,1024]{2,1,0:T(2,128)(2,1)S(1)}, bf16[240,2,1024]{2,1,0:T(2,128)(2,1)S(1)}, u32[]{:S(2)}, u32[]{:S(2)}) collective-permute-start(bf16[240,2,1024]{2,1,0:T(2,128)(2,1)S(1)} %slice_bitcast_fusion), channel_id=1, source_target_pairs={{0,1},{1,2},{2,3},{3,4},{4,5},{5,6},{6,7},{7,8},{8,9},{9,10},{10,1... | collective-permute-start | bytes 2949128 | tf_op jit(solution)/shard_map/ppermute | solution.py:59
  7.3 0.0 copy-start
  7.3 1.9 %copy-done = bf16[768,2,1,1024]{3,1,2,0:T(2,128)(2,1)S(1)} copy-done((bf16[768,2,1,1024]{3,1,2,0:T(2,128)(2,1)S(1)}, bf16[768,2,1,1024]{3,1,2,0:T(2,128)(2,1)}, u32[]{:S(2)}) %copy-start) | copy-done | bytes 3145752
  9.2 0.7 copy-done.2
  9.9 0.8 copy-done.3
  10.7 1.8 %shard_map.37 = (bf16[64,1024]{1,0:T(8,128)(2,1)S(1)}, bf16[64,1024]{1,0:T(8,128)(2,1)S(1)}, bf16[64,1024]{1,0:T(8,128)(2,1)S(1)}, bf16[64,1024]{1,0:T(8,128)(2,...) custom-call(f32[1,256]{1,0:T(1,128)S(1)} %bitcast.43, f32[16,1024]{1,0:T(8,128)S(1)} %copy-done.3, ...), custom_call_target="tpu_custom_call" | custom-call | flops 1073741824 | bytes 6291456 | tf_op jit(solution)/shard_map/pallas_call | solution.py:185
  12.5 3.1 %collective-permute-start.1 = (bf16[64,1024]{1,0:T(8,128)(2,1)S(1)}, bf16[64,1024]{1,0:T(8,128)(2,1)S(1)}, u32[]{:S(2)}, u32[]{:S(2)}) collective-permute-start(bf16[64,1024]{1,0:T(8,128)(2,1)S(1)} %get-tuple-element.30), channel_id=1, source_target_pairs={{0,8},{1,9},{2,10},{3,11},{4,12},{5,13},{6,14},{7,15},{8,16},{9,17... | collective-permute-start | bytes 393224 | tf_op jit(solution)/shard_map/ppermute | solution.py:38
  15.6 4.4 %collective-permute-start.2 = (bf16[64,1024]{1,0:T(8,128)(2,1)S(1)}, bf16[64,1024]{1,0:T(8,128)(2,1)S(1)}, u32[]{:S(2)}, u32[]{:S(2)}) collective-permute-start(bf16[64,1024]{1,0:T(8,128)(2,1)S(1)} %get-tuple-element.31), channel_id=1, source_target_pairs={{0,16},{1,17},{2,18},{3,19},{4,20},{5,21},{6,22},{7,23},{8,24},{9,... | collective-permute-start | bytes 393224 | tf_op jit(solution)/shard_map/ppermute | solution.py:38
  19.9 3.1 %collective-permute-start.3 = (bf16[64,1024]{1,0:T(8,128)(2,1)S(1)}, bf16[64,1024]{1,0:T(8,128)(2,1)S(1)}, u32[]{:S(2)}, u32[]{:S(2)}) collective-permute-start(bf16[64,1024]{1,0:T(8,128)(2,1)S(1)} %get-tuple-element.32), channel_id=1, source_target_pairs={{0,24},{1,25},{2,26},{3,27},{4,28},{5,29},{6,30},{7,31},{8,0},{9,1... | collective-permute-start | bytes 393224 | tf_op jit(solution)/shard_map/ppermute | solution.py:38
  23.0 5.8 %collective-permute-start.6 = (bf16[4,64,1024]{2,1,0:T(8,128)(2,1)S(1)}, bf16[4,64,1024]{2,1,0:T(8,128)(2,1)S(1)}, u32[]{:S(2)}, u32[]{:S(2)}) collective-permute-start(bf16[4,64,1024]{2,1,0:T(8,128)(2,1)S(1)} %get-tuple-element.37), channel_id=1, source_target_pairs={{0,4},{1,5},{2,6},{3,7},{4,0},{5,1},{6,2},{7,3},{8,12},{9,13},{10,... | collective-permute-start | bytes 1572872 | tf_op jit(solution)/shard_map/ppermute | solution.py:38
  28.8 0.0 collective-permute-done.1
  28.8 1.2 %collective-permute-done.2 = bf16[64,1024]{1,0:T(8,128)(2,1)S(1)} collective-permute-done((bf16[64,1024]{1,0:T(8,128)(2,1)S(1)}, bf16[64,1024]{1,0:T(8,128)(2,1)S(1)}, u32[]{:S(2)}, u32[]{:S(2)}) %collective-permute-start.2) | collective-permute-done | bytes 131104 | tf_op jit(solution)/shard_map/ppermute | solution.py:38
  30.1 0.0 collective-permute-done.3
  30.1 0.0 collective-permute-done.halo_ref
  30.1 1.9 %collective-permute-start.7 = (bf16[256,1024]{1,0:T(8,128)(2,1)S(1)}, bf16[256,1024]{1,0:T(8,128)(2,1)S(1)}, u32[]{:S(2)}, u32[]{:S(2)}) collective-permute-start(bf16[256,1024]{1,0:T(8,128)(2,1)S(1)} %pad_maximum_fusion.1), channel_id=1, source_target_pairs={{0,2},{1,3},{2,0},{3,1},{4,6},{5,7},{6,4},{7,5},{8,10},{9,11},{10,... | collective-permute-start | bytes 1572872 | tf_op jit(solution)/shard_map/ppermute | solution.py:38
  32.1 0.7 shard_map.38
  32.8 3.4 %collective-permute-start.5 = (bf16[4,32,1024]{2,1,0:T(8,128)(2,1)S(1)}, bf16[4,32,1024]{2,1,0:T(8,128)(2,1)S(1)}, u32[]{:S(2)}, u32[]{:S(2)}) collective-permute-start(bf16[4,32,1024]{2,1,0:T(8,128)(2,1)S(1)} %get-tuple-element.36), channel_id=1, source_target_pairs={{0,2},{1,3},{2,0},{3,1},{4,6},{5,7},{6,4},{7,5},{8,10},{9,11},{10,... | collective-permute-start | bytes 786440 | tf_op jit(solution)/shard_map/ppermute | solution.py:38
  36.2 1.9 %collective-permute-start.4 = (bf16[4,32,1024]{2,1,0:T(8,128)(2,1)S(1)}, bf16[4,32,1024]{2,1,0:T(8,128)(2,1)S(1)}, u32[]{:S(2)}, u32[]{:S(2)}) collective-permute-start(bf16[4,32,1024]{2,1,0:T(8,128)(2,1)S(1)} %get-tuple-element.35), channel_id=1, source_target_pairs={{0,4},{1,5},{2,6},{3,7},{4,0},{5,1},{6,2},{7,3},{8,12},{9,13},{10,... | collective-permute-start | bytes 786440 | tf_op jit(solution)/shard_map/ppermute | solution.py:38
  38.2 14.2 %collective-permute-done.6 = bf16[4,64,1024]{2,1,0:T(8,128)(2,1)S(1)} collective-permute-done((bf16[4,64,1024]{2,1,0:T(8,128)(2,1)S(1)}, bf16[4,64,1024]{2,1,0:T(8,128)(2,1)S(1)}, u32[]{:S(2)}, u32[]{:S(2)}) %collective-permute-start.6) | collective-permute-done | bytes 524320 | tf_op jit(solution)/shard_map/ppermute | solution.py:38
  52.4 9.2 %collective-permute-done.7 = bf16[256,1024]{1,0:T(8,128)(2,1)S(1)} collective-permute-done((bf16[256,1024]{1,0:T(8,128)(2,1)S(1)}, bf16[256,1024]{1,0:T(8,128)(2,1)S(1)}, u32[]{:S(2)}, u32[]{:S(2)}) %collective-permute-start.7) | collective-permute-done | bytes 524320 | tf_op jit(solution)/shard_map/ppermute | solution.py:38
  61.7 1.9 %collective-permute-start.10 = (bf16[96,1024]{1,0:T(8,128)(2,1)S(1)}, bf16[96,1024]{1,0:T(8,128)(2,1)S(1)}, u32[]{:S(2)}, u32[]{:S(2)}) collective-permute-start(bf16[96,1024]{1,0:T(8,128)(2,1)S(1)} %pad_maximum_fusion.7), channel_id=1, source_target_pairs={{0,24},{1,25},{2,26},{3,27},{4,28},{5,29},{6,30},{7,31},{8,0},{9,1... | collective-permute-start | bytes 589832 | tf_op jit(solution)/shard_map/ppermute | solution.py:38
  63.7 2.5 %collective-permute-start.9 = (bf16[96,1024]{1,0:T(8,128)(2,1)S(1)}, bf16[96,1024]{1,0:T(8,128)(2,1)S(1)}, u32[]{:S(2)}, u32[]{:S(2)}) collective-permute-start(bf16[96,1024]{1,0:T(8,128)(2,1)S(1)} %pad_maximum_fusion.6), channel_id=1, source_target_pairs={{0,16},{1,17},{2,18},{3,19},{4,20},{5,21},{6,22},{7,23},{8,24},{9,... | collective-permute-start | bytes 589832 | tf_op jit(solution)/shard_map/ppermute | solution.py:38
  66.2 2.7 %collective-permute-start.8 = (bf16[96,1024]{1,0:T(8,128)(2,1)S(1)}, bf16[96,1024]{1,0:T(8,128)(2,1)S(1)}, u32[]{:S(2)}, u32[]{:S(2)}) collective-permute-start(bf16[96,1024]{1,0:T(8,128)(2,1)S(1)} %pad_maximum_fusion.5), channel_id=1, source_target_pairs={{0,8},{1,9},{2,10},{3,11},{4,12},{5,13},{6,14},{7,15},{8,16},{9,17... | collective-permute-start | bytes 589832 | tf_op jit(solution)/shard_map/ppermute | solution.py:38
  69.0 0.0 collective-permute-done.5
  69.1 4.6 %collective-permute-start.15 = (bf16[512,1024]{1,0:T(8,128)(2,1)S(1)}, bf16[512,1024]{1,0:T(8,128)(2,1)S(1)}, u32[]{:S(2)}, u32[]{:S(2)}) collective-permute-start(bf16[512,1024]{1,0:T(8,128)(2,1)S(1)} %constant_dynamic-update-slice_fusion.4.refs_0_), channel_id=1, source_target_pairs={{0,1},{1,0},{2,3},{3,2},{4,5},{5,4},{6,7},{7,6},{8,9},{9,8},{10,11... | collective-permute-start | bytes 3145736 | tf_op jit(solution)/shard_map/ppermute | solution.py:38
  73.7 0.0 collective-permute-done.4
  73.7 0.0 collective-permute-done.9
  73.7 2.9 %collective-permute-done.8 = bf16[96,1024]{1,0:T(8,128)(2,1)S(1)} collective-permute-done((bf16[96,1024]{1,0:T(8,128)(2,1)S(1)}, bf16[96,1024]{1,0:T(8,128)(2,1)S(1)}, u32[]{:S(2)}, u32[]{:S(2)}) %collective-permute-start.8) | collective-permute-done | bytes 196640 | tf_op jit(solution)/shard_map/ppermute | solution.py:38
  76.7 3.6 %collective-permute-start.13 = (bf16[64,1024]{1,0:T(8,128)(2,1)S(1)}, bf16[64,1024]{1,0:T(8,128)(2,1)S(1)}, u32[]{:S(2)}, u32[]{:S(2)}) collective-permute-start(bf16[64,1024]{1,0:T(8,128)(2,1)S(1)} %pad_maximum_fusion.10), channel_id=1, source_target_pairs={{0,24},{1,25},{2,26},{3,27},{4,28},{5,29},{6,30},{7,31},{8,0},{9,1... | collective-permute-start | bytes 393224 | tf_op jit(solution)/shard_map/ppermute | solution.py:38
  80.4 1.9 %collective-permute-start.17 = (bf16[256,1024]{1,0:T(8,128)(2,1)S(1)}, bf16[256,1024]{1,0:T(8,128)(2,1)S(1)}, u32[]{:S(2)}, u32[]{:S(2)}) collective-permute-start(bf16[256,1024]{1,0:T(8,128)(2,1)S(1)} %pad_maximum_fusion.2), channel_id=1, source_target_pairs={{0,2},{1,3},{2,0},{3,1},{4,6},{5,7},{6,4},{7,5},{8,10},{9,11},{10,... | collective-permute-start | bytes 1572872 | tf_op jit(solution)/shard_map/ppermute | solution.py:38
  82.4 4.4 %collective-permute-start.16 = (bf16[384,1024]{1,0:T(8,128)(2,1)S(1)}, bf16[384,1024]{1,0:T(8,128)(2,1)S(1)}, u32[]{:S(2)}, u32[]{:S(2)}) collective-permute-start(bf16[384,1024]{1,0:T(8,128)(2,1)S(1)} %constant_dynamic-update-slice_fusion.9.refs_2_), channel_id=1, source_target_pairs={{0,1},{1,0},{2,3},{3,2},{4,5},{5,4},{6,7},{7,6},{8,9},{9,8},{10,11... | collective-permute-start | bytes 2359304 | tf_op jit(solution)/shard_map/ppermute | solution.py:38
  86.8 1.9 %collective-permute-start.12 = (bf16[64,1024]{1,0:T(8,128)(2,1)S(1)}, bf16[64,1024]{1,0:T(8,128)(2,1)S(1)}, u32[]{:S(2)}, u32[]{:S(2)}) collective-permute-start(bf16[64,1024]{1,0:T(8,128)(2,1)S(1)} %pad_maximum_fusion.9), channel_id=1, source_target_pairs={{0,16},{1,17},{2,18},{3,19},{4,20},{5,21},{6,22},{7,23},{8,24},{9,... | collective-permute-start | bytes 393224 | tf_op jit(solution)/shard_map/ppermute | solution.py:38
  88.8 0.0 collective-permute-done.13
  88.8 2.2 %collective-permute-start.11 = (bf16[64,1024]{1,0:T(8,128)(2,1)S(1)}, bf16[64,1024]{1,0:T(8,128)(2,1)S(1)}, u32[]{:S(2)}, u32[]{:S(2)}) collective-permute-start(bf16[64,1024]{1,0:T(8,128)(2,1)S(1)} %pad_maximum_fusion.8), channel_id=1, source_target_pairs={{0,8},{1,9},{2,10},{3,11},{4,12},{5,13},{6,14},{7,15},{8,16},{9,17... | collective-permute-start | bytes 393224 | tf_op jit(solution)/shard_map/ppermute | solution.py:38
  91.0 4.3 %collective-permute-done.12 = bf16[64,1024]{1,0:T(8,128)(2,1)S(1)} collective-permute-done((bf16[64,1024]{1,0:T(8,128)(2,1)S(1)}, bf16[64,1024]{1,0:T(8,128)(2,1)S(1)}, u32[]{:S(2)}, u32[]{:S(2)}) %collective-permute-start.12) | collective-permute-done | bytes 131104 | tf_op jit(solution)/shard_map/ppermute | solution.py:38
  95.4 3.2 %collective-permute-done.11 = bf16[64,1024]{1,0:T(8,128)(2,1)S(1)} collective-permute-done((bf16[64,1024]{1,0:T(8,128)(2,1)S(1)}, bf16[64,1024]{1,0:T(8,128)(2,1)S(1)}, u32[]{:S(2)}, u32[]{:S(2)}) %collective-permute-start.11) | collective-permute-done | bytes 131104 | tf_op jit(solution)/shard_map/ppermute | solution.py:38
  98.5 3.6 %collective-permute-start.18 = (bf16[128,1024]{1,0:T(8,128)(2,1)S(1)}, bf16[128,1024]{1,0:T(8,128)(2,1)S(1)}, u32[]{:S(2)}, u32[]{:S(2)}) collective-permute-start(bf16[128,1024]{1,0:T(8,128)(2,1)S(1)} %pad_maximum_fusion.3), channel_id=1, source_target_pairs={{0,2},{1,3},{2,0},{3,1},{4,6},{5,7},{6,4},{7,5},{8,10},{9,11},{10,... | collective-permute-start | bytes 786440 | tf_op jit(solution)/shard_map/ppermute | solution.py:38
  102.2 0.0 collective-permute-done.17.refs_4_
  102.2 0.0 collective-permute-done.16.refs_3_
  102.2 3.4 %shard_map.39.refs_4_ = f32[2,1024,256]{2,1,0:T(8,128)S(1)} custom-call(bf16[512,1024]{1,0:T(8,128)(2,1)S(1)} %constant_dynamic-update-slice_fusion.4.refs_0_, bf16[512,1024]{1,0:T(8,128)(2,1)S(1)} %collective-permute-done.15.refs_1_, bf16[384,1024]{1,0:T(8,128)(2,1)S(1)} %constant_dynamic-update-slice_fusion.9.refs_2_, ...), custom_call_target="tpu_custom_call" | custom-call | flops 17179869184 | bytes 4194304 | tf_op jit(solution)/shard_map/pallas_call | solution.py:164
  105.6 2.8 %collective-permute-done.18.refs_2_ = bf16[128,1024]{1,0:T(8,128)(2,1)S(1)} collective-permute-done((bf16[128,1024]{1,0:T(8,128)(2,1)S(1)}, bf16[128,1024]{1,0:T(8,128)(2,1)S(1)}, u32[]{:S(2)}, u32[]{:S(2)}) %collective-permute-start.18) | collective-permute-done | bytes 262176 | tf_op jit(solution)/shard_map/ppermute | solution.py:38
  108.5 0.1 pad_maximum_fusion
  108.5 2.9 %collective-permute-start.19 = (bf16[384,1024]{1,0:T(8,128)(2,1)S(1)}, bf16[384,1024]{1,0:T(8,128)(2,1)S(1)}, u32[]{:S(2)}, u32[]{:S(2)}) collective-permute-start(bf16[384,1024]{1,0:T(8,128)(2,1)S(1)} %pad_maximum_fusion), channel_id=1, source_target_pairs={{0,1},{1,0},{2,3},{3,2},{4,5},{5,4},{6,7},{7,6},{8,9},{9,8},{10,11... | collective-permute-start | bytes 2359304 | tf_op jit(solution)/shard_map/ppermute | solution.py:38
  111.5 1.9 %collective-permute-start.14 = (bf16[256,1024]{1,0:T(8,128)(2,1)S(1)}, bf16[256,1024]{1,0:T(8,128)(2,1)S(1)}, u32[]{:S(2)}, u32[]{:S(2)}) collective-permute-start(bf16[256,1024]{1,0:T(8,128)(2,1)S(1)} %constant_dynamic-update-slice_fusion.refs_0_), channel_id=1, source_target_pairs={{0,1},{1,0},{2,3},{3,2},{4,5},{5,4},{6,7},{7,6},{8,9},{9,8},{10,11... | collective-permute-start | bytes 1572872 | tf_op jit(solution)/shard_map/ppermute | solution.py:38
  113.4 1.9 %collective-permute-done.14.refs_1_ = bf16[256,1024]{1,0:T(8,128)(2,1)S(1)} collective-permute-done((bf16[256,1024]{1,0:T(8,128)(2,1)S(1)}, bf16[256,1024]{1,0:T(8,128)(2,1)S(1)}, u32[]{:S(2)}, u32[]{:S(2)}) %collective-permute-start.14) | collective-permute-done | bytes 524320 | tf_op jit(solution)/shard_map/ppermute | solution.py:38
  115.3 0.0 collective-permute-done.19.refs_3_
  115.3 3.3 %shard_map.40 = f32[2,1024,256]{2,1,0:T(8,128)} custom-call(bf16[256,1024]{1,0:T(8,128)(2,1)S(1)} %constant_dynamic-update-slice_fusion.refs_0_, bf16[256,1024]{1,0:T(8,128)(2,1)S(1)} %collective-permute-done.14.refs_1_, bf16[128,1024]{1,0:T(8,128)(2,1)S(1)} %collective-permute-done.18.refs_2_, bf16[384,1024]{1,0:T(8,128)(2,1)S(1)} %collective-permute-done.19.refs_3_, ...), custom_call_target="tpu_custom_call" | custom-call | flops 8589934592 | bytes 4194304 | tf_op jit(solution)/shard_map/pallas_call | solution.py:164
  (40 shorter events, 0.5 us)
Async XLA Ops:
  1.9 28.2 %collective-permute-start = (bf16[240,2,1024]{2,1,0:T(2,128)(2,1)S(1)}, bf16[240,2,1024]{2,1,0:T(2,128)(2,1)S(1)}, u32[]{:S(2)}, u32[]{:S(2)}) collective-permute-start(bf16[240,2,1024]{2,1,0:T(2,128)(2,1)S(1)} %slice_bitcast_fusion), channel_id=1, source_target_pairs={{0,1},{1,2},{2,3},{3,4},{4,5},{5,6},{6,7},{7,8},{8,9},{9,10},{10,1... | collective-permute-start | bytes 2949128 | tf_op jit(solution)/shard_map/ppermute | solution.py:59
  7.3 1.9 %copy-start = (bf16[768,2,1,1024]{3,1,2,0:T(2,128)(2,1)S(1)}, bf16[768,2,1,1024]{3,1,2,0:T(2,128)(2,1)}, u32[]{:S(2)}) copy-start(bf16[768,2,1,1024]{3,1,2,0:T(2,128)(2,1)} %param.3) | copy-start | bytes 9437188
  9.2 0.7 copy-start.2
  9.9 0.8 copy-start.3
  10.7 21.4 %copy-start.1 = (bf16[768,2,1,1024]{3,1,2,0:T(2,128)(2,1)S(1)}, bf16[768,2,1,1024]{3,1,2,0:T(2,128)(2,1)}, u32[]{:S(2)}) copy-start(bf16[768,2,1,1024]{3,1,2,0:T(2,128)(2,1)} %param.3) | copy-start | bytes 9437188
  12.5 16.4 %collective-permute-start.1 = (bf16[64,1024]{1,0:T(8,128)(2,1)S(1)}, bf16[64,1024]{1,0:T(8,128)(2,1)S(1)}, u32[]{:S(2)}, u32[]{:S(2)}) collective-permute-start(bf16[64,1024]{1,0:T(8,128)(2,1)S(1)} %get-tuple-element.30), channel_id=1, source_target_pairs={{0,8},{1,9},{2,10},{3,11},{4,12},{5,13},{6,14},{7,15},{8,16},{9,17... | collective-permute-start | bytes 393224 | tf_op jit(solution)/shard_map/ppermute | solution.py:38
  15.6 14.5 %collective-permute-start.2 = (bf16[64,1024]{1,0:T(8,128)(2,1)S(1)}, bf16[64,1024]{1,0:T(8,128)(2,1)S(1)}, u32[]{:S(2)}, u32[]{:S(2)}) collective-permute-start(bf16[64,1024]{1,0:T(8,128)(2,1)S(1)} %get-tuple-element.31), channel_id=1, source_target_pairs={{0,16},{1,17},{2,18},{3,19},{4,20},{5,21},{6,22},{7,23},{8,24},{9,... | collective-permute-start | bytes 393224 | tf_op jit(solution)/shard_map/ppermute | solution.py:38
  19.9 10.1 %collective-permute-start.3 = (bf16[64,1024]{1,0:T(8,128)(2,1)S(1)}, bf16[64,1024]{1,0:T(8,128)(2,1)S(1)}, u32[]{:S(2)}, u32[]{:S(2)}) collective-permute-start(bf16[64,1024]{1,0:T(8,128)(2,1)S(1)} %get-tuple-element.32), channel_id=1, source_target_pairs={{0,24},{1,25},{2,26},{3,27},{4,28},{5,29},{6,30},{7,31},{8,0},{9,1... | collective-permute-start | bytes 393224 | tf_op jit(solution)/shard_map/ppermute | solution.py:38
  23.0 29.4 %collective-permute-start.6 = (bf16[4,64,1024]{2,1,0:T(8,128)(2,1)S(1)}, bf16[4,64,1024]{2,1,0:T(8,128)(2,1)S(1)}, u32[]{:S(2)}, u32[]{:S(2)}) collective-permute-start(bf16[4,64,1024]{2,1,0:T(8,128)(2,1)S(1)} %get-tuple-element.37), channel_id=1, source_target_pairs={{0,4},{1,5},{2,6},{3,7},{4,0},{5,1},{6,2},{7,3},{8,12},{9,13},{10,... | collective-permute-start | bytes 1572872 | tf_op jit(solution)/shard_map/ppermute | solution.py:38
  30.1 31.5 %collective-permute-start.7 = (bf16[256,1024]{1,0:T(8,128)(2,1)S(1)}, bf16[256,1024]{1,0:T(8,128)(2,1)S(1)}, u32[]{:S(2)}, u32[]{:S(2)}) collective-permute-start(bf16[256,1024]{1,0:T(8,128)(2,1)S(1)} %pad_maximum_fusion.1), channel_id=1, source_target_pairs={{0,2},{1,3},{2,0},{3,1},{4,6},{5,7},{6,4},{7,5},{8,10},{9,11},{10,... | collective-permute-start | bytes 1572872 | tf_op jit(solution)/shard_map/ppermute | solution.py:38
  32.8 36.2 %collective-permute-start.5 = (bf16[4,32,1024]{2,1,0:T(8,128)(2,1)S(1)}, bf16[4,32,1024]{2,1,0:T(8,128)(2,1)S(1)}, u32[]{:S(2)}, u32[]{:S(2)}) collective-permute-start(bf16[4,32,1024]{2,1,0:T(8,128)(2,1)S(1)} %get-tuple-element.36), channel_id=1, source_target_pairs={{0,2},{1,3},{2,0},{3,1},{4,6},{5,7},{6,4},{7,5},{8,10},{9,11},{10,... | collective-permute-start | bytes 786440 | tf_op jit(solution)/shard_map/ppermute | solution.py:38
  36.2 37.4 %collective-permute-start.4 = (bf16[4,32,1024]{2,1,0:T(8,128)(2,1)S(1)}, bf16[4,32,1024]{2,1,0:T(8,128)(2,1)S(1)}, u32[]{:S(2)}, u32[]{:S(2)}) collective-permute-start(bf16[4,32,1024]{2,1,0:T(8,128)(2,1)S(1)} %get-tuple-element.35), channel_id=1, source_target_pairs={{0,4},{1,5},{2,6},{3,7},{4,0},{5,1},{6,2},{7,3},{8,12},{9,13},{10,... | collective-permute-start | bytes 786440 | tf_op jit(solution)/shard_map/ppermute | solution.py:38
  61.7 12.0 %collective-permute-start.10 = (bf16[96,1024]{1,0:T(8,128)(2,1)S(1)}, bf16[96,1024]{1,0:T(8,128)(2,1)S(1)}, u32[]{:S(2)}, u32[]{:S(2)}) collective-permute-start(bf16[96,1024]{1,0:T(8,128)(2,1)S(1)} %pad_maximum_fusion.7), channel_id=1, source_target_pairs={{0,24},{1,25},{2,26},{3,27},{4,28},{5,29},{6,30},{7,31},{8,0},{9,1... | collective-permute-start | bytes 589832 | tf_op jit(solution)/shard_map/ppermute | solution.py:38
  63.7 10.0 %collective-permute-start.9 = (bf16[96,1024]{1,0:T(8,128)(2,1)S(1)}, bf16[96,1024]{1,0:T(8,128)(2,1)S(1)}, u32[]{:S(2)}, u32[]{:S(2)}) collective-permute-start(bf16[96,1024]{1,0:T(8,128)(2,1)S(1)} %pad_maximum_fusion.6), channel_id=1, source_target_pairs={{0,16},{1,17},{2,18},{3,19},{4,20},{5,21},{6,22},{7,23},{8,24},{9,... | collective-permute-start | bytes 589832 | tf_op jit(solution)/shard_map/ppermute | solution.py:38
  66.2 10.3 %collective-permute-start.8 = (bf16[96,1024]{1,0:T(8,128)(2,1)S(1)}, bf16[96,1024]{1,0:T(8,128)(2,1)S(1)}, u32[]{:S(2)}, u32[]{:S(2)}) collective-permute-start(bf16[96,1024]{1,0:T(8,128)(2,1)S(1)} %pad_maximum_fusion.5), channel_id=1, source_target_pairs={{0,8},{1,9},{2,10},{3,11},{4,12},{5,13},{6,14},{7,15},{8,16},{9,17... | collective-permute-start | bytes 589832 | tf_op jit(solution)/shard_map/ppermute | solution.py:38
  69.1 33.2 %collective-permute-start.15 = (bf16[512,1024]{1,0:T(8,128)(2,1)S(1)}, bf16[512,1024]{1,0:T(8,128)(2,1)S(1)}, u32[]{:S(2)}, u32[]{:S(2)}) collective-permute-start(bf16[512,1024]{1,0:T(8,128)(2,1)S(1)} %constant_dynamic-update-slice_fusion.4.refs_0_), channel_id=1, source_target_pairs={{0,1},{1,0},{2,3},{3,2},{4,5},{5,4},{6,7},{7,6},{8,9},{9,8},{10,11... | collective-permute-start | bytes 3145736 | tf_op jit(solution)/shard_map/ppermute | solution.py:38
  76.7 12.1 %collective-permute-start.13 = (bf16[64,1024]{1,0:T(8,128)(2,1)S(1)}, bf16[64,1024]{1,0:T(8,128)(2,1)S(1)}, u32[]{:S(2)}, u32[]{:S(2)}) collective-permute-start(bf16[64,1024]{1,0:T(8,128)(2,1)S(1)} %pad_maximum_fusion.10), channel_id=1, source_target_pairs={{0,24},{1,25},{2,26},{3,27},{4,28},{5,29},{6,30},{7,31},{8,0},{9,1... | collective-permute-start | bytes 393224 | tf_op jit(solution)/shard_map/ppermute | solution.py:38
  80.4 21.8 %collective-permute-start.17 = (bf16[256,1024]{1,0:T(8,128)(2,1)S(1)}, bf16[256,1024]{1,0:T(8,128)(2,1)S(1)}, u32[]{:S(2)}, u32[]{:S(2)}) collective-permute-start(bf16[256,1024]{1,0:T(8,128)(2,1)S(1)} %pad_maximum_fusion.2), channel_id=1, source_target_pairs={{0,2},{1,3},{2,0},{3,1},{4,6},{5,7},{6,4},{7,5},{8,10},{9,11},{10,... | collective-permute-start | bytes 1572872 | tf_op jit(solution)/shard_map/ppermute | solution.py:38
  82.4 19.8 %collective-permute-start.16 = (bf16[384,1024]{1,0:T(8,128)(2,1)S(1)}, bf16[384,1024]{1,0:T(8,128)(2,1)S(1)}, u32[]{:S(2)}, u32[]{:S(2)}) collective-permute-start(bf16[384,1024]{1,0:T(8,128)(2,1)S(1)} %constant_dynamic-update-slice_fusion.9.refs_2_), channel_id=1, source_target_pairs={{0,1},{1,0},{2,3},{3,2},{4,5},{5,4},{6,7},{7,6},{8,9},{9,8},{10,11... | collective-permute-start | bytes 2359304 | tf_op jit(solution)/shard_map/ppermute | solution.py:38
  86.8 8.5 %collective-permute-start.12 = (bf16[64,1024]{1,0:T(8,128)(2,1)S(1)}, bf16[64,1024]{1,0:T(8,128)(2,1)S(1)}, u32[]{:S(2)}, u32[]{:S(2)}) collective-permute-start(bf16[64,1024]{1,0:T(8,128)(2,1)S(1)} %pad_maximum_fusion.9), channel_id=1, source_target_pairs={{0,16},{1,17},{2,18},{3,19},{4,20},{5,21},{6,22},{7,23},{8,24},{9,... | collective-permute-start | bytes 393224 | tf_op jit(solution)/shard_map/ppermute | solution.py:38
  88.8 9.7 %collective-permute-start.11 = (bf16[64,1024]{1,0:T(8,128)(2,1)S(1)}, bf16[64,1024]{1,0:T(8,128)(2,1)S(1)}, u32[]{:S(2)}, u32[]{:S(2)}) collective-permute-start(bf16[64,1024]{1,0:T(8,128)(2,1)S(1)} %pad_maximum_fusion.8), channel_id=1, source_target_pairs={{0,8},{1,9},{2,10},{3,11},{4,12},{5,13},{6,14},{7,15},{8,16},{9,17... | collective-permute-start | bytes 393224 | tf_op jit(solution)/shard_map/ppermute | solution.py:38
  98.5 9.9 %collective-permute-start.18 = (bf16[128,1024]{1,0:T(8,128)(2,1)S(1)}, bf16[128,1024]{1,0:T(8,128)(2,1)S(1)}, u32[]{:S(2)}, u32[]{:S(2)}) collective-permute-start(bf16[128,1024]{1,0:T(8,128)(2,1)S(1)} %pad_maximum_fusion.3), channel_id=1, source_target_pairs={{0,2},{1,3},{2,0},{3,1},{4,6},{5,7},{6,4},{7,5},{8,10},{9,11},{10,... | collective-permute-start | bytes 786440 | tf_op jit(solution)/shard_map/ppermute | solution.py:38
  108.5 6.7 %collective-permute-start.19 = (bf16[384,1024]{1,0:T(8,128)(2,1)S(1)}, bf16[384,1024]{1,0:T(8,128)(2,1)S(1)}, u32[]{:S(2)}, u32[]{:S(2)}) collective-permute-start(bf16[384,1024]{1,0:T(8,128)(2,1)S(1)} %pad_maximum_fusion), channel_id=1, source_target_pairs={{0,1},{1,0},{2,3},{3,2},{4,5},{5,4},{6,7},{7,6},{8,9},{9,8},{10,11... | collective-permute-start | bytes 2359304 | tf_op jit(solution)/shard_map/ppermute | solution.py:38
  111.5 3.8 %collective-permute-start.14 = (bf16[256,1024]{1,0:T(8,128)(2,1)S(1)}, bf16[256,1024]{1,0:T(8,128)(2,1)S(1)}, u32[]{:S(2)}, u32[]{:S(2)}) collective-permute-start(bf16[256,1024]{1,0:T(8,128)(2,1)S(1)} %constant_dynamic-update-slice_fusion.refs_0_), channel_id=1, source_target_pairs={{0,1},{1,0},{2,3},{3,2},{4,5},{5,4},{6,7},{7,6},{8,9},{9,8},{10,11... | collective-permute-start | bytes 1572872 | tf_op jit(solution)/shard_map/ppermute | solution.py:38

commit v4 on v3

--- a/solution.py
+++ b/solution.py
@@ -102,6 +102,13 @@
                 at = ((d * 2 + other) * 2 + ro) * BLOCK
                 wave = trig_ref[pl.ds(k * 2 + ro, 1), :]
                 band_ref[at : at + BLOCK, :] = (shifted * wave).astype(BF16)
+
+
+def tail_copy(volt_ref, out_ref, sem):
+    n = out_ref.shape[0]
+    copy = pltpu.make_async_copy(volt_ref.at[pl.ds(volt_ref.shape[0] - n, n)], out_ref, sem)
+    copy.start()
+    copy.wait()
 
 
 def filter_late(taps_ref, trig_ref, volt_ref, m0, m1, m2, m3, t_ref, band_ref):
@@ -180,8 +187,16 @@
 def shards(voltage, taps):
     samples_here = voltage.shape[0]
     volt = voltage.reshape(samples_here, 2, S)
-    halo = halo_of(volt[samples_here - (TAPS - 1) * FINE :])
     params = pltpu.CompilerParams(vmem_limit_bytes=40 << 20)
+    tail = pl.pallas_call(
+        tail_copy,
+        out_shape=shape((TAPS - 1) * FINE, 2, S),
+        in_specs=[pl.BlockSpec(memory_space=VMEM)],
+        out_specs=pl.BlockSpec(memory_space=VMEM),
+        scratch_shapes=[pltpu.SemaphoreType.DMA],
+        compiler_params=params,
+    )(volt)
+    halo = halo_of(tail)
     *late_out, band = pl.pallas_call(
         filter_late,
         out_shape=(*[shape(2 * ROWS, S)] * XS, shape(XS, 2 * ROWS, S), shape(16 * BLOCK, 2 * WINDOW)),
@@ -193,7 +208,7 @@
     ma = spread(late_out[:XS])
     halo, *ma = lax.optimization_barrier((halo, *ma))
     ma = jnp.concatenate(ma, 0)
-    ma_near = move(ma, near_z)
+    ma_near, ma_near2 = move(ma[:ROWS], near_z), move(ma[ROWS:], near_z)
     ta = move(late_out[XS], far_z)
     first_out = pl.pallas_call(
         filter_first,
@@ -208,17 +223,17 @@
     tb = move(tb, far_z)
     ta, ma_near = lax.optimization_barrier((ta, ma_near))
     second = spread([jnp.concatenate([ta[d], mb[d]], 0) for d in range(XS)])
-    tb, mb_near, *second = lax.optimization_barrier((tb, mb_near, *second))
+    tb, mb_near, ma_near2, *second = lax.optimization_barrier((tb, mb_near, ma_near2, *second))
     ta = jnp.concatenate([slab[: 2 * ROWS] for slab in second], 0)
     ta_near = move(ta, near_z)
     third = spread([jnp.concatenate([tb[d], mb_near[d]], 0) for d in range(XS)])
     tb_near = move(jnp.concatenate([slab[:ROWS] for slab in third], 0), near_z)
     second, third = jnp.concatenate(second, 0), jnp.concatenate(third, 0)
-    ma = jnp.concatenate([ma, ma_near], 0)
-    acc = correlate([ma, move(ma, other_core), second, move(second, other_core), ta_near], None)
+    ma = jnp.concatenate([ma, ma_near, ma_near2, second], 0)
+    acc = correlate([ma, move(ma, other_core), ta_near], None)
     acc, ta_near, tb_near = lax.optimization_barrier((acc, ta_near, tb_near))
-    near = move(jnp.concatenate([ta_near, tb_near], 0), other_core)
-    pieces = [third, move(third, other_core), tb_near, near]
+    last = jnp.concatenate([tb_near, third], 0)
+    pieces = [last, move(jnp.concatenate([last, ta_near], 0), other_core)]
     frames = samples_here // FINE * XS * ZS * CORES
     return correlate(pieces, acc, 1.0 / frames)[None]
 

time: 119 us -> 110 us (0.924)
  waiting for transfers between devices: 39.8 us -> 36.3 us
  local copies, waits for them, and re-layouts: 5.62 us -> 2.35 us
  starting transfers between devices: 63.3 us -> 60.4 us
    ppermute x19 -> x18, waiting for transfers between devices: 39.7 us -> 36.3 us  [move(): return lax.ppermute(array, 'tm', moves(rule))]
    ppermute x19 -> x18, starting transfers between devices: 57.9 us -> 55 us  [move(): return lax.ppermute(array, 'tm', moves(rule))]
    slice x1, local copies, waits for them, and re-layouts: 1.88 us -> 0.01 us  [shards(): ma_near, ma_near2 = (move(ma[:ROWS], near_z), move(ma[ROWS:], near_z))]
    unnamed x19 -> x21, local copies, waits for them, and re-layouts: 3.53 us -> 2.14 us
  transfers between devices with their start and end apart: 20 -> 19, of which waited for: 8 -> 9; matrix products, arithmetic and copies ran while one was open for 0% -> 0% of each run, Pallas kernels for 5% -> 5%
where the time goes in v4:
time: 110 us; the launch traced here: 109 us
  starting transfers between devices  60.4 us (55%)
  waiting for transfers between devices  36.3 us (33%)
  Pallas kernels  9.48 us (9%)
  local copies, waits for them, and re-layouts  2.35 us (2%)
    ppermute x18, starting transfers between devices, move(): return lax.ppermute(array, 'tm', moves(rule))  55 us
    ppermute x18, waiting for transfers between devices, move(): return lax.ppermute(array, 'tm', moves(rule))  36.3 us
    pallas_call x2, Pallas kernels, correlate(): pl.pallas_call(functools.partial(products, len(pieces), scale), grid=(4,)...  6.68 us
    ppermute x1, starting transfers between devices, halo_of(): return lax.ppermute(tail, 'tm', pairs)  5.39 us
  transfers between devices with their start and end apart: 19, of which 9 were waited for; matrix products, arithmetic and copies ran while one was open for 0% of the time, Pallas kernels for 5%

profile of v4, /device:TPU:1, one launch (start us, length us, event | category | flops | bytes accessed | tf_op | source)
XLA Modules:
  0.0 109.2 jit_solution(7481722721667692257)
XLA Ops:
  0.0 0.0 copy-start
  0.0 1.9 %copy-done = bf16[768,2,1,1024]{3,1,2,0:T(2,128)(2,1)S(1)} copy-done((bf16[768,2,1,1024]{3,1,2,0:T(2,128)(2,1)S(1)}, bf16[768,2,1,1024]{3,1,2,0:T(2,128)(2,1)}, u32[]{:S(2)}) %copy-start) | copy-done | bytes 3145752
  1.9 0.0 copy-start.1
  1.9 0.3 shard_map.37
  2.2 5.4 %collective-permute-start = (bf16[240,2,1024]{2,1,0:T(2,128)(2,1)S(1)}, bf16[240,2,1024]{2,1,0:T(2,128)(2,1)S(1)}, u32[]{:S(2)}, u32[]{:S(2)}) collective-permute-start(bf16[240,2,1024]{2,1,0:T(2,128)(2,1)S(1)} %shard_map.37), channel_id=1, source_target_pairs={{0,1},{1,2},{2,3},{3,4},{4,5},{5,6},{6,7},{7,8},{8,9},{9,10},{10,1... | collective-permute-start | bytes 2949128 | tf_op jit(solution)/shard_map/ppermute | solution.py:59
  7.6 0.0 copy-done.1
  7.6 0.0 copy-done.2
  7.6 1.7 %shard_map.38 = (bf16[64,1024]{1,0:T(8,128)(2,1)S(1)}, bf16[64,1024]{1,0:T(8,128)(2,1)S(1)}, bf16[64,1024]{1,0:T(8,128)(2,1)S(1)}, bf16[64,1024]{1,0:T(8,128)(2,...) custom-call(f32[1,256]{1,0:T(1,128)S(1)} %bitcast.43, f32[16,1024]{1,0:T(8,128)S(1)} %copy-done.2, ...), custom_call_target="tpu_custom_call" | custom-call | flops 1073741824 | bytes 6291456 | tf_op jit(solution)/shard_map/pallas_call | solution.py:200
  9.4 3.1 %collective-permute-start.1 = (bf16[64,1024]{1,0:T(8,128)(2,1)S(1)}, bf16[64,1024]{1,0:T(8,128)(2,1)S(1)}, u32[]{:S(2)}, u32[]{:S(2)}) collective-permute-start(bf16[64,1024]{1,0:T(8,128)(2,1)S(1)} %get-tuple-element.31), channel_id=1, source_target_pairs={{0,8},{1,9},{2,10},{3,11},{4,12},{5,13},{6,14},{7,15},{8,16},{9,17... | collective-permute-start | bytes 393224 | tf_op jit(solution)/shard_map/ppermute | solution.py:38
  12.5 4.4 %collective-permute-start.2 = (bf16[64,1024]{1,0:T(8,128)(2,1)S(1)}, bf16[64,1024]{1,0:T(8,128)(2,1)S(1)}, u32[]{:S(2)}, u32[]{:S(2)}) collective-permute-start(bf16[64,1024]{1,0:T(8,128)(2,1)S(1)} %get-tuple-element.32), channel_id=1, source_target_pairs={{0,16},{1,17},{2,18},{3,19},{4,20},{5,21},{6,22},{7,23},{8,24},{9,... | collective-permute-start | bytes 393224 | tf_op jit(solution)/shard_map/ppermute | solution.py:38
  16.9 3.1 %collective-permute-start.3 = (bf16[64,1024]{1,0:T(8,128)(2,1)S(1)}, bf16[64,1024]{1,0:T(8,128)(2,1)S(1)}, u32[]{:S(2)}, u32[]{:S(2)}) collective-permute-start(bf16[64,1024]{1,0:T(8,128)(2,1)S(1)} %get-tuple-element.33), channel_id=1, source_target_pairs={{0,24},{1,25},{2,26},{3,27},{4,28},{5,29},{6,30},{7,31},{8,0},{9,1... | collective-permute-start | bytes 393224 | tf_op jit(solution)/shard_map/ppermute | solution.py:38
  19.9 5.8 %collective-permute-start.4 = (bf16[4,64,1024]{2,1,0:T(8,128)(2,1)S(1)}, bf16[4,64,1024]{2,1,0:T(8,128)(2,1)S(1)}, u32[]{:S(2)}, u32[]{:S(2)}) collective-permute-start(bf16[4,64,1024]{2,1,0:T(8,128)(2,1)S(1)} %get-tuple-element.38), channel_id=1, source_target_pairs={{0,4},{1,5},{2,6},{3,7},{4,0},{5,1},{6,2},{7,3},{8,12},{9,13},{10,... | collective-permute-start | bytes 1572872 | tf_op jit(solution)/shard_map/ppermute | solution.py:38
  25.8 0.0 collective-permute-done.1
  25.8 4.6 %collective-permute-done.2 = bf16[64,1024]{1,0:T(8,128)(2,1)S(1)} collective-permute-done((bf16[64,1024]{1,0:T(8,128)(2,1)S(1)}, bf16[64,1024]{1,0:T(8,128)(2,1)S(1)}, u32[]{:S(2)}, u32[]{:S(2)}) %collective-permute-start.2) | collective-permute-done | bytes 131104 | tf_op jit(solution)/shard_map/ppermute | solution.py:38
  30.4 0.0 collective-permute-done.3
  30.4 0.0 collective-permute-done.halo_ref
  30.4 1.9 %collective-permute-start.5 = (bf16[32,1024]{1,0:T(8,128)(2,1)S(1)}, bf16[32,1024]{1,0:T(8,128)(2,1)S(1)}, u32[]{:S(2)}, u32[]{:S(2)}) collective-permute-start(bf16[32,1024]{1,0:T(8,128)(2,1)S(1)} %slice.75), channel_id=1, source_target_pairs={{0,2},{1,3},{2,0},{3,1},{4,6},{5,7},{6,4},{7,5},{8,10},{9,11},{10,... | collective-permute-start | bytes 196616 | tf_op jit(solution)/shard_map/ppermute | solution.py:38
  32.4 0.8 shard_map.39
  33.1 1.9 %collective-permute-start.6 = (bf16[4,32,1024]{2,1,0:T(8,128)(2,1)S(1)}, bf16[4,32,1024]{2,1,0:T(8,128)(2,1)S(1)}, u32[]{:S(2)}, u32[]{:S(2)}) collective-permute-start(bf16[4,32,1024]{2,1,0:T(8,128)(2,1)S(1)} %get-tuple-element.42), channel_id=1, source_target_pairs={{0,4},{1,5},{2,6},{3,7},{4,0},{5,1},{6,2},{7,3},{8,12},{9,13},{10,... | collective-permute-start | bytes 786440 | tf_op jit(solution)/shard_map/ppermute | solution.py:38
  35.1 3.4 %collective-permute-start.7 = (bf16[4,32,1024]{2,1,0:T(8,128)(2,1)S(1)}, bf16[4,32,1024]{2,1,0:T(8,128)(2,1)S(1)}, u32[]{:S(2)}, u32[]{:S(2)}) collective-permute-start(bf16[4,32,1024]{2,1,0:T(8,128)(2,1)S(1)} %get-tuple-element.43), channel_id=1, source_target_pairs={{0,2},{1,3},{2,0},{3,1},{4,6},{5,7},{6,4},{7,5},{8,10},{9,11},{10,... | collective-permute-start | bytes 786440 | tf_op jit(solution)/shard_map/ppermute | solution.py:38
  38.5 1.9 %collective-permute-start.8 = (bf16[224,1024]{1,0:T(8,128)(2,1)S(1)}, bf16[224,1024]{1,0:T(8,128)(2,1)S(1)}, u32[]{:S(2)}, u32[]{:S(2)}) collective-permute-start(bf16[224,1024]{1,0:T(8,128)(2,1)S(1)} %pad_maximum_fusion.1), channel_id=1, source_target_pairs={{0,2},{1,3},{2,0},{3,1},{4,6},{5,7},{6,4},{7,5},{8,10},{9,11},{10,... | collective-permute-start | bytes 1376264 | tf_op jit(solution)/shard_map/ppermute | solution.py:38
  40.5 14.4 %collective-permute-done.4 = bf16[4,64,1024]{2,1,0:T(8,128)(2,1)S(1)} collective-permute-done((bf16[4,64,1024]{2,1,0:T(8,128)(2,1)S(1)}, bf16[4,64,1024]{2,1,0:T(8,128)(2,1)S(1)}, u32[]{:S(2)}, u32[]{:S(2)}) %collective-permute-start.4) | collective-permute-done | bytes 524320 | tf_op jit(solution)/shard_map/ppermute | solution.py:38
  54.9 0.0 collective-permute-done.5
  55.0 2.1 %collective-permute-start.9 = (bf16[96,1024]{1,0:T(8,128)(2,1)S(1)}, bf16[96,1024]{1,0:T(8,128)(2,1)S(1)}, u32[]{:S(2)}, u32[]{:S(2)}) collective-permute-start(bf16[96,1024]{1,0:T(8,128)(2,1)S(1)} %pad_maximum_fusion.6), channel_id=1, source_target_pairs={{0,8},{1,9},{2,10},{3,11},{4,12},{5,13},{6,14},{7,15},{8,16},{9,17... | collective-permute-start | bytes 589832 | tf_op jit(solution)/shard_map/ppermute | solution.py:38
  57.2 2.8 %collective-permute-start.10 = (bf16[96,1024]{1,0:T(8,128)(2,1)S(1)}, bf16[96,1024]{1,0:T(8,128)(2,1)S(1)}, u32[]{:S(2)}, u32[]{:S(2)}) collective-permute-start(bf16[96,1024]{1,0:T(8,128)(2,1)S(1)} %pad_maximum_fusion.7), channel_id=1, source_target_pairs={{0,16},{1,17},{2,18},{3,19},{4,20},{5,21},{6,22},{7,23},{8,24},{9,... | collective-permute-start | bytes 589832 | tf_op jit(solution)/shard_map/ppermute | solution.py:38
  59.9 0.6 collective-permute-done.6
  60.6 2.9 %collective-permute-start.11 = (bf16[96,1024]{1,0:T(8,128)(2,1)S(1)}, bf16[96,1024]{1,0:T(8,128)(2,1)S(1)}, u32[]{:S(2)}, u32[]{:S(2)}) collective-permute-start(bf16[96,1024]{1,0:T(8,128)(2,1)S(1)} %pad_maximum_fusion.8), channel_id=1, source_target_pairs={{0,24},{1,25},{2,26},{3,27},{4,28},{5,29},{6,30},{7,31},{8,0},{9,1... | collective-permute-start | bytes 589832 | tf_op jit(solution)/shard_map/ppermute | solution.py:38
  63.5 0.0 collective-permute-done.7
  63.5 4.4 %collective-permute-done.9 = bf16[96,1024]{1,0:T(8,128)(2,1)S(1)} collective-permute-done((bf16[96,1024]{1,0:T(8,128)(2,1)S(1)}, bf16[96,1024]{1,0:T(8,128)(2,1)S(1)}, u32[]{:S(2)}, u32[]{:S(2)}) %collective-permute-start.9) | collective-permute-done | bytes 196640 | tf_op jit(solution)/shard_map/ppermute | solution.py:38
  67.9 0.0 collective-permute-done.10
  67.9 2.4 %collective-permute-done.11 = bf16[96,1024]{1,0:T(8,128)(2,1)S(1)} collective-permute-done((bf16[96,1024]{1,0:T(8,128)(2,1)S(1)}, bf16[96,1024]{1,0:T(8,128)(2,1)S(1)}, u32[]{:S(2)}, u32[]{:S(2)}) %collective-permute-start.11) | collective-permute-done | bytes 196640 | tf_op jit(solution)/shard_map/ppermute | solution.py:38
  70.3 0.0 collective-permute-done.8
  70.4 3.8 %collective-permute-start.12 = (bf16[896,1024]{1,0:T(8,128)(2,1)S(1)}, bf16[896,1024]{1,0:T(8,128)(2,1)S(1)}, u32[]{:S(2)}, u32[]{:S(2)}) collective-permute-start(bf16[896,1024]{1,0:T(8,128)(2,1)S(1)} %constant_dynamic-update-slice_fusion.refs_0_), channel_id=1, source_target_pairs={{0,1},{1,0},{2,3},{3,2},{4,5},{5,4},{6,7},{7,6},{8,9},{9,8},{10,11... | collective-permute-start | bytes 5505032 | tf_op jit(solution)/shard_map/ppermute | solution.py:38
  74.3 1.9 %collective-permute-start.13 = (bf16[256,1024]{1,0:T(8,128)(2,1)S(1)}, bf16[256,1024]{1,0:T(8,128)(2,1)S(1)}, u32[]{:S(2)}, u32[]{:S(2)}) collective-permute-start(bf16[256,1024]{1,0:T(8,128)(2,1)S(1)} %pad_maximum_fusion), channel_id=1, source_target_pairs={{0,2},{1,3},{2,0},{3,1},{4,6},{5,7},{6,4},{7,5},{8,10},{9,11},{10,... | collective-permute-start | bytes 1572872 | tf_op jit(solution)/shard_map/ppermute | solution.py:38
  76.3 2.5 %collective-permute-start.15 = (bf16[64,1024]{1,0:T(8,128)(2,1)S(1)}, bf16[64,1024]{1,0:T(8,128)(2,1)S(1)}, u32[]{:S(2)}, u32[]{:S(2)}) collective-permute-start(bf16[64,1024]{1,0:T(8,128)(2,1)S(1)} %pad_maximum_fusion.10), channel_id=1, source_target_pairs={{0,16},{1,17},{2,18},{3,19},{4,20},{5,21},{6,22},{7,23},{8,24},{9,... | collective-permute-start | bytes 393224 | tf_op jit(solution)/shard_map/ppermute | solution.py:38
  78.9 4.0 %collective-permute-start.16 = (bf16[64,1024]{1,0:T(8,128)(2,1)S(1)}, bf16[64,1024]{1,0:T(8,128)(2,1)S(1)}, u32[]{:S(2)}, u32[]{:S(2)}) collective-permute-start(bf16[64,1024]{1,0:T(8,128)(2,1)S(1)} %pad_maximum_fusion.11), channel_id=1, source_target_pairs={{0,24},{1,25},{2,26},{3,27},{4,28},{5,29},{6,30},{7,31},{8,0},{9,1... | collective-permute-start | bytes 393224 | tf_op jit(solution)/shard_map/ppermute | solution.py:38
  82.9 2.2 %collective-permute-start.14 = (bf16[64,1024]{1,0:T(8,128)(2,1)S(1)}, bf16[64,1024]{1,0:T(8,128)(2,1)S(1)}, u32[]{:S(2)}, u32[]{:S(2)}) collective-permute-start(bf16[64,1024]{1,0:T(8,128)(2,1)S(1)} %pad_maximum_fusion.9), channel_id=1, source_target_pairs={{0,8},{1,9},{2,10},{3,11},{4,12},{5,13},{6,14},{7,15},{8,16},{9,17... | collective-permute-start | bytes 393224 | tf_op jit(solution)/shard_map/ppermute | solution.py:38
  85.1 0.0 collective-permute-done.15
  85.1 2.5 %collective-permute-done.16 = bf16[64,1024]{1,0:T(8,128)(2,1)S(1)} collective-permute-done((bf16[64,1024]{1,0:T(8,128)(2,1)S(1)}, bf16[64,1024]{1,0:T(8,128)(2,1)S(1)}, u32[]{:S(2)}, u32[]{:S(2)}) %collective-permute-start.16) | collective-permute-done | bytes 131104 | tf_op jit(solution)/shard_map/ppermute | solution.py:38
  87.6 2.9 %collective-permute-done.14 = bf16[64,1024]{1,0:T(8,128)(2,1)S(1)} collective-permute-done((bf16[64,1024]{1,0:T(8,128)(2,1)S(1)}, bf16[64,1024]{1,0:T(8,128)(2,1)S(1)}, u32[]{:S(2)}, u32[]{:S(2)}) %collective-permute-start.14) | collective-permute-done | bytes 131104 | tf_op jit(solution)/shard_map/ppermute | solution.py:38
  90.5 3.0 %collective-permute-start.17 = (bf16[128,1024]{1,0:T(8,128)(2,1)S(1)}, bf16[128,1024]{1,0:T(8,128)(2,1)S(1)}, u32[]{:S(2)}, u32[]{:S(2)}) collective-permute-start(bf16[128,1024]{1,0:T(8,128)(2,1)S(1)} %pad_maximum_fusion.4), channel_id=1, source_target_pairs={{0,2},{1,3},{2,0},{3,1},{4,6},{5,7},{6,4},{7,5},{8,10},{9,11},{10,... | collective-permute-start | bytes 786440 | tf_op jit(solution)/shard_map/ppermute | solution.py:38
  93.6 0.0 collective-permute-done.13.refs_2_
  93.6 0.0 collective-permute-done.12.refs_1_
  93.6 3.4 %shard_map.40.refs_2_ = f32[2,1024,256]{2,1,0:T(8,128)S(1)} custom-call(bf16[896,1024]{1,0:T(8,128)(2,1)S(1)} %constant_dynamic-update-slice_fusion.refs_0_, bf16[896,1024]{1,0:T(8,128)(2,1)S(1)} %collective-permute-done.12.refs_1_, bf16[256,1024]{1,0:T(8,128)(2,1)S(1)} %collective-permute-done.13.refs_2_), custom_call_target="tpu_custom_call" | custom-call | flops 17179869184 | bytes 4194304 | tf_op jit(solution)/shard_map/pallas_call | solution.py:171
  97.0 1.8 %collective-permute-done.17 = bf16[128,1024]{1,0:T(8,128)(2,1)S(1)} collective-permute-done((bf16[128,1024]{1,0:T(8,128)(2,1)S(1)}, bf16[128,1024]{1,0:T(8,128)(2,1)S(1)}, u32[]{:S(2)}, u32[]{:S(2)}) %collective-permute-start.17) | collective-permute-done | bytes 262176 | tf_op jit(solution)/shard_map/ppermute | solution.py:38
  99.0 4.3 %collective-permute-start.18 = (bf16[640,1024]{1,0:T(8,128)(2,1)S(1)}, bf16[640,1024]{1,0:T(8,128)(2,1)S(1)}, u32[]{:S(2)}, u32[]{:S(2)}) collective-permute-start(bf16[640,1024]{1,0:T(8,128)(2,1)S(1)} %constant_dynamic-update-slice_fusion.15), channel_id=1, source_target_pairs={{0,1},{1,0},{2,3},{3,2},{4,5},{5,4},{6,7},{7,6},{8,9},{9,8},{10,11... | collective-permute-start | bytes 3932168 | tf_op jit(solution)/shard_map/ppermute | solution.py:38
  103.3 2.6 %collective-permute-done.18.refs_1_ = bf16[640,1024]{1,0:T(8,128)(2,1)S(1)} collective-permute-done((bf16[640,1024]{1,0:T(8,128)(2,1)S(1)}, bf16[640,1024]{1,0:T(8,128)(2,1)S(1)}, u32[]{:S(2)}, u32[]{:S(2)}) %collective-permute-start.18) | collective-permute-done | bytes 1310752 | tf_op jit(solution)/shard_map/ppermute | solution.py:38
  105.9 3.3 %shard_map.41 = f32[2,1024,256]{2,1,0:T(8,128)} custom-call(bf16[384,1024]{1,0:T(8,128)(2,1)S(1)} %get-tuple-element.77.refs_0_, bf16[640,1024]{1,0:T(8,128)(2,1)S(1)} %collective-permute-done.18.refs_1_, f32[2,1024,256]{2,1,0:T(8,128)S(1)} %shard_map.40.refs_2_), custom_call_target="tpu_custom_call" | custom-call | flops 8589934592 | bytes 4194304 | tf_op jit(solution)/shard_map/pallas_call | solution.py:171
  (39 shorter events, 0.6 us)
Async XLA Ops:
  0.0 1.9 %copy-start = (bf16[768,2,1,1024]{3,1,2,0:T(2,128)(2,1)S(1)}, bf16[768,2,1,1024]{3,1,2,0:T(2,128)(2,1)}, u32[]{:S(2)}) copy-start(bf16[768,2,1,1024]{3,1,2,0:T(2,128)(2,1)} %param.3) | copy-start | bytes 9437188
  1.9 5.7 %copy-start.1 = (f32[256]{0:T(256)S(1)}, f32[256]{0:T(256)}, u32[]{:S(2)}) copy-start(f32[256]{0:T(256)} %param.4) | copy-start | bytes 3076
  1.9 5.7 %copy-start.2 = (f32[16,1024]{1,0:T(8,128)S(1)}, f32[16,1024]{1,0:T(8,128)}, u32[]{:S(2)}) copy-start(f32[16,1024]{1,0:T(8,128)} %constant.2.clone.trig_ref) | copy-start | bytes 196612
  2.2 28.2 %collective-permute-start = (bf16[240,2,1024]{2,1,0:T(2,128)(2,1)S(1)}, bf16[240,2,1024]{2,1,0:T(2,128)(2,1)S(1)}, u32[]{:S(2)}, u32[]{:S(2)}) collective-permute-start(bf16[240,2,1024]{2,1,0:T(2,128)(2,1)S(1)} %shard_map.37), channel_id=1, source_target_pairs={{0,1},{1,2},{2,3},{3,4},{4,5},{5,6},{6,7},{7,8},{8,9},{9,10},{10,1... | collective-permute-start | bytes 2949128 | tf_op jit(solution)/shard_map/ppermute | solution.py:59
  9.4 16.4 %collective-permute-start.1 = (bf16[64,1024]{1,0:T(8,128)(2,1)S(1)}, bf16[64,1024]{1,0:T(8,128)(2,1)S(1)}, u32[]{:S(2)}, u32[]{:S(2)}) collective-permute-start(bf16[64,1024]{1,0:T(8,128)(2,1)S(1)} %get-tuple-element.31), channel_id=1, source_target_pairs={{0,8},{1,9},{2,10},{3,11},{4,12},{5,13},{6,14},{7,15},{8,16},{9,17... | collective-permute-start | bytes 393224 | tf_op jit(solution)/shard_map/ppermute | solution.py:38
  12.5 17.9 %collective-permute-start.2 = (bf16[64,1024]{1,0:T(8,128)(2,1)S(1)}, bf16[64,1024]{1,0:T(8,128)(2,1)S(1)}, u32[]{:S(2)}, u32[]{:S(2)}) collective-permute-start(bf16[64,1024]{1,0:T(8,128)(2,1)S(1)} %get-tuple-element.32), channel_id=1, source_target_pairs={{0,16},{1,17},{2,18},{3,19},{4,20},{5,21},{6,22},{7,23},{8,24},{9,... | collective-permute-start | bytes 393224 | tf_op jit(solution)/shard_map/ppermute | solution.py:38
  16.9 13.6 %collective-permute-start.3 = (bf16[64,1024]{1,0:T(8,128)(2,1)S(1)}, bf16[64,1024]{1,0:T(8,128)(2,1)S(1)}, u32[]{:S(2)}, u32[]{:S(2)}) collective-permute-start(bf16[64,1024]{1,0:T(8,128)(2,1)S(1)} %get-tuple-element.33), channel_id=1, source_target_pairs={{0,24},{1,25},{2,26},{3,27},{4,28},{5,29},{6,30},{7,31},{8,0},{9,1... | collective-permute-start | bytes 393224 | tf_op jit(solution)/shard_map/ppermute | solution.py:38
  19.9 35.0 %collective-permute-start.4 = (bf16[4,64,1024]{2,1,0:T(8,128)(2,1)S(1)}, bf16[4,64,1024]{2,1,0:T(8,128)(2,1)S(1)}, u32[]{:S(2)}, u32[]{:S(2)}) collective-permute-start(bf16[4,64,1024]{2,1,0:T(8,128)(2,1)S(1)} %get-tuple-element.38), channel_id=1, source_target_pairs={{0,4},{1,5},{2,6},{3,7},{4,0},{5,1},{6,2},{7,3},{8,12},{9,13},{10,... | collective-permute-start | bytes 1572872 | tf_op jit(solution)/shard_map/ppermute | solution.py:38
  30.4 24.5 %collective-permute-start.5 = (bf16[32,1024]{1,0:T(8,128)(2,1)S(1)}, bf16[32,1024]{1,0:T(8,128)(2,1)S(1)}, u32[]{:S(2)}, u32[]{:S(2)}) collective-permute-start(bf16[32,1024]{1,0:T(8,128)(2,1)S(1)} %slice.75), channel_id=1, source_target_pairs={{0,2},{1,3},{2,0},{3,1},{4,6},{5,7},{6,4},{7,5},{8,10},{9,11},{10,... | collective-permute-start | bytes 196616 | tf_op jit(solution)/shard_map/ppermute | solution.py:38
  33.1 27.4 %collective-permute-start.6 = (bf16[4,32,1024]{2,1,0:T(8,128)(2,1)S(1)}, bf16[4,32,1024]{2,1,0:T(8,128)(2,1)S(1)}, u32[]{:S(2)}, u32[]{:S(2)}) collective-permute-start(bf16[4,32,1024]{2,1,0:T(8,128)(2,1)S(1)} %get-tuple-element.42), channel_id=1, source_target_pairs={{0,4},{1,5},{2,6},{3,7},{4,0},{5,1},{6,2},{7,3},{8,12},{9,13},{10,... | collective-permute-start | bytes 786440 | tf_op jit(solution)/shard_map/ppermute | solution.py:38
  35.1 28.5 %collective-permute-start.7 = (bf16[4,32,1024]{2,1,0:T(8,128)(2,1)S(1)}, bf16[4,32,1024]{2,1,0:T(8,128)(2,1)S(1)}, u32[]{:S(2)}, u32[]{:S(2)}) collective-permute-start(bf16[4,32,1024]{2,1,0:T(8,128)(2,1)S(1)} %get-tuple-element.43), channel_id=1, source_target_pairs={{0,2},{1,3},{2,0},{3,1},{4,6},{5,7},{6,4},{7,5},{8,10},{9,11},{10,... | collective-permute-start | bytes 786440 | tf_op jit(solution)/shard_map/ppermute | solution.py:38
  38.5 31.8 %collective-permute-start.8 = (bf16[224,1024]{1,0:T(8,128)(2,1)S(1)}, bf16[224,1024]{1,0:T(8,128)(2,1)S(1)}, u32[]{:S(2)}, u32[]{:S(2)}) collective-permute-start(bf16[224,1024]{1,0:T(8,128)(2,1)S(1)} %pad_maximum_fusion.1), channel_id=1, source_target_pairs={{0,2},{1,3},{2,0},{3,1},{4,6},{5,7},{6,4},{7,5},{8,10},{9,11},{10,... | collective-permute-start | bytes 1376264 | tf_op jit(solution)/shard_map/ppermute | solution.py:38
  55.0 12.9 %collective-permute-start.9 = (bf16[96,1024]{1,0:T(8,128)(2,1)S(1)}, bf16[96,1024]{1,0:T(8,128)(2,1)S(1)}, u32[]{:S(2)}, u32[]{:S(2)}) collective-permute-start(bf16[96,1024]{1,0:T(8,128)(2,1)S(1)} %pad_maximum_fusion.6), channel_id=1, source_target_pairs={{0,8},{1,9},{2,10},{3,11},{4,12},{5,13},{6,14},{7,15},{8,16},{9,17... | collective-permute-start | bytes 589832 | tf_op jit(solution)/shard_map/ppermute | solution.py:38
  57.2 10.8 %collective-permute-start.10 = (bf16[96,1024]{1,0:T(8,128)(2,1)S(1)}, bf16[96,1024]{1,0:T(8,128)(2,1)S(1)}, u32[]{:S(2)}, u32[]{:S(2)}) collective-permute-start(bf16[96,1024]{1,0:T(8,128)(2,1)S(1)} %pad_maximum_fusion.7), channel_id=1, source_target_pairs={{0,16},{1,17},{2,18},{3,19},{4,20},{5,21},{6,22},{7,23},{8,24},{9,... | collective-permute-start | bytes 589832 | tf_op jit(solution)/shard_map/ppermute | solution.py:38
  60.6 9.7 %collective-permute-start.11 = (bf16[96,1024]{1,0:T(8,128)(2,1)S(1)}, bf16[96,1024]{1,0:T(8,128)(2,1)S(1)}, u32[]{:S(2)}, u32[]{:S(2)}) collective-permute-start(bf16[96,1024]{1,0:T(8,128)(2,1)S(1)} %pad_maximum_fusion.8), channel_id=1, source_target_pairs={{0,24},{1,25},{2,26},{3,27},{4,28},{5,29},{6,30},{7,31},{8,0},{9,1... | collective-permute-start | bytes 589832 | tf_op jit(solution)/shard_map/ppermute | solution.py:38
  70.4 23.2 %collective-permute-start.12 = (bf16[896,1024]{1,0:T(8,128)(2,1)S(1)}, bf16[896,1024]{1,0:T(8,128)(2,1)S(1)}, u32[]{:S(2)}, u32[]{:S(2)}) collective-permute-start(bf16[896,1024]{1,0:T(8,128)(2,1)S(1)} %constant_dynamic-update-slice_fusion.refs_0_), channel_id=1, source_target_pairs={{0,1},{1,0},{2,3},{3,2},{4,5},{5,4},{6,7},{7,6},{8,9},{9,8},{10,11... | collective-permute-start | bytes 5505032 | tf_op jit(solution)/shard_map/ppermute | solution.py:38
  74.3 19.3 %collective-permute-start.13 = (bf16[256,1024]{1,0:T(8,128)(2,1)S(1)}, bf16[256,1024]{1,0:T(8,128)(2,1)S(1)}, u32[]{:S(2)}, u32[]{:S(2)}) collective-permute-start(bf16[256,1024]{1,0:T(8,128)(2,1)S(1)} %pad_maximum_fusion), channel_id=1, source_target_pairs={{0,2},{1,3},{2,0},{3,1},{4,6},{5,7},{6,4},{7,5},{8,10},{9,11},{10,... | collective-permute-start | bytes 1572872 | tf_op jit(solution)/shard_map/ppermute | solution.py:38
  76.3 8.8 %collective-permute-start.15 = (bf16[64,1024]{1,0:T(8,128)(2,1)S(1)}, bf16[64,1024]{1,0:T(8,128)(2,1)S(1)}, u32[]{:S(2)}, u32[]{:S(2)}) collective-permute-start(bf16[64,1024]{1,0:T(8,128)(2,1)S(1)} %pad_maximum_fusion.10), channel_id=1, source_target_pairs={{0,16},{1,17},{2,18},{3,19},{4,20},{5,21},{6,22},{7,23},{8,24},{9,... | collective-permute-start | bytes 393224 | tf_op jit(solution)/shard_map/ppermute | solution.py:38
  78.9 8.8 %collective-permute-start.16 = (bf16[64,1024]{1,0:T(8,128)(2,1)S(1)}, bf16[64,1024]{1,0:T(8,128)(2,1)S(1)}, u32[]{:S(2)}, u32[]{:S(2)}) collective-permute-start(bf16[64,1024]{1,0:T(8,128)(2,1)S(1)} %pad_maximum_fusion.11), channel_id=1, source_target_pairs={{0,24},{1,25},{2,26},{3,27},{4,28},{5,29},{6,30},{7,31},{8,0},{9,1... | collective-permute-start | bytes 393224 | tf_op jit(solution)/shard_map/ppermute | solution.py:38
  82.9 7.6 %collective-permute-start.14 = (bf16[64,1024]{1,0:T(8,128)(2,1)S(1)}, bf16[64,1024]{1,0:T(8,128)(2,1)S(1)}, u32[]{:S(2)}, u32[]{:S(2)}) collective-permute-start(bf16[64,1024]{1,0:T(8,128)(2,1)S(1)} %pad_maximum_fusion.9), channel_id=1, source_target_pairs={{0,8},{1,9},{2,10},{3,11},{4,12},{5,13},{6,14},{7,15},{8,16},{9,17... | collective-permute-start | bytes 393224 | tf_op jit(solution)/shard_map/ppermute | solution.py:38
  90.5 8.3 %collective-permute-start.17 = (bf16[128,1024]{1,0:T(8,128)(2,1)S(1)}, bf16[128,1024]{1,0:T(8,128)(2,1)S(1)}, u32[]{:S(2)}, u32[]{:S(2)}) collective-permute-start(bf16[128,1024]{1,0:T(8,128)(2,1)S(1)} %pad_maximum_fusion.4), channel_id=1, source_target_pairs={{0,2},{1,3},{2,0},{3,1},{4,6},{5,7},{6,4},{7,5},{8,10},{9,11},{10,... | collective-permute-start | bytes 786440 | tf_op jit(solution)/shard_map/ppermute | solution.py:38
  99.0 6.9 %collective-permute-start.18 = (bf16[640,1024]{1,0:T(8,128)(2,1)S(1)}, bf16[640,1024]{1,0:T(8,128)(2,1)S(1)}, u32[]{:S(2)}, u32[]{:S(2)}) collective-permute-start(bf16[640,1024]{1,0:T(8,128)(2,1)S(1)} %constant_dynamic-update-slice_fusion.15), channel_id=1, source_target_pairs={{0,1},{1,0},{2,3},{3,2},{4,5},{5,4},{6,7},{7,6},{8,9},{9,8},{10,11... | collective-permute-start | bytes 3932168 | tf_op jit(solution)/shard_map/ppermute | solution.py:38

commit v5 on v2

--- a/solution.py
+++ b/solution.py
@@ -102,6 +102,13 @@
                 at = ((d * 2 + other) * 2 + ro) * BLOCK
                 wave = trig_ref[pl.ds(k * 2 + ro, 1), :]
                 band_ref[at : at + BLOCK, :] = (shifted * wave).astype(BF16)
+
+
+def tail_copy(volt_ref, out_ref, sem):
+    n = out_ref.shape[0]
+    copy = pltpu.make_async_copy(volt_ref.at[pl.ds(volt_ref.shape[0] - n, n)], out_ref, sem)
+    copy.start()
+    copy.wait()
 
 
 def filter_late(taps_ref, trig_ref, volt_ref, band_ref, *out_refs):
@@ -184,8 +191,16 @@
 def shards(voltage, taps):
     samples_here = voltage.shape[0]
     volt = voltage.reshape(samples_here, 2, S)
-    halo = halo_of(volt[samples_here - (TAPS - 1) * FINE :])
     params = pltpu.CompilerParams(vmem_limit_bytes=40 << 20)
+    tail = pl.pallas_call(
+        tail_copy,
+        out_shape=shape((TAPS - 1) * FINE, 2, S),
+        in_specs=[pl.BlockSpec(memory_space=VMEM)],
+        out_specs=pl.BlockSpec(memory_space=VMEM),
+        scratch_shapes=[pltpu.SemaphoreType.DMA],
+        compiler_params=params,
+    )(volt)
+    halo = halo_of(tail)
     band, *late_out = pl.pallas_call(
         filter_late,
         out_shape=(shape(4 * FOUT * BLOCK // 2, 2 * WINDOW), *[shape(4 * ROWS, S)] * XS),
@@ -208,17 +223,18 @@
     ma = part(late_all, 0)
     ma_near = move(ma, near_z)
     first_all = spread(first_out)
-    ta, ma_near, *first_all = lax.optimization_barrier((ta, ma_near, *first_all))
     tb = move(part(first_all, 1), far_z)
-    second = jnp.concatenate([ta, part(first_all, 0)], 0)
-    second_near = move(second, near_z)
-    tb_near = move(tb, near_z)
+    ta_near = move(ta, near_z)
+    b_own = jnp.concatenate([part(first_all, 0), tb], 0)
+    b_near = move(b_own, near_z)
     ma = jnp.concatenate([ma, ma_near], 0)
     acc = correlate([ma, move(ma, other_core)], None)
-    own = jnp.concatenate([second, tb], 0)
+    acc, ta_near, b_near = lax.optimization_barrier((acc, ta_near, b_near))
+    near = jnp.concatenate([ta_near, b_near], 0)
+    near_core = move(near, other_core)
+    own = jnp.concatenate([ta, b_own], 0)
     acc = correlate([own, move(own, other_core)], acc)
-    near = jnp.concatenate(lax.optimization_barrier((second_near, tb_near)), 0)
-    pieces = [near, move(near, other_core)]
+    pieces = [near, near_core]
     frames = samples_here // FINE * XS * ZS * CORES
     return correlate(pieces, acc, 1.0 / frames)[None]
 

time: 110 us -> 109 us (level)
  waiting for transfers between devices: 45.5 us -> 49.9 us
  local copies, waits for them, and re-layouts: 5.7 us -> 2.29 us
  starting transfers between devices: 48.2 us -> 45.2 us
    ppermute x14, waiting for transfers between devices: 45.5 us -> 49.9 us  [move(): return lax.ppermute(array, 'tm', moves(rule))]
    ppermute x14, starting transfers between devices: 42.9 us -> 39.7 us  [move(): return lax.ppermute(array, 'tm', moves(rule))]
    slice x1 -> x4, local copies, waits for them, and re-layouts: 1.88 us -> 0.12 us  [part(): slab[other * half:(other + 1) * half]]
    unnamed x18 -> x14, local copies, waits for them, and re-layouts: 3.75 us -> 2.05 us
  transfers between devices with their start and end apart: 15 -> 15, of which waited for: 7 -> 6; matrix products, arithmetic and copies ran while one was open for 0% -> 0% of each run, Pallas kernels for 6% -> 6%
where the time goes in v5:
time: 109 us; the launch traced here: 108 us
  waiting for transfers between devices  49.9 us (46%)
  starting transfers between devices  45.2 us (41%)
  Pallas kernels  10.3 us (9%)
  local copies, waits for them, and re-layouts  2.29 us (2%)
    ppermute x14, waiting for transfers between devices, move(): return lax.ppermute(array, 'tm', moves(rule))  49.9 us
    ppermute x14, starting transfers between devices, move(): return lax.ppermute(array, 'tm', moves(rule))  39.7 us
    pallas_call x3, Pallas kernels, correlate(): pl.pallas_call(functools.partial(products, len(pieces), scale), grid=(4,)...  7.46 us
    ppermute x1, starting transfers between devices, halo_of(): return lax.ppermute(tail, 'tm', pairs)  5.52 us
  transfers between devices with their start and end apart: 15, of which 6 were waited for; matrix products, arithmetic and copies ran while one was open for 0% of the time, Pallas kernels for 6%

profile of v5, /device:TPU:1, one launch (start us, length us, event | category | flops | bytes accessed | tf_op | source)
XLA Modules:
  0.0 108.1 jit_solution(8354002166890051788)
XLA Ops:
  0.0 0.0 copy-start.2
  0.0 0.0 copy-start
  0.0 1.9 %copy-done = bf16[768,2,1,1024]{3,1,2,0:T(2,128)(2,1)S(1)} copy-done((bf16[768,2,1,1024]{3,1,2,0:T(2,128)(2,1)S(1)}, bf16[768,2,1,1024]{3,1,2,0:T(2,128)(2,1)}, u32[]{:S(2)}) %copy-start) | copy-done | bytes 3145752
  1.9 0.0 copy-start.1
  1.9 0.0 copy-start.3
  1.9 0.3 shard_map.37
  2.2 5.5 %collective-permute-start = (bf16[240,2,1024]{2,1,0:T(2,128)(2,1)S(1)}, bf16[240,2,1024]{2,1,0:T(2,128)(2,1)S(1)}, u32[]{:S(2)}, u32[]{:S(2)}) collective-permute-start(bf16[240,2,1024]{2,1,0:T(2,128)(2,1)S(1)} %shard_map.37), channel_id=1, source_target_pairs={{0,1},{1,2},{2,3},{3,4},{4,5},{5,6},{6,7},{7,8},{8,9},{9,10},{10,1... | collective-permute-start | bytes 2949128 | tf_op jit(solution)/shard_map/ppermute | solution.py:59
  7.8 0.0 copy-done.2
  7.8 0.0 copy-done.1
  7.8 0.0 copy-done.3
  7.8 1.7 %shard_map.38 = (bf16[256,1024]{1,0:T(8,128)(2,1)S(1)}, bf16[128,1024]{1,0:T(8,128)(2,1)S(1)}, bf16[128,1024]{1,0:T(8,128)(2,1)S(1)}, bf16[128,1024]{1,0:T(8,128)(2,1)S(1)}, bf16[128,1024]{1,0:T(8,128)(2,1)S(1)}) custom-call(f32[1,256]{1,0:T(1,128)S(1)} %bitcast.6, f32[16,1024]{1,0:T(8,128)S(1)} %copy-done.3, bf16[768,2,1024]{2,1,0:T(2,128)(2,1)S(1)} %bitcast.4), custom_call_target="tpu_custom_call" | custom-call | flops 1073741824 | bytes 6291456 | tf_op jit(solution)/shard_map/pallas_call | solution.py:204
  9.5 3.1 %collective-permute-start.1 = (bf16[128,1024]{1,0:T(8,128)(2,1)S(1)}, bf16[128,1024]{1,0:T(8,128)(2,1)S(1)}, u32[]{:S(2)}, u32[]{:S(2)}) collective-permute-start(bf16[128,1024]{1,0:T(8,128)(2,1)S(1)} %get-tuple-element.23), channel_id=1, source_target_pairs={{0,8},{1,9},{2,10},{3,11},{4,12},{5,13},{6,14},{7,15},{8,16},{9,17... | collective-permute-start | bytes 786440 | tf_op jit(solution)/shard_map/ppermute | solution.py:38
  12.7 4.4 %collective-permute-start.2 = (bf16[128,1024]{1,0:T(8,128)(2,1)S(1)}, bf16[128,1024]{1,0:T(8,128)(2,1)S(1)}, u32[]{:S(2)}, u32[]{:S(2)}) collective-permute-start(bf16[128,1024]{1,0:T(8,128)(2,1)S(1)} %get-tuple-element.24), channel_id=1, source_target_pairs={{0,16},{1,17},{2,18},{3,19},{4,20},{5,21},{6,22},{7,23},{8,24},{9,... | collective-permute-start | bytes 786440 | tf_op jit(solution)/shard_map/ppermute | solution.py:38
  17.0 3.1 %collective-permute-start.3 = (bf16[128,1024]{1,0:T(8,128)(2,1)S(1)}, bf16[128,1024]{1,0:T(8,128)(2,1)S(1)}, u32[]{:S(2)}, u32[]{:S(2)}) collective-permute-start(bf16[128,1024]{1,0:T(8,128)(2,1)S(1)} %get-tuple-element.25), channel_id=1, source_target_pairs={{0,24},{1,25},{2,26},{3,27},{4,28},{5,29},{6,30},{7,31},{8,0},{9,1... | collective-permute-start | bytes 786440 | tf_op jit(solution)/shard_map/ppermute | solution.py:38
  20.1 7.0 %collective-permute-done.1 = bf16[128,1024]{1,0:T(8,128)(2,1)S(1)} collective-permute-done((bf16[128,1024]{1,0:T(8,128)(2,1)S(1)}, bf16[128,1024]{1,0:T(8,128)(2,1)S(1)}, u32[]{:S(2)}, u32[]{:S(2)}) %collective-permute-start.1) | collective-permute-done | bytes 262176 | tf_op jit(solution)/shard_map/ppermute | solution.py:38
  27.1 9.1 %collective-permute-done.2 = bf16[128,1024]{1,0:T(8,128)(2,1)S(1)} collective-permute-done((bf16[128,1024]{1,0:T(8,128)(2,1)S(1)}, bf16[128,1024]{1,0:T(8,128)(2,1)S(1)}, u32[]{:S(2)}, u32[]{:S(2)}) %collective-permute-start.2) | collective-permute-done | bytes 262176 | tf_op jit(solution)/shard_map/ppermute | solution.py:38
  36.2 0.0 collective-permute-done.3
  36.2 0.0 collective-permute-done.halo_ref
  36.4 1.9 %collective-permute-start.4 = (bf16[256,1024]{1,0:T(8,128)(2,1)S(1)}, bf16[256,1024]{1,0:T(8,128)(2,1)S(1)}, u32[]{:S(2)}, u32[]{:S(2)}) collective-permute-start(bf16[256,1024]{1,0:T(8,128)(2,1)S(1)} %pad_maximum_fusion), channel_id=1, source_target_pairs={{0,2},{1,3},{2,0},{3,1},{4,6},{5,7},{6,4},{7,5},{8,10},{9,11},{10,... | collective-permute-start | bytes 1572872 | tf_op jit(solution)/shard_map/ppermute | solution.py:38
  38.4 1.9 %collective-permute-start.6 = (bf16[256,1024]{1,0:T(8,128)(2,1)S(1)}, bf16[256,1024]{1,0:T(8,128)(2,1)S(1)}, u32[]{:S(2)}, u32[]{:S(2)}) collective-permute-start(bf16[256,1024]{1,0:T(8,128)(2,1)S(1)} %pad_maximum_fusion.1), channel_id=1, source_target_pairs={{0,4},{1,5},{2,6},{3,7},{4,0},{5,1},{6,2},{7,3},{8,12},{9,13},{10,... | collective-permute-start | bytes 1572872 | tf_op jit(solution)/shard_map/ppermute | solution.py:38
  40.3 0.8 shard_map.40
  41.0 1.9 %collective-permute-start.8 = (bf16[64,1024]{1,0:T(8,128)(2,1)S(1)}, bf16[64,1024]{1,0:T(8,128)(2,1)S(1)}, u32[]{:S(2)}, u32[]{:S(2)}) collective-permute-start(bf16[64,1024]{1,0:T(8,128)(2,1)S(1)} %get-tuple-element.33), channel_id=1, source_target_pairs={{0,8},{1,9},{2,10},{3,11},{4,12},{5,13},{6,14},{7,15},{8,16},{9,17... | collective-permute-start | bytes 393224 | tf_op jit(solution)/shard_map/ppermute | solution.py:38
  43.0 2.1 %collective-permute-start.9 = (bf16[64,1024]{1,0:T(8,128)(2,1)S(1)}, bf16[64,1024]{1,0:T(8,128)(2,1)S(1)}, u32[]{:S(2)}, u32[]{:S(2)}) collective-permute-start(bf16[64,1024]{1,0:T(8,128)(2,1)S(1)} %get-tuple-element.34), channel_id=1, source_target_pairs={{0,16},{1,17},{2,18},{3,19},{4,20},{5,21},{6,22},{7,23},{8,24},{9,... | collective-permute-start | bytes 393224 | tf_op jit(solution)/shard_map/ppermute | solution.py:38
  45.1 4.4 %collective-permute-start.10 = (bf16[64,1024]{1,0:T(8,128)(2,1)S(1)}, bf16[64,1024]{1,0:T(8,128)(2,1)S(1)}, u32[]{:S(2)}, u32[]{:S(2)}) collective-permute-start(bf16[64,1024]{1,0:T(8,128)(2,1)S(1)} %get-tuple-element.35), channel_id=1, source_target_pairs={{0,24},{1,25},{2,26},{3,27},{4,28},{5,29},{6,30},{7,31},{8,0},{9,1... | collective-permute-start | bytes 393224 | tf_op jit(solution)/shard_map/ppermute | solution.py:38
  49.5 5.3 %collective-permute-done.4 = bf16[256,1024]{1,0:T(8,128)(2,1)S(1)} collective-permute-done((bf16[256,1024]{1,0:T(8,128)(2,1)S(1)}, bf16[256,1024]{1,0:T(8,128)(2,1)S(1)}, u32[]{:S(2)}, u32[]{:S(2)}) %collective-permute-start.4) | collective-permute-done | bytes 524320 | tf_op jit(solution)/shard_map/ppermute | solution.py:38
  54.8 3.1 %collective-permute-start.5 = (bf16[512,1024]{1,0:T(8,128)(2,1)S(1)}, bf16[512,1024]{1,0:T(8,128)(2,1)S(1)}, u32[]{:S(2)}, u32[]{:S(2)}) collective-permute-start(bf16[512,1024]{1,0:T(8,128)(2,1)S(1)} %constant_dynamic-update-slice_fusion.refs_0_), channel_id=1, source_target_pairs={{0,1},{1,0},{2,3},{3,2},{4,5},{5,4},{6,7},{7,6},{8,9},{9,8},{10,11... | collective-permute-start | bytes 3145736 | tf_op jit(solution)/shard_map/ppermute | solution.py:38
  58.0 7.6 %collective-permute-done.6 = bf16[256,1024]{1,0:T(8,128)(2,1)S(1)} collective-permute-done((bf16[256,1024]{1,0:T(8,128)(2,1)S(1)}, bf16[256,1024]{1,0:T(8,128)(2,1)S(1)}, u32[]{:S(2)}, u32[]{:S(2)}) %collective-permute-start.6) | collective-permute-done | bytes 524320 | tf_op jit(solution)/shard_map/ppermute | solution.py:38
  65.6 0.0 collective-permute-done.8
  65.6 0.0 collective-permute-done.9
  65.7 0.0 collective-permute-done.10
  65.7 1.9 %collective-permute-start.11 = (bf16[128,1024]{1,0:T(8,128)(2,1)S(1)}, bf16[128,1024]{1,0:T(8,128)(2,1)S(1)}, u32[]{:S(2)}, u32[]{:S(2)}) collective-permute-start(bf16[128,1024]{1,0:T(8,128)(2,1)S(1)} %pad_maximum_fusion.2), channel_id=1, source_target_pairs={{0,4},{1,5},{2,6},{3,7},{4,0},{5,1},{6,2},{7,3},{8,12},{9,13},{10,... | collective-permute-start | bytes 786440 | tf_op jit(solution)/shard_map/ppermute | solution.py:38
  67.7 3.4 %collective-permute-start.7 = (bf16[256,1024]{1,0:T(8,128)(2,1)S(1)}, bf16[256,1024]{1,0:T(8,128)(2,1)S(1)}, u32[]{:S(2)}, u32[]{:S(2)}) collective-permute-start(bf16[256,1024]{1,0:T(8,128)(2,1)S(1)} %collective-permute-done.6), channel_id=1, source_target_pairs={{0,2},{1,3},{2,0},{3,1},{4,6},{5,7},{6,4},{7,5},{8,10},{9,11},{10,... | collective-permute-start | bytes 1572872 | tf_op jit(solution)/shard_map/ppermute | solution.py:38
  71.0 10.2 %collective-permute-done.11 = bf16[128,1024]{1,0:T(8,128)(2,1)S(1)} collective-permute-done((bf16[128,1024]{1,0:T(8,128)(2,1)S(1)}, bf16[128,1024]{1,0:T(8,128)(2,1)S(1)}, u32[]{:S(2)}, u32[]{:S(2)}) %collective-permute-start.11) | collective-permute-done | bytes 262176 | tf_op jit(solution)/shard_map/ppermute | solution.py:38
  81.2 0.1 constant_dynamic-update-slice_fusion.8
  81.3 1.9 %collective-permute-start.12 = (bf16[256,1024]{1,0:T(8,128)(2,1)S(1)}, bf16[256,1024]{1,0:T(8,128)(2,1)S(1)}, u32[]{:S(2)}, u32[]{:S(2)}) collective-permute-start(bf16[256,1024]{1,0:T(8,128)(2,1)S(1)} %get-tuple-element.40), channel_id=1, source_target_pairs={{0,2},{1,3},{2,0},{3,1},{4,6},{5,7},{6,4},{7,5},{8,10},{9,11},{10,... | collective-permute-start | bytes 1572872 | tf_op jit(solution)/shard_map/ppermute | solution.py:38
  83.2 2.5 %collective-permute-start.14 = (bf16[512,1024]{1,0:T(8,128)(2,1)S(1)}, bf16[512,1024]{1,0:T(8,128)(2,1)S(1)}, u32[]{:S(2)}, u32[]{:S(2)}) collective-permute-start(bf16[512,1024]{1,0:T(8,128)(2,1)S(1)} %get-tuple-element.39.refs_0_), channel_id=1, source_target_pairs={{0,1},{1,0},{2,3},{3,2},{4,5},{5,4},{6,7},{7,6},{8,9},{9,8},{10,11... | collective-permute-start | bytes 3145736 | tf_op jit(solution)/shard_map/ppermute | solution.py:38
  85.7 0.0 collective-permute-done.5.refs_1_
  85.7 2.0 %shard_map.39.refs_2_ = f32[2,1024,256]{2,1,0:T(8,128)S(1)} custom-call(bf16[512,1024]{1,0:T(8,128)(2,1)S(1)} %constant_dynamic-update-slice_fusion.refs_0_, bf16[512,1024]{1,0:T(8,128)(2,1)S(1)} %collective-permute-done.5.refs_1_), custom_call_target="tpu_custom_call" | custom-call | flops 1073741824 | bytes 4194304 | tf_op jit(solution)/shard_map/pallas_call | solution.py:170
  87.8 0.0 collective-permute-done.7
  87.8 10.7 %collective-permute-done.12 = bf16[256,1024]{1,0:T(8,128)(2,1)S(1)} collective-permute-done((bf16[256,1024]{1,0:T(8,128)(2,1)S(1)}, bf16[256,1024]{1,0:T(8,128)(2,1)S(1)}, u32[]{:S(2)}, u32[]{:S(2)}) %collective-permute-start.12) | collective-permute-done | bytes 524320 | tf_op jit(solution)/shard_map/ppermute | solution.py:38
  98.6 4.1 %collective-permute-start.13 = (bf16[512,1024]{1,0:T(8,128)(2,1)S(1)}, bf16[512,1024]{1,0:T(8,128)(2,1)S(1)}, u32[]{:S(2)}, u32[]{:S(2)}) collective-permute-start(bf16[512,1024]{1,0:T(8,128)(2,1)S(1)} %constant_dynamic-update-slice_fusion.6.refs_0_), channel_id=1, source_target_pairs={{0,1},{1,0},{2,3},{3,2},{4,5},{5,4},{6,7},{7,6},{8,9},{9,8},{10,11... | collective-permute-start | bytes 3145736 | tf_op jit(solution)/shard_map/ppermute | solution.py:38
  102.6 0.0 collective-permute-done.14.refs_1_
  102.7 2.2 %shard_map.41.refs_2_ = f32[2,1024,256]{2,1,0:T(8,128)S(1)} custom-call(bf16[512,1024]{1,0:T(8,128)(2,1)S(1)} %get-tuple-element.39.refs_0_, bf16[512,1024]{1,0:T(8,128)(2,1)S(1)} %collective-permute-done.14.refs_1_, f32[2,1024,256]{2,1,0:T(8,128)S(1)} %shard_map.39.refs_2_), custom_call_target="tpu_custom_call" | custom-call | flops 1073741824 | bytes 4194304 | tf_op jit(solution)/shard_map/pallas_call | solution.py:170
  104.9 0.0 collective-permute-done.13.refs_1_
  104.9 3.2 %shard_map.42 = f32[2,1024,256]{2,1,0:T(8,128)} custom-call(bf16[512,1024]{1,0:T(8,128)(2,1)S(1)} %constant_dynamic-update-slice_fusion.6.refs_0_, bf16[512,1024]{1,0:T(8,128)(2,1)S(1)} %collective-permute-done.13.refs_1_, f32[2,1024,256]{2,1,0:T(8,128)S(1)} %shard_map.41.refs_2_), custom_call_target="tpu_custom_call" | custom-call | flops 1073741824 | bytes 4194304 | tf_op jit(solution)/shard_map/pallas_call | solution.py:170
  (15 shorter events, 0.4 us)
Async XLA Ops:
  0.0 7.8 %copy-start.2 = (f32[256]{0:T(256)S(1)}, f32[256]{0:T(256)}, u32[]{:S(2)}) copy-start(f32[256]{0:T(256)} %param.4) | copy-start | bytes 3076
  0.0 1.9 %copy-start = (bf16[768,2,1,1024]{3,1,2,0:T(2,128)(2,1)S(1)}, bf16[768,2,1,1024]{3,1,2,0:T(2,128)(2,1)}, u32[]{:S(2)}) copy-start(bf16[768,2,1,1024]{3,1,2,0:T(2,128)(2,1)} %param.3) | copy-start | bytes 9437188
  1.9 5.9 %copy-start.1 = (bf16[768,2,1,1024]{3,1,2,0:T(2,128)(2,1)S(1)}, bf16[768,2,1,1024]{3,1,2,0:T(2,128)(2,1)}, u32[]{:S(2)}) copy-start(bf16[768,2,1,1024]{3,1,2,0:T(2,128)(2,1)} %param.3) | copy-start | bytes 9437188
  1.9 5.9 %copy-start.3 = (f32[16,1024]{1,0:T(8,128)S(1)}, f32[16,1024]{1,0:T(8,128)}, u32[]{:S(2)}) copy-start(f32[16,1024]{1,0:T(8,128)} %constant.2.clone.trig_ref) | copy-start | bytes 196612
  2.2 34.0 %collective-permute-start = (bf16[240,2,1024]{2,1,0:T(2,128)(2,1)S(1)}, bf16[240,2,1024]{2,1,0:T(2,128)(2,1)S(1)}, u32[]{:S(2)}, u32[]{:S(2)}) collective-permute-start(bf16[240,2,1024]{2,1,0:T(2,128)(2,1)S(1)} %shard_map.37), channel_id=1, source_target_pairs={{0,1},{1,2},{2,3},{3,4},{4,5},{5,6},{6,7},{7,8},{8,9},{9,10},{10,1... | collective-permute-start | bytes 2949128 | tf_op jit(solution)/shard_map/ppermute | solution.py:59
  9.5 17.6 %collective-permute-start.1 = (bf16[128,1024]{1,0:T(8,128)(2,1)S(1)}, bf16[128,1024]{1,0:T(8,128)(2,1)S(1)}, u32[]{:S(2)}, u32[]{:S(2)}) collective-permute-start(bf16[128,1024]{1,0:T(8,128)(2,1)S(1)} %get-tuple-element.23), channel_id=1, source_target_pairs={{0,8},{1,9},{2,10},{3,11},{4,12},{5,13},{6,14},{7,15},{8,16},{9,17... | collective-permute-start | bytes 786440 | tf_op jit(solution)/shard_map/ppermute | solution.py:38
  12.7 23.5 %collective-permute-start.2 = (bf16[128,1024]{1,0:T(8,128)(2,1)S(1)}, bf16[128,1024]{1,0:T(8,128)(2,1)S(1)}, u32[]{:S(2)}, u32[]{:S(2)}) collective-permute-start(bf16[128,1024]{1,0:T(8,128)(2,1)S(1)} %get-tuple-element.24), channel_id=1, source_target_pairs={{0,16},{1,17},{2,18},{3,19},{4,20},{5,21},{6,22},{7,23},{8,24},{9,... | collective-permute-start | bytes 786440 | tf_op jit(solution)/shard_map/ppermute | solution.py:38
  17.0 19.2 %collective-permute-start.3 = (bf16[128,1024]{1,0:T(8,128)(2,1)S(1)}, bf16[128,1024]{1,0:T(8,128)(2,1)S(1)}, u32[]{:S(2)}, u32[]{:S(2)}) collective-permute-start(bf16[128,1024]{1,0:T(8,128)(2,1)S(1)} %get-tuple-element.25), channel_id=1, source_target_pairs={{0,24},{1,25},{2,26},{3,27},{4,28},{5,29},{6,30},{7,31},{8,0},{9,1... | collective-permute-start | bytes 786440 | tf_op jit(solution)/shard_map/ppermute | solution.py:38
  36.4 18.4 %collective-permute-start.4 = (bf16[256,1024]{1,0:T(8,128)(2,1)S(1)}, bf16[256,1024]{1,0:T(8,128)(2,1)S(1)}, u32[]{:S(2)}, u32[]{:S(2)}) collective-permute-start(bf16[256,1024]{1,0:T(8,128)(2,1)S(1)} %pad_maximum_fusion), channel_id=1, source_target_pairs={{0,2},{1,3},{2,0},{3,1},{4,6},{5,7},{6,4},{7,5},{8,10},{9,11},{10,... | collective-permute-start | bytes 1572872 | tf_op jit(solution)/shard_map/ppermute | solution.py:38
  38.4 27.2 %collective-permute-start.6 = (bf16[256,1024]{1,0:T(8,128)(2,1)S(1)}, bf16[256,1024]{1,0:T(8,128)(2,1)S(1)}, u32[]{:S(2)}, u32[]{:S(2)}) collective-permute-start(bf16[256,1024]{1,0:T(8,128)(2,1)S(1)} %pad_maximum_fusion.1), channel_id=1, source_target_pairs={{0,4},{1,5},{2,6},{3,7},{4,0},{5,1},{6,2},{7,3},{8,12},{9,13},{10,... | collective-permute-start | bytes 1572872 | tf_op jit(solution)/shard_map/ppermute | solution.py:38
  41.0 24.6 %collective-permute-start.8 = (bf16[64,1024]{1,0:T(8,128)(2,1)S(1)}, bf16[64,1024]{1,0:T(8,128)(2,1)S(1)}, u32[]{:S(2)}, u32[]{:S(2)}) collective-permute-start(bf16[64,1024]{1,0:T(8,128)(2,1)S(1)} %get-tuple-element.33), channel_id=1, source_target_pairs={{0,8},{1,9},{2,10},{3,11},{4,12},{5,13},{6,14},{7,15},{8,16},{9,17... | collective-permute-start | bytes 393224 | tf_op jit(solution)/shard_map/ppermute | solution.py:38
  43.0 22.7 %collective-permute-start.9 = (bf16[64,1024]{1,0:T(8,128)(2,1)S(1)}, bf16[64,1024]{1,0:T(8,128)(2,1)S(1)}, u32[]{:S(2)}, u32[]{:S(2)}) collective-permute-start(bf16[64,1024]{1,0:T(8,128)(2,1)S(1)} %get-tuple-element.34), channel_id=1, source_target_pairs={{0,16},{1,17},{2,18},{3,19},{4,20},{5,21},{6,22},{7,23},{8,24},{9,... | collective-permute-start | bytes 393224 | tf_op jit(solution)/shard_map/ppermute | solution.py:38
  45.1 20.6 %collective-permute-start.10 = (bf16[64,1024]{1,0:T(8,128)(2,1)S(1)}, bf16[64,1024]{1,0:T(8,128)(2,1)S(1)}, u32[]{:S(2)}, u32[]{:S(2)}) collective-permute-start(bf16[64,1024]{1,0:T(8,128)(2,1)S(1)} %get-tuple-element.35), channel_id=1, source_target_pairs={{0,24},{1,25},{2,26},{3,27},{4,28},{5,29},{6,30},{7,31},{8,0},{9,1... | collective-permute-start | bytes 393224 | tf_op jit(solution)/shard_map/ppermute | solution.py:38
  54.8 30.9 %collective-permute-start.5 = (bf16[512,1024]{1,0:T(8,128)(2,1)S(1)}, bf16[512,1024]{1,0:T(8,128)(2,1)S(1)}, u32[]{:S(2)}, u32[]{:S(2)}) collective-permute-start(bf16[512,1024]{1,0:T(8,128)(2,1)S(1)} %constant_dynamic-update-slice_fusion.refs_0_), channel_id=1, source_target_pairs={{0,1},{1,0},{2,3},{3,2},{4,5},{5,4},{6,7},{7,6},{8,9},{9,8},{10,11... | collective-permute-start | bytes 3145736 | tf_op jit(solution)/shard_map/ppermute | solution.py:38
  65.7 15.5 %collective-permute-start.11 = (bf16[128,1024]{1,0:T(8,128)(2,1)S(1)}, bf16[128,1024]{1,0:T(8,128)(2,1)S(1)}, u32[]{:S(2)}, u32[]{:S(2)}) collective-permute-start(bf16[128,1024]{1,0:T(8,128)(2,1)S(1)} %pad_maximum_fusion.2), channel_id=1, source_target_pairs={{0,4},{1,5},{2,6},{3,7},{4,0},{5,1},{6,2},{7,3},{8,12},{9,13},{10,... | collective-permute-start | bytes 786440 | tf_op jit(solution)/shard_map/ppermute | solution.py:38
  67.7 20.1 %collective-permute-start.7 = (bf16[256,1024]{1,0:T(8,128)(2,1)S(1)}, bf16[256,1024]{1,0:T(8,128)(2,1)S(1)}, u32[]{:S(2)}, u32[]{:S(2)}) collective-permute-start(bf16[256,1024]{1,0:T(8,128)(2,1)S(1)} %collective-permute-done.6), channel_id=1, source_target_pairs={{0,2},{1,3},{2,0},{3,1},{4,6},{5,7},{6,4},{7,5},{8,10},{9,11},{10,... | collective-permute-start | bytes 1572872 | tf_op jit(solution)/shard_map/ppermute | solution.py:38
  81.3 17.2 %collective-permute-start.12 = (bf16[256,1024]{1,0:T(8,128)(2,1)S(1)}, bf16[256,1024]{1,0:T(8,128)(2,1)S(1)}, u32[]{:S(2)}, u32[]{:S(2)}) collective-permute-start(bf16[256,1024]{1,0:T(8,128)(2,1)S(1)} %get-tuple-element.40), channel_id=1, source_target_pairs={{0,2},{1,3},{2,0},{3,1},{4,6},{5,7},{6,4},{7,5},{8,10},{9,11},{10,... | collective-permute-start | bytes 1572872 | tf_op jit(solution)/shard_map/ppermute | solution.py:38
  83.2 19.4 %collective-permute-start.14 = (bf16[512,1024]{1,0:T(8,128)(2,1)S(1)}, bf16[512,1024]{1,0:T(8,128)(2,1)S(1)}, u32[]{:S(2)}, u32[]{:S(2)}) collective-permute-start(bf16[512,1024]{1,0:T(8,128)(2,1)S(1)} %get-tuple-element.39.refs_0_), channel_id=1, source_target_pairs={{0,1},{1,0},{2,3},{3,2},{4,5},{5,4},{6,7},{7,6},{8,9},{9,8},{10,11... | collective-permute-start | bytes 3145736 | tf_op jit(solution)/shard_map/ppermute | solution.py:38
  98.6 6.3 %collective-permute-start.13 = (bf16[512,1024]{1,0:T(8,128)(2,1)S(1)}, bf16[512,1024]{1,0:T(8,128)(2,1)S(1)}, u32[]{:S(2)}, u32[]{:S(2)}) collective-permute-start(bf16[512,1024]{1,0:T(8,128)(2,1)S(1)} %constant_dynamic-update-slice_fusion.6.refs_0_), channel_id=1, source_target_pairs={{0,1},{1,0},{2,3},{3,2},{4,5},{5,4},{6,7},{7,6},{8,9},{9,8},{10,11... | collective-permute-start | bytes 3145736 | tf_op jit(solution)/shard_map/ppermute | solution.py:38

commit v6 on v5

--- a/solution.py
+++ b/solution.py
@@ -223,16 +223,20 @@
     ma = part(late_all, 0)
     ma_near = move(ma, near_z)
     first_all = spread(first_out)
-    tb = move(part(first_all, 1), far_z)
+    ma_near, *first_all = lax.optimization_barrier((ma_near, *first_all))
+    mb, tb = part(first_all, 0), part(first_all, 1)
+    mb_near, mb_rest = move(mb[: 4 * ROWS], near_z), mb[:0]
+    tb, tb_rest = move(tb[: 4 * ROWS], far_z), tb[:0]
+    ta, mb_near = lax.optimization_barrier((ta, mb_near))
     ta_near = move(ta, near_z)
-    b_own = jnp.concatenate([part(first_all, 0), tb], 0)
-    b_near = move(b_own, near_z)
+    tb = jnp.concatenate([tb, tb_rest], 0)
+    tb_near = move(tb, near_z)
     ma = jnp.concatenate([ma, ma_near], 0)
     acc = correlate([ma, move(ma, other_core)], None)
-    acc, ta_near, b_near = lax.optimization_barrier((acc, ta_near, b_near))
-    near = jnp.concatenate([ta_near, b_near], 0)
+    acc, ta_near, tb_near = lax.optimization_barrier((acc, ta_near, tb_near))
+    near = jnp.concatenate([ta_near, tb_near, tb], 0)
     near_core = move(near, other_core)
-    own = jnp.concatenate([ta, b_own], 0)
+    own = jnp.concatenate([ta, mb, mb_near, mb_rest], 0)
     acc = correlate([own, move(own, other_core)], acc)
     pieces = [near, near_core]
     frames = samples_here // FINE * XS * ZS * CORES

time: 109 us -> 109 us (level)
    ppermute x14 -> x15, starting transfers between devices: 39.7 us -> 40.4 us  [move(): return lax.ppermute(array, 'tm', moves(rule))]
    ppermute x14 -> x15, waiting for transfers between devices: 49.9 us -> 49.8 us  [move(): return lax.ppermute(array, 'tm', moves(rule))]
  transfers between devices with their start and end apart: 15 -> 16, of which waited for: 6 -> 9; matrix products, arithmetic and copies ran while one was open for 0% -> 0% of each run, Pallas kernels for 6% -> 6%
where the time goes in v6:
time: 109 us
  waiting for transfers between devices  49.8 us (46%)
  starting transfers between devices  45.9 us (42%)
  Pallas kernels  10.3 us (9%)
  local copies, waits for them, and re-layouts  2.26 us (2%)
    ppermute x15, waiting for transfers between devices, move(): return lax.ppermute(array, 'tm', moves(rule))  49.8 us
    ppermute x15, starting transfers between devices, move(): return lax.ppermute(array, 'tm', moves(rule))  40.4 us
    pallas_call x3, Pallas kernels, correlate(): pl.pallas_call(functools.partial(products, len(pieces), scale), grid=(4,)...  7.46 us
    ppermute x1, starting transfers between devices, halo_of(): return lax.ppermute(tail, 'tm', pairs)  5.52 us
  transfers between devices with their start and end apart: 16, of which 9 were waited for; matrix products, arithmetic and copies ran while one was open for 0% of the time, Pallas kernels for 6%

profile of v6, /device:TPU:1, one launch (start us, length us, event | category | flops | bytes accessed | tf_op | source)
XLA Modules:
  0.0 108.8 jit_solution(7908890862327312165)
XLA Ops:
  0.0 0.0 copy-start.2
  0.0 0.0 copy-start
  0.0 1.9 %copy-done = bf16[768,2,1,1024]{3,1,2,0:T(2,128)(2,1)S(1)} copy-done((bf16[768,2,1,1024]{3,1,2,0:T(2,128)(2,1)S(1)}, bf16[768,2,1,1024]{3,1,2,0:T(2,128)(2,1)}, u32[]{:S(2)}) %copy-start) | copy-done | bytes 3145752
  1.9 0.0 copy-start.1
  1.9 0.0 copy-start.3
  1.9 0.3 shard_map.37
  2.2 5.5 %collective-permute-start = (bf16[240,2,1024]{2,1,0:T(2,128)(2,1)S(1)}, bf16[240,2,1024]{2,1,0:T(2,128)(2,1)S(1)}, u32[]{:S(2)}, u32[]{:S(2)}) collective-permute-start(bf16[240,2,1024]{2,1,0:T(2,128)(2,1)S(1)} %shard_map.37), channel_id=1, source_target_pairs={{0,1},{1,2},{2,3},{3,4},{4,5},{5,6},{6,7},{7,8},{8,9},{9,10},{10,1... | collective-permute-start | bytes 2949128 | tf_op jit(solution)/shard_map/ppermute | solution.py:59
  7.8 0.0 copy-done.2
  7.8 0.0 copy-done.1
  7.8 0.0 copy-done.3
  7.8 1.7 %shard_map.38 = (bf16[256,1024]{1,0:T(8,128)(2,1)S(1)}, bf16[128,1024]{1,0:T(8,128)(2,1)S(1)}, bf16[128,1024]{1,0:T(8,128)(2,1)S(1)}, bf16[128,1024]{1,0:T(8,128)(2,1)S(1)}, bf16[128,1024]{1,0:T(8,128)(2,1)S(1)}) custom-call(f32[1,256]{1,0:T(1,128)S(1)} %bitcast.6, f32[16,1024]{1,0:T(8,128)S(1)} %copy-done.3, bf16[768,2,1024]{2,1,0:T(2,128)(2,1)S(1)} %bitcast.4), custom_call_target="tpu_custom_call" | custom-call | flops 1073741824 | bytes 6291456 | tf_op jit(solution)/shard_map/pallas_call | solution.py:204
  9.5 3.1 %collective-permute-start.1 = (bf16[128,1024]{1,0:T(8,128)(2,1)S(1)}, bf16[128,1024]{1,0:T(8,128)(2,1)S(1)}, u32[]{:S(2)}, u32[]{:S(2)}) collective-permute-start(bf16[128,1024]{1,0:T(8,128)(2,1)S(1)} %get-tuple-element.30), channel_id=1, source_target_pairs={{0,8},{1,9},{2,10},{3,11},{4,12},{5,13},{6,14},{7,15},{8,16},{9,17... | collective-permute-start | bytes 786440 | tf_op jit(solution)/shard_map/ppermute | solution.py:38
  12.7 4.4 %collective-permute-start.2 = (bf16[128,1024]{1,0:T(8,128)(2,1)S(1)}, bf16[128,1024]{1,0:T(8,128)(2,1)S(1)}, u32[]{:S(2)}, u32[]{:S(2)}) collective-permute-start(bf16[128,1024]{1,0:T(8,128)(2,1)S(1)} %get-tuple-element.31), channel_id=1, source_target_pairs={{0,16},{1,17},{2,18},{3,19},{4,20},{5,21},{6,22},{7,23},{8,24},{9,... | collective-permute-start | bytes 786440 | tf_op jit(solution)/shard_map/ppermute | solution.py:38
  17.0 3.1 %collective-permute-start.3 = (bf16[128,1024]{1,0:T(8,128)(2,1)S(1)}, bf16[128,1024]{1,0:T(8,128)(2,1)S(1)}, u32[]{:S(2)}, u32[]{:S(2)}) collective-permute-start(bf16[128,1024]{1,0:T(8,128)(2,1)S(1)} %get-tuple-element.32), channel_id=1, source_target_pairs={{0,24},{1,25},{2,26},{3,27},{4,28},{5,29},{6,30},{7,31},{8,0},{9,1... | collective-permute-start | bytes 786440 | tf_op jit(solution)/shard_map/ppermute | solution.py:38
  20.1 7.0 %collective-permute-done.1 = bf16[128,1024]{1,0:T(8,128)(2,1)S(1)} collective-permute-done((bf16[128,1024]{1,0:T(8,128)(2,1)S(1)}, bf16[128,1024]{1,0:T(8,128)(2,1)S(1)}, u32[]{:S(2)}, u32[]{:S(2)}) %collective-permute-start.1) | collective-permute-done | bytes 262176 | tf_op jit(solution)/shard_map/ppermute | solution.py:38
  27.1 9.1 %collective-permute-done.2 = bf16[128,1024]{1,0:T(8,128)(2,1)S(1)} collective-permute-done((bf16[128,1024]{1,0:T(8,128)(2,1)S(1)}, bf16[128,1024]{1,0:T(8,128)(2,1)S(1)}, u32[]{:S(2)}, u32[]{:S(2)}) %collective-permute-start.2) | collective-permute-done | bytes 262176 | tf_op jit(solution)/shard_map/ppermute | solution.py:38
  36.2 0.0 collective-permute-done.3
  36.2 0.0 collective-permute-done.halo_ref
  36.4 1.9 %collective-permute-start.4 = (bf16[256,1024]{1,0:T(8,128)(2,1)S(1)}, bf16[256,1024]{1,0:T(8,128)(2,1)S(1)}, u32[]{:S(2)}, u32[]{:S(2)}) collective-permute-start(bf16[256,1024]{1,0:T(8,128)(2,1)S(1)} %pad_maximum_fusion), channel_id=1, source_target_pairs={{0,2},{1,3},{2,0},{3,1},{4,6},{5,7},{6,4},{7,5},{8,10},{9,11},{10,... | collective-permute-start | bytes 1572872 | tf_op jit(solution)/shard_map/ppermute | solution.py:38
  38.3 1.9 %collective-permute-start.9 = (bf16[256,1024]{1,0:T(8,128)(2,1)S(1)}, bf16[256,1024]{1,0:T(8,128)(2,1)S(1)}, u32[]{:S(2)}, u32[]{:S(2)}) collective-permute-start(bf16[256,1024]{1,0:T(8,128)(2,1)S(1)} %pad_maximum_fusion.1), channel_id=1, source_target_pairs={{0,4},{1,5},{2,6},{3,7},{4,0},{5,1},{6,2},{7,3},{8,12},{9,13},{10,... | collective-permute-start | bytes 1572872 | tf_op jit(solution)/shard_map/ppermute | solution.py:38
  40.3 0.8 shard_map.39
  41.0 1.9 %collective-permute-start.5 = (bf16[64,1024]{1,0:T(8,128)(2,1)S(1)}, bf16[64,1024]{1,0:T(8,128)(2,1)S(1)}, u32[]{:S(2)}, u32[]{:S(2)}) collective-permute-start(bf16[64,1024]{1,0:T(8,128)(2,1)S(1)} %get-tuple-element.40), channel_id=1, source_target_pairs={{0,8},{1,9},{2,10},{3,11},{4,12},{5,13},{6,14},{7,15},{8,16},{9,17... | collective-permute-start | bytes 393224 | tf_op jit(solution)/shard_map/ppermute | solution.py:38
  43.0 2.1 %collective-permute-start.6 = (bf16[64,1024]{1,0:T(8,128)(2,1)S(1)}, bf16[64,1024]{1,0:T(8,128)(2,1)S(1)}, u32[]{:S(2)}, u32[]{:S(2)}) collective-permute-start(bf16[64,1024]{1,0:T(8,128)(2,1)S(1)} %get-tuple-element.41), channel_id=1, source_target_pairs={{0,16},{1,17},{2,18},{3,19},{4,20},{5,21},{6,22},{7,23},{8,24},{9,... | collective-permute-start | bytes 393224 | tf_op jit(solution)/shard_map/ppermute | solution.py:38
  45.1 4.4 %collective-permute-start.7 = (bf16[64,1024]{1,0:T(8,128)(2,1)S(1)}, bf16[64,1024]{1,0:T(8,128)(2,1)S(1)}, u32[]{:S(2)}, u32[]{:S(2)}) collective-permute-start(bf16[64,1024]{1,0:T(8,128)(2,1)S(1)} %get-tuple-element.42), channel_id=1, source_target_pairs={{0,24},{1,25},{2,26},{3,27},{4,28},{5,29},{6,30},{7,31},{8,0},{9,1... | collective-permute-start | bytes 393224 | tf_op jit(solution)/shard_map/ppermute | solution.py:38
  49.5 0.0 collective-permute-done.5
  49.5 1.6 %collective-permute-done.6 = bf16[64,1024]{1,0:T(8,128)(2,1)S(1)} collective-permute-done((bf16[64,1024]{1,0:T(8,128)(2,1)S(1)}, bf16[64,1024]{1,0:T(8,128)(2,1)S(1)}, u32[]{:S(2)}, u32[]{:S(2)}) %collective-permute-start.6) | collective-permute-done | bytes 131104 | tf_op jit(solution)/shard_map/ppermute | solution.py:38
  51.1 2.9 %collective-permute-done.7 = bf16[64,1024]{1,0:T(8,128)(2,1)S(1)} collective-permute-done((bf16[64,1024]{1,0:T(8,128)(2,1)S(1)}, bf16[64,1024]{1,0:T(8,128)(2,1)S(1)}, u32[]{:S(2)}, u32[]{:S(2)}) %collective-permute-start.7) | collective-permute-done | bytes 131104 | tf_op jit(solution)/shard_map/ppermute | solution.py:38
  54.0 0.7 collective-permute-done.4
  54.9 2.6 %collective-permute-start.10 = (bf16[128,1024]{1,0:T(8,128)(2,1)S(1)}, bf16[128,1024]{1,0:T(8,128)(2,1)S(1)}, u32[]{:S(2)}, u32[]{:S(2)}) collective-permute-start(bf16[128,1024]{1,0:T(8,128)(2,1)S(1)} %pad_maximum_fusion.2), channel_id=1, source_target_pairs={{0,2},{1,3},{2,0},{3,1},{4,6},{5,7},{6,4},{7,5},{8,10},{9,11},{10,... | collective-permute-start | bytes 786440 | tf_op jit(solution)/shard_map/ppermute | solution.py:38
  57.5 3.6 %collective-permute-start.8 = (bf16[512,1024]{1,0:T(8,128)(2,1)S(1)}, bf16[512,1024]{1,0:T(8,128)(2,1)S(1)}, u32[]{:S(2)}, u32[]{:S(2)}) collective-permute-start(bf16[512,1024]{1,0:T(8,128)(2,1)S(1)} %constant_dynamic-update-slice_fusion.refs_0_), channel_id=1, source_target_pairs={{0,1},{1,0},{2,3},{3,2},{4,5},{5,4},{6,7},{7,6},{8,9},{9,8},{10,11... | collective-permute-start | bytes 3145736 | tf_op jit(solution)/shard_map/ppermute | solution.py:38
  61.1 4.5 %collective-permute-done.9 = bf16[256,1024]{1,0:T(8,128)(2,1)S(1)} collective-permute-done((bf16[256,1024]{1,0:T(8,128)(2,1)S(1)}, bf16[256,1024]{1,0:T(8,128)(2,1)S(1)}, u32[]{:S(2)}, u32[]{:S(2)}) %collective-permute-start.9) | collective-permute-done | bytes 524320 | tf_op jit(solution)/shard_map/ppermute | solution.py:38
  65.6 6.3 %collective-permute-done.10 = bf16[128,1024]{1,0:T(8,128)(2,1)S(1)} collective-permute-done((bf16[128,1024]{1,0:T(8,128)(2,1)S(1)}, bf16[128,1024]{1,0:T(8,128)(2,1)S(1)}, u32[]{:S(2)}, u32[]{:S(2)}) %collective-permute-start.10) | collective-permute-done | bytes 262176 | tf_op jit(solution)/shard_map/ppermute | solution.py:38
  72.0 1.9 %collective-permute-start.12 = (bf16[128,1024]{1,0:T(8,128)(2,1)S(1)}, bf16[128,1024]{1,0:T(8,128)(2,1)S(1)}, u32[]{:S(2)}, u32[]{:S(2)}) collective-permute-start(bf16[128,1024]{1,0:T(8,128)(2,1)S(1)} %pad_maximum_fusion.3), channel_id=1, source_target_pairs={{0,4},{1,5},{2,6},{3,7},{4,0},{5,1},{6,2},{7,3},{8,12},{9,13},{10,... | collective-permute-start | bytes 786440 | tf_op jit(solution)/shard_map/ppermute | solution.py:38
  74.0 1.9 %collective-permute-start.11 = (bf16[256,1024]{1,0:T(8,128)(2,1)S(1)}, bf16[256,1024]{1,0:T(8,128)(2,1)S(1)}, u32[]{:S(2)}, u32[]{:S(2)}) collective-permute-start(bf16[256,1024]{1,0:T(8,128)(2,1)S(1)} %collective-permute-done.9), channel_id=1, source_target_pairs={{0,2},{1,3},{2,0},{3,1},{4,6},{5,7},{6,4},{7,5},{8,10},{9,11},{10,... | collective-permute-start | bytes 1572872 | tf_op jit(solution)/shard_map/ppermute | solution.py:38
  75.9 11.8 %collective-permute-done.12 = bf16[128,1024]{1,0:T(8,128)(2,1)S(1)} collective-permute-done((bf16[128,1024]{1,0:T(8,128)(2,1)S(1)}, bf16[128,1024]{1,0:T(8,128)(2,1)S(1)}, u32[]{:S(2)}, u32[]{:S(2)}) %collective-permute-start.12) | collective-permute-done | bytes 262176 | tf_op jit(solution)/shard_map/ppermute | solution.py:38
  87.7 1.9 %collective-permute-start.13 = (bf16[128,1024]{1,0:T(8,128)(2,1)S(1)}, bf16[128,1024]{1,0:T(8,128)(2,1)S(1)}, u32[]{:S(2)}, u32[]{:S(2)}) collective-permute-start(bf16[128,1024]{1,0:T(8,128)(2,1)S(1)} %collective-permute-done.12), channel_id=1, source_target_pairs={{0,2},{1,3},{2,0},{3,1},{4,6},{5,7},{6,4},{7,5},{8,10},{9,11},{10,... | collective-permute-start | bytes 786440 | tf_op jit(solution)/shard_map/ppermute | solution.py:38
  89.6 2.5 %collective-permute-start.15 = (bf16[512,1024]{1,0:T(8,128)(2,1)S(1)}, bf16[512,1024]{1,0:T(8,128)(2,1)S(1)}, u32[]{:S(2)}, u32[]{:S(2)}) collective-permute-start(bf16[512,1024]{1,0:T(8,128)(2,1)S(1)} %constant_dynamic-update-slice_fusion.8.refs_0_), channel_id=1, source_target_pairs={{0,1},{1,0},{2,3},{3,2},{4,5},{5,4},{6,7},{7,6},{8,9},{9,8},{10,11... | collective-permute-start | bytes 3145736 | tf_op jit(solution)/shard_map/ppermute | solution.py:38
  92.1 0.0 collective-permute-done.8.refs_1_
  92.1 2.0 %shard_map.40.refs_2_ = f32[2,1024,256]{2,1,0:T(8,128)S(1)} custom-call(bf16[512,1024]{1,0:T(8,128)(2,1)S(1)} %constant_dynamic-update-slice_fusion.refs_0_, bf16[512,1024]{1,0:T(8,128)(2,1)S(1)} %collective-permute-done.8.refs_1_), custom_call_target="tpu_custom_call" | custom-call | flops 1073741824 | bytes 4194304 | tf_op jit(solution)/shard_map/pallas_call | solution.py:170
  94.2 5.8 %collective-permute-done.13 = bf16[128,1024]{1,0:T(8,128)(2,1)S(1)} collective-permute-done((bf16[128,1024]{1,0:T(8,128)(2,1)S(1)}, bf16[128,1024]{1,0:T(8,128)(2,1)S(1)}, u32[]{:S(2)}, u32[]{:S(2)}) %collective-permute-start.13) | collective-permute-done | bytes 262176 | tf_op jit(solution)/shard_map/ppermute | solution.py:38
  100.0 0.0 collective-permute-done.11
  100.1 3.2 %collective-permute-start.14 = (bf16[512,1024]{1,0:T(8,128)(2,1)S(1)}, bf16[512,1024]{1,0:T(8,128)(2,1)S(1)}, u32[]{:S(2)}, u32[]{:S(2)}) collective-permute-start(bf16[512,1024]{1,0:T(8,128)(2,1)S(1)} %constant_dynamic-update-slice_fusion.5.refs_0_), channel_id=1, source_target_pairs={{0,1},{1,0},{2,3},{3,2},{4,5},{5,4},{6,7},{7,6},{8,9},{9,8},{10,11... | collective-permute-start | bytes 3145736 | tf_op jit(solution)/shard_map/ppermute | solution.py:38
  103.3 0.0 collective-permute-done.15.refs_1_
  103.3 2.3 %shard_map.41.refs_2_ = f32[2,1024,256]{2,1,0:T(8,128)S(1)} custom-call(bf16[512,1024]{1,0:T(8,128)(2,1)S(1)} %constant_dynamic-update-slice_fusion.8.refs_0_, bf16[512,1024]{1,0:T(8,128)(2,1)S(1)} %collective-permute-done.15.refs_1_, f32[2,1024,256]{2,1,0:T(8,128)S(1)} %shard_map.40.refs_2_), custom_call_target="tpu_custom_call" | custom-call | flops 1073741824 | bytes 4194304 | tf_op jit(solution)/shard_map/pallas_call | solution.py:170
  105.6 0.0 collective-permute-done.14.refs_1_
  105.6 3.2 %shard_map.42 = f32[2,1024,256]{2,1,0:T(8,128)} custom-call(bf16[512,1024]{1,0:T(8,128)(2,1)S(1)} %constant_dynamic-update-slice_fusion.5.refs_0_, bf16[512,1024]{1,0:T(8,128)(2,1)S(1)} %collective-permute-done.14.refs_1_, f32[2,1024,256]{2,1,0:T(8,128)S(1)} %shard_map.41.refs_2_), custom_call_target="tpu_custom_call" | custom-call | flops 1073741824 | bytes 4194304 | tf_op jit(solution)/shard_map/pallas_call | solution.py:170
  (22 shorter events, 0.5 us)
Async XLA Ops:
  0.0 7.8 %copy-start.2 = (f32[256]{0:T(256)S(1)}, f32[256]{0:T(256)}, u32[]{:S(2)}) copy-start(f32[256]{0:T(256)} %param.4) | copy-start | bytes 3076
  0.0 1.9 %copy-start = (bf16[768,2,1,1024]{3,1,2,0:T(2,128)(2,1)S(1)}, bf16[768,2,1,1024]{3,1,2,0:T(2,128)(2,1)}, u32[]{:S(2)}) copy-start(bf16[768,2,1,1024]{3,1,2,0:T(2,128)(2,1)} %param.3) | copy-start | bytes 9437188
  1.9 5.9 %copy-start.1 = (bf16[768,2,1,1024]{3,1,2,0:T(2,128)(2,1)S(1)}, bf16[768,2,1,1024]{3,1,2,0:T(2,128)(2,1)}, u32[]{:S(2)}) copy-start(bf16[768,2,1,1024]{3,1,2,0:T(2,128)(2,1)} %param.3) | copy-start | bytes 9437188
  1.9 5.9 %copy-start.3 = (f32[16,1024]{1,0:T(8,128)S(1)}, f32[16,1024]{1,0:T(8,128)}, u32[]{:S(2)}) copy-start(f32[16,1024]{1,0:T(8,128)} %constant.2.clone.trig_ref) | copy-start | bytes 196612
  2.2 34.0 %collective-permute-start = (bf16[240,2,1024]{2,1,0:T(2,128)(2,1)S(1)}, bf16[240,2,1024]{2,1,0:T(2,128)(2,1)S(1)}, u32[]{:S(2)}, u32[]{:S(2)}) collective-permute-start(bf16[240,2,1024]{2,1,0:T(2,128)(2,1)S(1)} %shard_map.37), channel_id=1, source_target_pairs={{0,1},{1,2},{2,3},{3,4},{4,5},{5,6},{6,7},{7,8},{8,9},{9,10},{10,1... | collective-permute-start | bytes 2949128 | tf_op jit(solution)/shard_map/ppermute | solution.py:59
  9.5 17.6 %collective-permute-start.1 = (bf16[128,1024]{1,0:T(8,128)(2,1)S(1)}, bf16[128,1024]{1,0:T(8,128)(2,1)S(1)}, u32[]{:S(2)}, u32[]{:S(2)}) collective-permute-start(bf16[128,1024]{1,0:T(8,128)(2,1)S(1)} %get-tuple-element.30), channel_id=1, source_target_pairs={{0,8},{1,9},{2,10},{3,11},{4,12},{5,13},{6,14},{7,15},{8,16},{9,17... | collective-permute-start | bytes 786440 | tf_op jit(solution)/shard_map/ppermute | solution.py:38
  12.7 23.5 %collective-permute-start.2 = (bf16[128,1024]{1,0:T(8,128)(2,1)S(1)}, bf16[128,1024]{1,0:T(8,128)(2,1)S(1)}, u32[]{:S(2)}, u32[]{:S(2)}) collective-permute-start(bf16[128,1024]{1,0:T(8,128)(2,1)S(1)} %get-tuple-element.31), channel_id=1, source_target_pairs={{0,16},{1,17},{2,18},{3,19},{4,20},{5,21},{6,22},{7,23},{8,24},{9,... | collective-permute-start | bytes 786440 | tf_op jit(solution)/shard_map/ppermute | solution.py:38
  17.0 19.2 %collective-permute-start.3 = (bf16[128,1024]{1,0:T(8,128)(2,1)S(1)}, bf16[128,1024]{1,0:T(8,128)(2,1)S(1)}, u32[]{:S(2)}, u32[]{:S(2)}) collective-permute-start(bf16[128,1024]{1,0:T(8,128)(2,1)S(1)} %get-tuple-element.32), channel_id=1, source_target_pairs={{0,24},{1,25},{2,26},{3,27},{4,28},{5,29},{6,30},{7,31},{8,0},{9,1... | collective-permute-start | bytes 786440 | tf_op jit(solution)/shard_map/ppermute | solution.py:38
  36.4 18.4 %collective-permute-start.4 = (bf16[256,1024]{1,0:T(8,128)(2,1)S(1)}, bf16[256,1024]{1,0:T(8,128)(2,1)S(1)}, u32[]{:S(2)}, u32[]{:S(2)}) collective-permute-start(bf16[256,1024]{1,0:T(8,128)(2,1)S(1)} %pad_maximum_fusion), channel_id=1, source_target_pairs={{0,2},{1,3},{2,0},{3,1},{4,6},{5,7},{6,4},{7,5},{8,10},{9,11},{10,... | collective-permute-start | bytes 1572872 | tf_op jit(solution)/shard_map/ppermute | solution.py:38
  38.3 27.2 %collective-permute-start.9 = (bf16[256,1024]{1,0:T(8,128)(2,1)S(1)}, bf16[256,1024]{1,0:T(8,128)(2,1)S(1)}, u32[]{:S(2)}, u32[]{:S(2)}) collective-permute-start(bf16[256,1024]{1,0:T(8,128)(2,1)S(1)} %pad_maximum_fusion.1), channel_id=1, source_target_pairs={{0,4},{1,5},{2,6},{3,7},{4,0},{5,1},{6,2},{7,3},{8,12},{9,13},{10,... | collective-permute-start | bytes 1572872 | tf_op jit(solution)/shard_map/ppermute | solution.py:38
  41.0 8.4 %collective-permute-start.5 = (bf16[64,1024]{1,0:T(8,128)(2,1)S(1)}, bf16[64,1024]{1,0:T(8,128)(2,1)S(1)}, u32[]{:S(2)}, u32[]{:S(2)}) collective-permute-start(bf16[64,1024]{1,0:T(8,128)(2,1)S(1)} %get-tuple-element.40), channel_id=1, source_target_pairs={{0,8},{1,9},{2,10},{3,11},{4,12},{5,13},{6,14},{7,15},{8,16},{9,17... | collective-permute-start | bytes 393224 | tf_op jit(solution)/shard_map/ppermute | solution.py:38
  43.0 8.1 %collective-permute-start.6 = (bf16[64,1024]{1,0:T(8,128)(2,1)S(1)}, bf16[64,1024]{1,0:T(8,128)(2,1)S(1)}, u32[]{:S(2)}, u32[]{:S(2)}) collective-permute-start(bf16[64,1024]{1,0:T(8,128)(2,1)S(1)} %get-tuple-element.41), channel_id=1, source_target_pairs={{0,16},{1,17},{2,18},{3,19},{4,20},{5,21},{6,22},{7,23},{8,24},{9,... | collective-permute-start | bytes 393224 | tf_op jit(solution)/shard_map/ppermute | solution.py:38
  45.1 8.9 %collective-permute-start.7 = (bf16[64,1024]{1,0:T(8,128)(2,1)S(1)}, bf16[64,1024]{1,0:T(8,128)(2,1)S(1)}, u32[]{:S(2)}, u32[]{:S(2)}) collective-permute-start(bf16[64,1024]{1,0:T(8,128)(2,1)S(1)} %get-tuple-element.42), channel_id=1, source_target_pairs={{0,24},{1,25},{2,26},{3,27},{4,28},{5,29},{6,30},{7,31},{8,0},{9,1... | collective-permute-start | bytes 393224 | tf_op jit(solution)/shard_map/ppermute | solution.py:38
  54.9 17.0 %collective-permute-start.10 = (bf16[128,1024]{1,0:T(8,128)(2,1)S(1)}, bf16[128,1024]{1,0:T(8,128)(2,1)S(1)}, u32[]{:S(2)}, u32[]{:S(2)}) collective-permute-start(bf16[128,1024]{1,0:T(8,128)(2,1)S(1)} %pad_maximum_fusion.2), channel_id=1, source_target_pairs={{0,2},{1,3},{2,0},{3,1},{4,6},{5,7},{6,4},{7,5},{8,10},{9,11},{10,... | collective-permute-start | bytes 786440 | tf_op jit(solution)/shard_map/ppermute | solution.py:38
  57.5 34.6 %collective-permute-start.8 = (bf16[512,1024]{1,0:T(8,128)(2,1)S(1)}, bf16[512,1024]{1,0:T(8,128)(2,1)S(1)}, u32[]{:S(2)}, u32[]{:S(2)}) collective-permute-start(bf16[512,1024]{1,0:T(8,128)(2,1)S(1)} %constant_dynamic-update-slice_fusion.refs_0_), channel_id=1, source_target_pairs={{0,1},{1,0},{2,3},{3,2},{4,5},{5,4},{6,7},{7,6},{8,9},{9,8},{10,11... | collective-permute-start | bytes 3145736 | tf_op jit(solution)/shard_map/ppermute | solution.py:38
  72.0 15.7 %collective-permute-start.12 = (bf16[128,1024]{1,0:T(8,128)(2,1)S(1)}, bf16[128,1024]{1,0:T(8,128)(2,1)S(1)}, u32[]{:S(2)}, u32[]{:S(2)}) collective-permute-start(bf16[128,1024]{1,0:T(8,128)(2,1)S(1)} %pad_maximum_fusion.3), channel_id=1, source_target_pairs={{0,4},{1,5},{2,6},{3,7},{4,0},{5,1},{6,2},{7,3},{8,12},{9,13},{10,... | collective-permute-start | bytes 786440 | tf_op jit(solution)/shard_map/ppermute | solution.py:38
  74.0 26.0 %collective-permute-start.11 = (bf16[256,1024]{1,0:T(8,128)(2,1)S(1)}, bf16[256,1024]{1,0:T(8,128)(2,1)S(1)}, u32[]{:S(2)}, u32[]{:S(2)}) collective-permute-start(bf16[256,1024]{1,0:T(8,128)(2,1)S(1)} %collective-permute-done.9), channel_id=1, source_target_pairs={{0,2},{1,3},{2,0},{3,1},{4,6},{5,7},{6,4},{7,5},{8,10},{9,11},{10,... | collective-permute-start | bytes 1572872 | tf_op jit(solution)/shard_map/ppermute | solution.py:38
  87.7 12.3 %collective-permute-start.13 = (bf16[128,1024]{1,0:T(8,128)(2,1)S(1)}, bf16[128,1024]{1,0:T(8,128)(2,1)S(1)}, u32[]{:S(2)}, u32[]{:S(2)}) collective-permute-start(bf16[128,1024]{1,0:T(8,128)(2,1)S(1)} %collective-permute-done.12), channel_id=1, source_target_pairs={{0,2},{1,3},{2,0},{3,1},{4,6},{5,7},{6,4},{7,5},{8,10},{9,11},{10,... | collective-permute-start | bytes 786440 | tf_op jit(solution)/shard_map/ppermute | solution.py:38
  89.6 13.7 %collective-permute-start.15 = (bf16[512,1024]{1,0:T(8,128)(2,1)S(1)}, bf16[512,1024]{1,0:T(8,128)(2,1)S(1)}, u32[]{:S(2)}, u32[]{:S(2)}) collective-permute-start(bf16[512,1024]{1,0:T(8,128)(2,1)S(1)} %constant_dynamic-update-slice_fusion.8.refs_0_), channel_id=1, source_target_pairs={{0,1},{1,0},{2,3},{3,2},{4,5},{5,4},{6,7},{7,6},{8,9},{9,8},{10,11... | collective-permute-start | bytes 3145736 | tf_op jit(solution)/shard_map/ppermute | solution.py:38
  100.1 5.5 %collective-permute-start.14 = (bf16[512,1024]{1,0:T(8,128)(2,1)S(1)}, bf16[512,1024]{1,0:T(8,128)(2,1)S(1)}, u32[]{:S(2)}, u32[]{:S(2)}) collective-permute-start(bf16[512,1024]{1,0:T(8,128)(2,1)S(1)} %constant_dynamic-update-slice_fusion.5.refs_0_), channel_id=1, source_target_pairs={{0,1},{1,0},{2,3},{3,2},{4,5},{5,4},{6,7},{7,6},{8,9},{9,8},{10,11... | collective-permute-start | bytes 3145736 | tf_op jit(solution)/shard_map/ppermute | solution.py:38

commit v7 on v5

--- a/solution.py
+++ b/solution.py
@@ -55,8 +55,11 @@
 
 
 def halo_of(tail):
-    pairs = [(i, i + 1) for i in range(XS * ZS * CORES - 1)]
-    return lax.ppermute(tail, "tm", pairs)
+    run = ZS * CORES
+    pairs = [(i, i + 1) for i in range(XS * run - 1)]
+    inside = [pair for pair in pairs if pair[1] % run]
+    across = [pair for pair in pairs if not pair[1] % run]
+    return lax.ppermute(tail, "tm", inside), lax.ppermute(tail, "tm", across)
 
 
 def trig_table():
@@ -123,10 +126,10 @@
                 out_refs[d][at : at + ROWS, :] = out[(2 * d + other) * ROWS : (2 * d + other + 1) * ROWS]
 
 
-def filter_first(halo_ref, volt_ref, band_ref, *out_refs):
+def filter_first(halo_ref, wrap_ref, volt_ref, band_ref, *out_refs):
     here = BLOCK * FINE
     own = volt_ref[0:here].reshape(2 * here, S)
-    prior = halo_ref[...].reshape(2 * here - 2 * FINE, S)
+    prior = (halo_ref[...] + wrap_ref[...]).reshape(2 * here - 2 * FINE, S)
     band = band_ref[...]
     out = jnp.dot(band[:, 2 * here :], own, preferred_element_type=F32)
     out += jnp.dot(band[:, 2 * FINE : 2 * here], prior, preferred_element_type=F32)
@@ -200,7 +203,7 @@
         scratch_shapes=[pltpu.SemaphoreType.DMA],
         compiler_params=params,
     )(volt)
-    halo = halo_of(tail)
+    halo, wrap = halo_of(tail)
     band, *late_out = pl.pallas_call(
         filter_late,
         out_shape=(shape(4 * FOUT * BLOCK // 2, 2 * WINDOW), *[shape(4 * ROWS, S)] * XS),
@@ -214,11 +217,11 @@
     first_out = pl.pallas_call(
         filter_first,
         out_shape=[shape(2 * ROWS, S)] * XS,
-        in_specs=spec(3),
+        in_specs=spec(4),
         out_specs=spec(XS),
         compiler_params=params,
         cost_estimate=pl.CostEstimate(flops=1 << 29, bytes_accessed=3 << 20, transcendentals=0),
-    )(halo, volt, band)
+    )(halo, wrap, volt, band)
     ta = move(part(late_all, 1), far_z)
     ma = part(late_all, 0)
     ma_near = move(ma, near_z)

time: 109 us -> 106 us (0.972)
  waiting for transfers between devices: 49.9 us -> 44.2 us
  starting transfers between devices: 45.2 us -> 48 us
    ppermute x14, waiting for transfers between devices: 49.9 us -> 44.2 us  [move(): return lax.ppermute(array, 'tm', moves(rule))]
    ppermute x14, starting transfers between devices: 39.7 us -> 41.7 us  [move(): return lax.ppermute(array, 'tm', moves(rule))]
    ppermute x1 -> x2, starting transfers between devices: 5.52 us -> 6.25 us  [halo_of(): return (lax.ppermute(tail, 'tm', inside), lax.ppermute(tail, 'tm', across))]
  transfers between devices with their start and end apart: 15 -> 16, of which waited for: 6 -> 6; matrix products, arithmetic and copies ran while one was open for 0% -> 0% of each run, Pallas kernels for 6% -> 7%
where the time goes in v7:
time: 106 us; the launch traced here: 105 us
  starting transfers between devices  48 us (45%)
  waiting for transfers between devices  44.2 us (42%)
  Pallas kernels  10.3 us (10%)
  local copies, waits for them, and re-layouts  2.28 us (2%)
    ppermute x14, waiting for transfers between devices, move(): return lax.ppermute(array, 'tm', moves(rule))  44.2 us
    ppermute x14, starting transfers between devices, move(): return lax.ppermute(array, 'tm', moves(rule))  41.7 us
    pallas_call x3, Pallas kernels, correlate(): pl.pallas_call(functools.partial(products, len(pieces), scale), grid=(4,)...  7.47 us
    ppermute x2, starting transfers between devices, halo_of(): return (lax.ppermute(tail, 'tm', inside), lax.ppermute(tail, 'tm', across))  6.25 us
  transfers between devices with their start and end apart: 16, of which 6 were waited for; matrix products, arithmetic and copies ran while one was open for 0% of the time, Pallas kernels for 7%

profile of v7, /device:TPU:1, one launch (start us, length us, event | category | flops | bytes accessed | tf_op | source)
XLA Modules:
  0.0 105.3 jit_solution(2506210790990774366)
XLA Ops:
  0.0 0.0 copy-start.2
  0.0 0.0 copy-start
  0.0 1.9 %copy-done = bf16[768,2,1,1024]{3,1,2,0:T(2,128)(2,1)S(1)} copy-done((bf16[768,2,1,1024]{3,1,2,0:T(2,128)(2,1)S(1)}, bf16[768,2,1,1024]{3,1,2,0:T(2,128)(2,1)}, u32[]{:S(2)}) %copy-start) | copy-done | bytes 3145752
  1.9 0.0 copy-start.1
  1.9 0.0 copy-start.3
  1.9 0.3 shard_map.37
  2.2 5.5 %collective-permute-start = (bf16[240,2,1024]{2,1,0:T(2,128)(2,1)S(1)}, bf16[240,2,1024]{2,1,0:T(2,128)(2,1)S(1)}, u32[]{:S(2)}, u32[]{:S(2)}) collective-permute-start(bf16[240,2,1024]{2,1,0:T(2,128)(2,1)S(1)} %shard_map.37), channel_id=1, source_target_pairs={{0,1},{1,2},{2,3},{3,4},{4,5},{5,6},{6,7},{8,9},{9,10},{10,11},{11... | collective-permute-start | bytes 2949128 | tf_op jit(solution)/shard_map/ppermute | solution.py:62
  7.8 0.0 copy-done.2
  7.8 0.0 copy-done.1
  7.8 0.0 copy-done.3
  7.8 1.7 %shard_map.38 = (bf16[256,1024]{1,0:T(8,128)(2,1)S(1)}, bf16[128,1024]{1,0:T(8,128)(2,1)S(1)}, bf16[128,1024]{1,0:T(8,128)(2,1)S(1)}, bf16[128,1024]{1,0:T(8,128)(2,1)S(1)}, bf16[128,1024]{1,0:T(8,128)(2,1)S(1)}) custom-call(f32[1,256]{1,0:T(1,128)S(1)} %bitcast.6, f32[16,1024]{1,0:T(8,128)S(1)} %copy-done.3, bf16[768,2,1024]{2,1,0:T(2,128)(2,1)S(1)} %bitcast.4), custom_call_target="tpu_custom_call" | custom-call | flops 1073741824 | bytes 6291456 | tf_op jit(solution)/shard_map/pallas_call | solution.py:207
  9.5 3.1 %collective-permute-start.1 = (bf16[128,1024]{1,0:T(8,128)(2,1)S(1)}, bf16[128,1024]{1,0:T(8,128)(2,1)S(1)}, u32[]{:S(2)}, u32[]{:S(2)}) collective-permute-start(bf16[128,1024]{1,0:T(8,128)(2,1)S(1)} %get-tuple-element.23), channel_id=1, source_target_pairs={{0,8},{1,9},{2,10},{3,11},{4,12},{5,13},{6,14},{7,15},{8,16},{9,17... | collective-permute-start | bytes 786440 | tf_op jit(solution)/shard_map/ppermute | solution.py:38
  12.7 4.4 %collective-permute-start.2 = (bf16[128,1024]{1,0:T(8,128)(2,1)S(1)}, bf16[128,1024]{1,0:T(8,128)(2,1)S(1)}, u32[]{:S(2)}, u32[]{:S(2)}) collective-permute-start(bf16[128,1024]{1,0:T(8,128)(2,1)S(1)} %get-tuple-element.24), channel_id=1, source_target_pairs={{0,16},{1,17},{2,18},{3,19},{4,20},{5,21},{6,22},{7,23},{8,24},{9,... | collective-permute-start | bytes 786440 | tf_op jit(solution)/shard_map/ppermute | solution.py:38
  17.0 3.1 %collective-permute-start.3 = (bf16[128,1024]{1,0:T(8,128)(2,1)S(1)}, bf16[128,1024]{1,0:T(8,128)(2,1)S(1)}, u32[]{:S(2)}, u32[]{:S(2)}) collective-permute-start(bf16[128,1024]{1,0:T(8,128)(2,1)S(1)} %get-tuple-element.25), channel_id=1, source_target_pairs={{0,24},{1,25},{2,26},{3,27},{4,28},{5,29},{6,30},{7,31},{8,0},{9,1... | collective-permute-start | bytes 786440 | tf_op jit(solution)/shard_map/ppermute | solution.py:38
  20.1 0.7 collective-permute-start.8
  20.8 0.0 collective-permute-done.1
  20.8 4.5 %collective-permute-done.2 = bf16[128,1024]{1,0:T(8,128)(2,1)S(1)} collective-permute-done((bf16[128,1024]{1,0:T(8,128)(2,1)S(1)}, bf16[128,1024]{1,0:T(8,128)(2,1)S(1)}, u32[]{:S(2)}, u32[]{:S(2)}) %collective-permute-start.2) | collective-permute-done | bytes 262176 | tf_op jit(solution)/shard_map/ppermute | solution.py:38
  25.3 2.7 %collective-permute-done.3 = bf16[128,1024]{1,0:T(8,128)(2,1)S(1)} collective-permute-done((bf16[128,1024]{1,0:T(8,128)(2,1)S(1)}, bf16[128,1024]{1,0:T(8,128)(2,1)S(1)}, u32[]{:S(2)}, u32[]{:S(2)}) %collective-permute-start.3) | collective-permute-done | bytes 262176 | tf_op jit(solution)/shard_map/ppermute | solution.py:38
  28.1 0.0 collective-permute-done.halo_ref
  28.3 3.5 %collective-permute-start.4 = (bf16[256,1024]{1,0:T(8,128)(2,1)S(1)}, bf16[256,1024]{1,0:T(8,128)(2,1)S(1)}, u32[]{:S(2)}, u32[]{:S(2)}) collective-permute-start(bf16[256,1024]{1,0:T(8,128)(2,1)S(1)} %pad_maximum_fusion), channel_id=1, source_target_pairs={{0,2},{1,3},{2,0},{3,1},{4,6},{5,7},{6,4},{7,5},{8,10},{9,11},{10,... | collective-permute-start | bytes 1572872 | tf_op jit(solution)/shard_map/ppermute | solution.py:38
  31.8 3.7 %collective-permute-start.6 = (bf16[256,1024]{1,0:T(8,128)(2,1)S(1)}, bf16[256,1024]{1,0:T(8,128)(2,1)S(1)}, u32[]{:S(2)}, u32[]{:S(2)}) collective-permute-start(bf16[256,1024]{1,0:T(8,128)(2,1)S(1)} %pad_maximum_fusion.1), channel_id=1, source_target_pairs={{0,4},{1,5},{2,6},{3,7},{4,0},{5,1},{6,2},{7,3},{8,12},{9,13},{10,... | collective-permute-start | bytes 1572872 | tf_op jit(solution)/shard_map/ppermute | solution.py:38
  35.5 0.0 collective-permute-done.8.wrap_ref
  35.5 0.8 shard_map.40
  36.4 4.4 %collective-permute-start.9 = (bf16[64,1024]{1,0:T(8,128)(2,1)S(1)}, bf16[64,1024]{1,0:T(8,128)(2,1)S(1)}, u32[]{:S(2)}, u32[]{:S(2)}) collective-permute-start(bf16[64,1024]{1,0:T(8,128)(2,1)S(1)} %get-tuple-element.33), channel_id=1, source_target_pairs={{0,8},{1,9},{2,10},{3,11},{4,12},{5,13},{6,14},{7,15},{8,16},{9,17... | collective-permute-start | bytes 393224 | tf_op jit(solution)/shard_map/ppermute | solution.py:38
  40.8 3.0 %collective-permute-start.10 = (bf16[64,1024]{1,0:T(8,128)(2,1)S(1)}, bf16[64,1024]{1,0:T(8,128)(2,1)S(1)}, u32[]{:S(2)}, u32[]{:S(2)}) collective-permute-start(bf16[64,1024]{1,0:T(8,128)(2,1)S(1)} %get-tuple-element.34), channel_id=1, source_target_pairs={{0,16},{1,17},{2,18},{3,19},{4,20},{5,21},{6,22},{7,23},{8,24},{9,... | collective-permute-start | bytes 393224 | tf_op jit(solution)/shard_map/ppermute | solution.py:38
  43.8 3.2 %collective-permute-start.11 = (bf16[64,1024]{1,0:T(8,128)(2,1)S(1)}, bf16[64,1024]{1,0:T(8,128)(2,1)S(1)}, u32[]{:S(2)}, u32[]{:S(2)}) collective-permute-start(bf16[64,1024]{1,0:T(8,128)(2,1)S(1)} %get-tuple-element.35), channel_id=1, source_target_pairs={{0,24},{1,25},{2,26},{3,27},{4,28},{5,29},{6,30},{7,31},{8,0},{9,1... | collective-permute-start | bytes 393224 | tf_op jit(solution)/shard_map/ppermute | solution.py:38
  47.0 13.3 %collective-permute-done.4 = bf16[256,1024]{1,0:T(8,128)(2,1)S(1)} collective-permute-done((bf16[256,1024]{1,0:T(8,128)(2,1)S(1)}, bf16[256,1024]{1,0:T(8,128)(2,1)S(1)}, u32[]{:S(2)}, u32[]{:S(2)}) %collective-permute-start.4) | collective-permute-done | bytes 524320 | tf_op jit(solution)/shard_map/ppermute | solution.py:38
  60.4 2.4 %collective-permute-start.5 = (bf16[512,1024]{1,0:T(8,128)(2,1)S(1)}, bf16[512,1024]{1,0:T(8,128)(2,1)S(1)}, u32[]{:S(2)}, u32[]{:S(2)}) collective-permute-start(bf16[512,1024]{1,0:T(8,128)(2,1)S(1)} %constant_dynamic-update-slice_fusion.refs_0_), channel_id=1, source_target_pairs={{0,1},{1,0},{2,3},{3,2},{4,5},{5,4},{6,7},{7,6},{8,9},{9,8},{10,11... | collective-permute-start | bytes 3145736 | tf_op jit(solution)/shard_map/ppermute | solution.py:38
  62.8 0.0 collective-permute-done.6
  62.8 0.0 collective-permute-done.9
  62.9 0.0 collective-permute-done.10
  62.9 0.0 collective-permute-done.11
  63.0 1.9 %collective-permute-start.12 = (bf16[128,1024]{1,0:T(8,128)(2,1)S(1)}, bf16[128,1024]{1,0:T(8,128)(2,1)S(1)}, u32[]{:S(2)}, u32[]{:S(2)}) collective-permute-start(bf16[128,1024]{1,0:T(8,128)(2,1)S(1)} %pad_maximum_fusion.2), channel_id=1, source_target_pairs={{0,4},{1,5},{2,6},{3,7},{4,0},{5,1},{6,2},{7,3},{8,12},{9,13},{10,... | collective-permute-start | bytes 786440 | tf_op jit(solution)/shard_map/ppermute | solution.py:38
  64.9 2.0 %collective-permute-start.7 = (bf16[256,1024]{1,0:T(8,128)(2,1)S(1)}, bf16[256,1024]{1,0:T(8,128)(2,1)S(1)}, u32[]{:S(2)}, u32[]{:S(2)}) collective-permute-start(bf16[256,1024]{1,0:T(8,128)(2,1)S(1)} %collective-permute-done.6), channel_id=1, source_target_pairs={{0,2},{1,3},{2,0},{3,1},{4,6},{5,7},{6,4},{7,5},{8,10},{9,11},{10,... | collective-permute-start | bytes 1572872 | tf_op jit(solution)/shard_map/ppermute | solution.py:38
  66.9 11.7 %collective-permute-done.12 = bf16[128,1024]{1,0:T(8,128)(2,1)S(1)} collective-permute-done((bf16[128,1024]{1,0:T(8,128)(2,1)S(1)}, bf16[128,1024]{1,0:T(8,128)(2,1)S(1)}, u32[]{:S(2)}, u32[]{:S(2)}) %collective-permute-start.12) | collective-permute-done | bytes 262176 | tf_op jit(solution)/shard_map/ppermute | solution.py:38
  78.7 0.1 constant_dynamic-update-slice_fusion.8
  78.8 1.9 %collective-permute-start.13 = (bf16[256,1024]{1,0:T(8,128)(2,1)S(1)}, bf16[256,1024]{1,0:T(8,128)(2,1)S(1)}, u32[]{:S(2)}, u32[]{:S(2)}) collective-permute-start(bf16[256,1024]{1,0:T(8,128)(2,1)S(1)} %get-tuple-element.40), channel_id=1, source_target_pairs={{0,2},{1,3},{2,0},{3,1},{4,6},{5,7},{6,4},{7,5},{8,10},{9,11},{10,... | collective-permute-start | bytes 1572872 | tf_op jit(solution)/shard_map/ppermute | solution.py:38
  80.7 2.4 %collective-permute-start.15 = (bf16[512,1024]{1,0:T(8,128)(2,1)S(1)}, bf16[512,1024]{1,0:T(8,128)(2,1)S(1)}, u32[]{:S(2)}, u32[]{:S(2)}) collective-permute-start(bf16[512,1024]{1,0:T(8,128)(2,1)S(1)} %get-tuple-element.39.refs_0_), channel_id=1, source_target_pairs={{0,1},{1,0},{2,3},{3,2},{4,5},{5,4},{6,7},{7,6},{8,9},{9,8},{10,11... | collective-permute-start | bytes 3145736 | tf_op jit(solution)/shard_map/ppermute | solution.py:38
  83.1 0.0 collective-permute-done.5.refs_1_
  83.1 2.0 %shard_map.39.refs_2_ = f32[2,1024,256]{2,1,0:T(8,128)S(1)} custom-call(bf16[512,1024]{1,0:T(8,128)(2,1)S(1)} %constant_dynamic-update-slice_fusion.refs_0_, bf16[512,1024]{1,0:T(8,128)(2,1)S(1)} %collective-permute-done.5.refs_1_), custom_call_target="tpu_custom_call" | custom-call | flops 1073741824 | bytes 4194304 | tf_op jit(solution)/shard_map/pallas_call | solution.py:173
  85.2 0.7 collective-permute-done.7
  85.9 11.2 %collective-permute-done.13 = bf16[256,1024]{1,0:T(8,128)(2,1)S(1)} collective-permute-done((bf16[256,1024]{1,0:T(8,128)(2,1)S(1)}, bf16[256,1024]{1,0:T(8,128)(2,1)S(1)}, u32[]{:S(2)}, u32[]{:S(2)}) %collective-permute-start.13) | collective-permute-done | bytes 524320 | tf_op jit(solution)/shard_map/ppermute | solution.py:38
  97.2 2.7 %collective-permute-start.14 = (bf16[512,1024]{1,0:T(8,128)(2,1)S(1)}, bf16[512,1024]{1,0:T(8,128)(2,1)S(1)}, u32[]{:S(2)}, u32[]{:S(2)}) collective-permute-start(bf16[512,1024]{1,0:T(8,128)(2,1)S(1)} %constant_dynamic-update-slice_fusion.6.refs_0_), channel_id=1, source_target_pairs={{0,1},{1,0},{2,3},{3,2},{4,5},{5,4},{6,7},{7,6},{8,9},{9,8},{10,11... | collective-permute-start | bytes 3145736 | tf_op jit(solution)/shard_map/ppermute | solution.py:38
  99.9 0.0 collective-permute-done.15.refs_1_
  99.9 2.3 %shard_map.41.refs_2_ = f32[2,1024,256]{2,1,0:T(8,128)S(1)} custom-call(bf16[512,1024]{1,0:T(8,128)(2,1)S(1)} %get-tuple-element.39.refs_0_, bf16[512,1024]{1,0:T(8,128)(2,1)S(1)} %collective-permute-done.15.refs_1_, f32[2,1024,256]{2,1,0:T(8,128)S(1)} %shard_map.39.refs_2_), custom_call_target="tpu_custom_call" | custom-call | flops 1073741824 | bytes 4194304 | tf_op jit(solution)/shard_map/pallas_call | solution.py:173
  102.2 0.0 collective-permute-done.14.refs_1_
  102.2 3.2 %shard_map.42 = f32[2,1024,256]{2,1,0:T(8,128)} custom-call(bf16[512,1024]{1,0:T(8,128)(2,1)S(1)} %constant_dynamic-update-slice_fusion.6.refs_0_, bf16[512,1024]{1,0:T(8,128)(2,1)S(1)} %collective-permute-done.14.refs_1_, f32[2,1024,256]{2,1,0:T(8,128)S(1)} %shard_map.41.refs_2_), custom_call_target="tpu_custom_call" | custom-call | flops 1073741824 | bytes 4194304 | tf_op jit(solution)/shard_map/pallas_call | solution.py:173
  (15 shorter events, 0.4 us)
Async XLA Ops:
  0.0 7.8 %copy-start.2 = (f32[256]{0:T(256)S(1)}, f32[256]{0:T(256)}, u32[]{:S(2)}) copy-start(f32[256]{0:T(256)} %param.4) | copy-start | bytes 3076
  0.0 1.9 %copy-start = (bf16[768,2,1,1024]{3,1,2,0:T(2,128)(2,1)S(1)}, bf16[768,2,1,1024]{3,1,2,0:T(2,128)(2,1)}, u32[]{:S(2)}) copy-start(bf16[768,2,1,1024]{3,1,2,0:T(2,128)(2,1)} %param.3) | copy-start | bytes 9437188
  1.9 5.9 %copy-start.1 = (bf16[768,2,1,1024]{3,1,2,0:T(2,128)(2,1)S(1)}, bf16[768,2,1,1024]{3,1,2,0:T(2,128)(2,1)}, u32[]{:S(2)}) copy-start(bf16[768,2,1,1024]{3,1,2,0:T(2,128)(2,1)} %param.3) | copy-start | bytes 9437188
  1.9 5.9 %copy-start.3 = (f32[16,1024]{1,0:T(8,128)S(1)}, f32[16,1024]{1,0:T(8,128)}, u32[]{:S(2)}) copy-start(f32[16,1024]{1,0:T(8,128)} %constant.2.clone.trig_ref) | copy-start | bytes 196612
  2.2 25.8 %collective-permute-start = (bf16[240,2,1024]{2,1,0:T(2,128)(2,1)S(1)}, bf16[240,2,1024]{2,1,0:T(2,128)(2,1)S(1)}, u32[]{:S(2)}, u32[]{:S(2)}) collective-permute-start(bf16[240,2,1024]{2,1,0:T(2,128)(2,1)S(1)} %shard_map.37), channel_id=1, source_target_pairs={{0,1},{1,2},{2,3},{3,4},{4,5},{5,6},{6,7},{8,9},{9,10},{10,11},{11... | collective-permute-start | bytes 2949128 | tf_op jit(solution)/shard_map/ppermute | solution.py:62
  9.5 11.3 %collective-permute-start.1 = (bf16[128,1024]{1,0:T(8,128)(2,1)S(1)}, bf16[128,1024]{1,0:T(8,128)(2,1)S(1)}, u32[]{:S(2)}, u32[]{:S(2)}) collective-permute-start(bf16[128,1024]{1,0:T(8,128)(2,1)S(1)} %get-tuple-element.23), channel_id=1, source_target_pairs={{0,8},{1,9},{2,10},{3,11},{4,12},{5,13},{6,14},{7,15},{8,16},{9,17... | collective-permute-start | bytes 786440 | tf_op jit(solution)/shard_map/ppermute | solution.py:38
  12.7 12.7 %collective-permute-start.2 = (bf16[128,1024]{1,0:T(8,128)(2,1)S(1)}, bf16[128,1024]{1,0:T(8,128)(2,1)S(1)}, u32[]{:S(2)}, u32[]{:S(2)}) collective-permute-start(bf16[128,1024]{1,0:T(8,128)(2,1)S(1)} %get-tuple-element.24), channel_id=1, source_target_pairs={{0,16},{1,17},{2,18},{3,19},{4,20},{5,21},{6,22},{7,23},{8,24},{9,... | collective-permute-start | bytes 786440 | tf_op jit(solution)/shard_map/ppermute | solution.py:38
  17.0 11.0 %collective-permute-start.3 = (bf16[128,1024]{1,0:T(8,128)(2,1)S(1)}, bf16[128,1024]{1,0:T(8,128)(2,1)S(1)}, u32[]{:S(2)}, u32[]{:S(2)}) collective-permute-start(bf16[128,1024]{1,0:T(8,128)(2,1)S(1)} %get-tuple-element.25), channel_id=1, source_target_pairs={{0,24},{1,25},{2,26},{3,27},{4,28},{5,29},{6,30},{7,31},{8,0},{9,1... | collective-permute-start | bytes 786440 | tf_op jit(solution)/shard_map/ppermute | solution.py:38
  20.1 15.4 %collective-permute-start.8 = (bf16[240,2,1024]{2,1,0:T(2,128)(2,1)S(1)}, bf16[240,2,1024]{2,1,0:T(2,128)(2,1)S(1)}, u32[]{:S(2)}, u32[]{:S(2)}) collective-permute-start(bf16[240,2,1024]{2,1,0:T(2,128)(2,1)S(1)} %shard_map.37), channel_id=1, source_target_pairs={{7,8},{15,16},{23,24},{39,40},{47,48},{55,56},{71,72},{79,80},{87,... | collective-permute-start | bytes 2949128 | tf_op jit(solution)/shard_map/ppermute | solution.py:62
  28.3 32.0 %collective-permute-start.4 = (bf16[256,1024]{1,0:T(8,128)(2,1)S(1)}, bf16[256,1024]{1,0:T(8,128)(2,1)S(1)}, u32[]{:S(2)}, u32[]{:S(2)}) collective-permute-start(bf16[256,1024]{1,0:T(8,128)(2,1)S(1)} %pad_maximum_fusion), channel_id=1, source_target_pairs={{0,2},{1,3},{2,0},{3,1},{4,6},{5,7},{6,4},{7,5},{8,10},{9,11},{10,... | collective-permute-start | bytes 1572872 | tf_op jit(solution)/shard_map/ppermute | solution.py:38
  31.8 31.0 %collective-permute-start.6 = (bf16[256,1024]{1,0:T(8,128)(2,1)S(1)}, bf16[256,1024]{1,0:T(8,128)(2,1)S(1)}, u32[]{:S(2)}, u32[]{:S(2)}) collective-permute-start(bf16[256,1024]{1,0:T(8,128)(2,1)S(1)} %pad_maximum_fusion.1), channel_id=1, source_target_pairs={{0,4},{1,5},{2,6},{3,7},{4,0},{5,1},{6,2},{7,3},{8,12},{9,13},{10,... | collective-permute-start | bytes 1572872 | tf_op jit(solution)/shard_map/ppermute | solution.py:38
  36.4 26.5 %collective-permute-start.9 = (bf16[64,1024]{1,0:T(8,128)(2,1)S(1)}, bf16[64,1024]{1,0:T(8,128)(2,1)S(1)}, u32[]{:S(2)}, u32[]{:S(2)}) collective-permute-start(bf16[64,1024]{1,0:T(8,128)(2,1)S(1)} %get-tuple-element.33), channel_id=1, source_target_pairs={{0,8},{1,9},{2,10},{3,11},{4,12},{5,13},{6,14},{7,15},{8,16},{9,17... | collective-permute-start | bytes 393224 | tf_op jit(solution)/shard_map/ppermute | solution.py:38
  40.8 22.1 %collective-permute-start.10 = (bf16[64,1024]{1,0:T(8,128)(2,1)S(1)}, bf16[64,1024]{1,0:T(8,128)(2,1)S(1)}, u32[]{:S(2)}, u32[]{:S(2)}) collective-permute-start(bf16[64,1024]{1,0:T(8,128)(2,1)S(1)} %get-tuple-element.34), channel_id=1, source_target_pairs={{0,16},{1,17},{2,18},{3,19},{4,20},{5,21},{6,22},{7,23},{8,24},{9,... | collective-permute-start | bytes 393224 | tf_op jit(solution)/shard_map/ppermute | solution.py:38
  43.8 19.1 %collective-permute-start.11 = (bf16[64,1024]{1,0:T(8,128)(2,1)S(1)}, bf16[64,1024]{1,0:T(8,128)(2,1)S(1)}, u32[]{:S(2)}, u32[]{:S(2)}) collective-permute-start(bf16[64,1024]{1,0:T(8,128)(2,1)S(1)} %get-tuple-element.35), channel_id=1, source_target_pairs={{0,24},{1,25},{2,26},{3,27},{4,28},{5,29},{6,30},{7,31},{8,0},{9,1... | collective-permute-start | bytes 393224 | tf_op jit(solution)/shard_map/ppermute | solution.py:38
  60.4 22.7 %collective-permute-start.5 = (bf16[512,1024]{1,0:T(8,128)(2,1)S(1)}, bf16[512,1024]{1,0:T(8,128)(2,1)S(1)}, u32[]{:S(2)}, u32[]{:S(2)}) collective-permute-start(bf16[512,1024]{1,0:T(8,128)(2,1)S(1)} %constant_dynamic-update-slice_fusion.refs_0_), channel_id=1, source_target_pairs={{0,1},{1,0},{2,3},{3,2},{4,5},{5,4},{6,7},{7,6},{8,9},{9,8},{10,11... | collective-permute-start | bytes 3145736 | tf_op jit(solution)/shard_map/ppermute | solution.py:38
  63.0 15.7 %collective-permute-start.12 = (bf16[128,1024]{1,0:T(8,128)(2,1)S(1)}, bf16[128,1024]{1,0:T(8,128)(2,1)S(1)}, u32[]{:S(2)}, u32[]{:S(2)}) collective-permute-start(bf16[128,1024]{1,0:T(8,128)(2,1)S(1)} %pad_maximum_fusion.2), channel_id=1, source_target_pairs={{0,4},{1,5},{2,6},{3,7},{4,0},{5,1},{6,2},{7,3},{8,12},{9,13},{10,... | collective-permute-start | bytes 786440 | tf_op jit(solution)/shard_map/ppermute | solution.py:38
  64.9 21.0 %collective-permute-start.7 = (bf16[256,1024]{1,0:T(8,128)(2,1)S(1)}, bf16[256,1024]{1,0:T(8,128)(2,1)S(1)}, u32[]{:S(2)}, u32[]{:S(2)}) collective-permute-start(bf16[256,1024]{1,0:T(8,128)(2,1)S(1)} %collective-permute-done.6), channel_id=1, source_target_pairs={{0,2},{1,3},{2,0},{3,1},{4,6},{5,7},{6,4},{7,5},{8,10},{9,11},{10,... | collective-permute-start | bytes 1572872 | tf_op jit(solution)/shard_map/ppermute | solution.py:38
  78.8 18.3 %collective-permute-start.13 = (bf16[256,1024]{1,0:T(8,128)(2,1)S(1)}, bf16[256,1024]{1,0:T(8,128)(2,1)S(1)}, u32[]{:S(2)}, u32[]{:S(2)}) collective-permute-start(bf16[256,1024]{1,0:T(8,128)(2,1)S(1)} %get-tuple-element.40), channel_id=1, source_target_pairs={{0,2},{1,3},{2,0},{3,1},{4,6},{5,7},{6,4},{7,5},{8,10},{9,11},{10,... | collective-permute-start | bytes 1572872 | tf_op jit(solution)/shard_map/ppermute | solution.py:38
  80.7 19.2 %collective-permute-start.15 = (bf16[512,1024]{1,0:T(8,128)(2,1)S(1)}, bf16[512,1024]{1,0:T(8,128)(2,1)S(1)}, u32[]{:S(2)}, u32[]{:S(2)}) collective-permute-start(bf16[512,1024]{1,0:T(8,128)(2,1)S(1)} %get-tuple-element.39.refs_0_), channel_id=1, source_target_pairs={{0,1},{1,0},{2,3},{3,2},{4,5},{5,4},{6,7},{7,6},{8,9},{9,8},{10,11... | collective-permute-start | bytes 3145736 | tf_op jit(solution)/shard_map/ppermute | solution.py:38
  97.2 5.0 %collective-permute-start.14 = (bf16[512,1024]{1,0:T(8,128)(2,1)S(1)}, bf16[512,1024]{1,0:T(8,128)(2,1)S(1)}, u32[]{:S(2)}, u32[]{:S(2)}) collective-permute-start(bf16[512,1024]{1,0:T(8,128)(2,1)S(1)} %constant_dynamic-update-slice_fusion.6.refs_0_), channel_id=1, source_target_pairs={{0,1},{1,0},{2,3},{3,2},{4,5},{5,4},{6,7},{7,6},{8,9},{9,8},{10,11... | collective-permute-start | bytes 3145736 | tf_op jit(solution)/shard_map/ppermute | solution.py:38

commit v8 on v7

--- a/solution.py
+++ b/solution.py
@@ -226,18 +226,18 @@
     ma = part(late_all, 0)
     ma_near = move(ma, near_z)
     first_all = spread(first_out)
+    mb = part(first_all, 0)
     tb = move(part(first_all, 1), far_z)
     ta_near = move(ta, near_z)
-    b_own = jnp.concatenate([part(first_all, 0), tb], 0)
-    b_near = move(b_own, near_z)
+    b_near = move(jnp.concatenate([mb, tb], 0), near_z)
     ma = jnp.concatenate([ma, ma_near], 0)
     acc = correlate([ma, move(ma, other_core)], None)
-    acc, ta_near, b_near = lax.optimization_barrier((acc, ta_near, b_near))
-    near = jnp.concatenate([ta_near, b_near], 0)
-    near_core = move(near, other_core)
-    own = jnp.concatenate([ta, b_own], 0)
-    acc = correlate([own, move(own, other_core)], acc)
-    pieces = [near, near_core]
+    own = jnp.concatenate([ta, mb], 0)
+    acc = correlate([own, move(own, other_core), ta_near], acc)
+    ta_core = move(ta_near, other_core)
+    acc, b_near, ta_core = lax.optimization_barrier((acc, b_near, ta_core))
+    last = jnp.concatenate([b_near, tb], 0)
+    pieces = [ta_core, last, move(last, other_core)]
     frames = samples_here // FINE * XS * ZS * CORES
     return correlate(pieces, acc, 1.0 / frames)[None]
 

time: 106 us -> 106 us (level)
  waiting for transfers between devices: 44.2 us -> 39 us
  starting transfers between devices: 48 us -> 52.9 us
    ppermute x14 -> x15, waiting for transfers between devices: 44.2 us -> 39 us  [move(): return lax.ppermute(array, 'tm', moves(rule))]
    ppermute x14 -> x15, starting transfers between devices: 41.7 us -> 46.7 us  [move(): return lax.ppermute(array, 'tm', moves(rule))]
  transfers between devices with their start and end apart: 16 -> 17, of which waited for: 6 -> 6; matrix products, arithmetic and copies ran while one was open for 0% -> 0% of each run, Pallas kernels for 7% -> 7%
where the time goes in v8:
time: 106 us; the launch traced here: 105 us
  starting transfers between devices  52.9 us (50%)
  waiting for transfers between devices  39 us (37%)
  Pallas kernels  10.7 us (10%)
  local copies, waits for them, and re-layouts  2.23 us (2%)
    ppermute x15, starting transfers between devices, move(): return lax.ppermute(array, 'tm', moves(rule))  46.7 us
    ppermute x15, waiting for transfers between devices, move(): return lax.ppermute(array, 'tm', moves(rule))  39 us
    pallas_call x3, Pallas kernels, correlate(): pl.pallas_call(functools.partial(products, len(pieces), scale), grid=(4,)...  7.82 us
    ppermute x2, starting transfers between devices, halo_of(): return (lax.ppermute(tail, 'tm', inside), lax.ppermute(tail, 'tm', across))  6.25 us
  transfers between devices with their start and end apart: 17, of which 6 were waited for; matrix products, arithmetic and copies ran while one was open for 0% of the time, Pallas kernels for 7%

profile of v8, /device:TPU:1, one launch (start us, length us, event | category | flops | bytes accessed | tf_op | source)
XLA Modules:
  0.0 105.3 jit_solution(6250270833298032080)
XLA Ops:
  0.0 0.0 copy-start.2
  0.0 0.0 copy-start
  0.0 1.9 %copy-done = bf16[768,2,1,1024]{3,1,2,0:T(2,128)(2,1)S(1)} copy-done((bf16[768,2,1,1024]{3,1,2,0:T(2,128)(2,1)S(1)}, bf16[768,2,1,1024]{3,1,2,0:T(2,128)(2,1)}, u32[]{:S(2)}) %copy-start) | copy-done | bytes 3145752
  1.9 0.0 copy-start.1
  1.9 0.0 copy-start.3
  1.9 0.3 shard_map.37
  2.2 5.5 %collective-permute-start = (bf16[240,2,1024]{2,1,0:T(2,128)(2,1)S(1)}, bf16[240,2,1024]{2,1,0:T(2,128)(2,1)S(1)}, u32[]{:S(2)}, u32[]{:S(2)}) collective-permute-start(bf16[240,2,1024]{2,1,0:T(2,128)(2,1)S(1)} %shard_map.37), channel_id=1, source_target_pairs={{0,1},{1,2},{2,3},{3,4},{4,5},{5,6},{6,7},{8,9},{9,10},{10,11},{11... | collective-permute-start | bytes 2949128 | tf_op jit(solution)/shard_map/ppermute | solution.py:62
  7.8 0.0 copy-done.2
  7.8 0.0 copy-done.1
  7.8 0.0 copy-done.3
  7.8 1.7 %shard_map.38 = (bf16[256,1024]{1,0:T(8,128)(2,1)S(1)}, bf16[128,1024]{1,0:T(8,128)(2,1)S(1)}, bf16[128,1024]{1,0:T(8,128)(2,1)S(1)}, bf16[128,1024]{1,0:T(8,128)(2,1)S(1)}, bf16[128,1024]{1,0:T(8,128)(2,1)S(1)}) custom-call(f32[1,256]{1,0:T(1,128)S(1)} %bitcast.6, f32[16,1024]{1,0:T(8,128)S(1)} %copy-done.3, bf16[768,2,1024]{2,1,0:T(2,128)(2,1)S(1)} %bitcast.4), custom_call_target="tpu_custom_call" | custom-call | flops 1073741824 | bytes 6291456 | tf_op jit(solution)/shard_map/pallas_call | solution.py:207
  9.5 3.1 %collective-permute-start.1 = (bf16[128,1024]{1,0:T(8,128)(2,1)S(1)}, bf16[128,1024]{1,0:T(8,128)(2,1)S(1)}, u32[]{:S(2)}, u32[]{:S(2)}) collective-permute-start(bf16[128,1024]{1,0:T(8,128)(2,1)S(1)} %get-tuple-element.23), channel_id=1, source_target_pairs={{0,8},{1,9},{2,10},{3,11},{4,12},{5,13},{6,14},{7,15},{8,16},{9,17... | collective-permute-start | bytes 786440 | tf_op jit(solution)/shard_map/ppermute | solution.py:38
  12.7 4.4 %collective-permute-start.2 = (bf16[128,1024]{1,0:T(8,128)(2,1)S(1)}, bf16[128,1024]{1,0:T(8,128)(2,1)S(1)}, u32[]{:S(2)}, u32[]{:S(2)}) collective-permute-start(bf16[128,1024]{1,0:T(8,128)(2,1)S(1)} %get-tuple-element.24), channel_id=1, source_target_pairs={{0,16},{1,17},{2,18},{3,19},{4,20},{5,21},{6,22},{7,23},{8,24},{9,... | collective-permute-start | bytes 786440 | tf_op jit(solution)/shard_map/ppermute | solution.py:38
  17.0 3.1 %collective-permute-start.3 = (bf16[128,1024]{1,0:T(8,128)(2,1)S(1)}, bf16[128,1024]{1,0:T(8,128)(2,1)S(1)}, u32[]{:S(2)}, u32[]{:S(2)}) collective-permute-start(bf16[128,1024]{1,0:T(8,128)(2,1)S(1)} %get-tuple-element.25), channel_id=1, source_target_pairs={{0,24},{1,25},{2,26},{3,27},{4,28},{5,29},{6,30},{7,31},{8,0},{9,1... | collective-permute-start | bytes 786440 | tf_op jit(solution)/shard_map/ppermute | solution.py:38
  20.1 0.7 collective-permute-start.5
  20.8 0.0 collective-permute-done.1
  20.8 4.5 %collective-permute-done.2 = bf16[128,1024]{1,0:T(8,128)(2,1)S(1)} collective-permute-done((bf16[128,1024]{1,0:T(8,128)(2,1)S(1)}, bf16[128,1024]{1,0:T(8,128)(2,1)S(1)}, u32[]{:S(2)}, u32[]{:S(2)}) %collective-permute-start.2) | collective-permute-done | bytes 262176 | tf_op jit(solution)/shard_map/ppermute | solution.py:38
  25.3 2.7 %collective-permute-done.3 = bf16[128,1024]{1,0:T(8,128)(2,1)S(1)} collective-permute-done((bf16[128,1024]{1,0:T(8,128)(2,1)S(1)}, bf16[128,1024]{1,0:T(8,128)(2,1)S(1)}, u32[]{:S(2)}, u32[]{:S(2)}) %collective-permute-start.3) | collective-permute-done | bytes 262176 | tf_op jit(solution)/shard_map/ppermute | solution.py:38
  28.1 0.0 collective-permute-done.halo_ref
  28.3 3.5 %collective-permute-start.11 = (bf16[256,1024]{1,0:T(8,128)(2,1)S(1)}, bf16[256,1024]{1,0:T(8,128)(2,1)S(1)}, u32[]{:S(2)}, u32[]{:S(2)}) collective-permute-start(bf16[256,1024]{1,0:T(8,128)(2,1)S(1)} %pad_maximum_fusion.1), channel_id=1, source_target_pairs={{0,2},{1,3},{2,0},{3,1},{4,6},{5,7},{6,4},{7,5},{8,10},{9,11},{10,... | collective-permute-start | bytes 1572872 | tf_op jit(solution)/shard_map/ppermute | solution.py:38
  31.8 3.7 %collective-permute-start.4 = (bf16[256,1024]{1,0:T(8,128)(2,1)S(1)}, bf16[256,1024]{1,0:T(8,128)(2,1)S(1)}, u32[]{:S(2)}, u32[]{:S(2)}) collective-permute-start(bf16[256,1024]{1,0:T(8,128)(2,1)S(1)} %pad_maximum_fusion), channel_id=1, source_target_pairs={{0,4},{1,5},{2,6},{3,7},{4,0},{5,1},{6,2},{7,3},{8,12},{9,13},{10,... | collective-permute-start | bytes 1572872 | tf_op jit(solution)/shard_map/ppermute | solution.py:38
  35.5 0.0 collective-permute-done.5.wrap_ref
  35.5 0.8 shard_map.39
  36.4 4.4 %collective-permute-start.6 = (bf16[64,1024]{1,0:T(8,128)(2,1)S(1)}, bf16[64,1024]{1,0:T(8,128)(2,1)S(1)}, u32[]{:S(2)}, u32[]{:S(2)}) collective-permute-start(bf16[64,1024]{1,0:T(8,128)(2,1)S(1)} %get-tuple-element.33), channel_id=1, source_target_pairs={{0,8},{1,9},{2,10},{3,11},{4,12},{5,13},{6,14},{7,15},{8,16},{9,17... | collective-permute-start | bytes 393224 | tf_op jit(solution)/shard_map/ppermute | solution.py:38
  40.8 3.0 %collective-permute-start.7 = (bf16[64,1024]{1,0:T(8,128)(2,1)S(1)}, bf16[64,1024]{1,0:T(8,128)(2,1)S(1)}, u32[]{:S(2)}, u32[]{:S(2)}) collective-permute-start(bf16[64,1024]{1,0:T(8,128)(2,1)S(1)} %get-tuple-element.34), channel_id=1, source_target_pairs={{0,16},{1,17},{2,18},{3,19},{4,20},{5,21},{6,22},{7,23},{8,24},{9,... | collective-permute-start | bytes 393224 | tf_op jit(solution)/shard_map/ppermute | solution.py:38
  43.8 3.2 %collective-permute-start.8 = (bf16[64,1024]{1,0:T(8,128)(2,1)S(1)}, bf16[64,1024]{1,0:T(8,128)(2,1)S(1)}, u32[]{:S(2)}, u32[]{:S(2)}) collective-permute-start(bf16[64,1024]{1,0:T(8,128)(2,1)S(1)} %get-tuple-element.35), channel_id=1, source_target_pairs={{0,24},{1,25},{2,26},{3,27},{4,28},{5,29},{6,30},{7,31},{8,0},{9,1... | collective-permute-start | bytes 393224 | tf_op jit(solution)/shard_map/ppermute | solution.py:38
  47.0 13.3 %collective-permute-done.11 = bf16[256,1024]{1,0:T(8,128)(2,1)S(1)} collective-permute-done((bf16[256,1024]{1,0:T(8,128)(2,1)S(1)}, bf16[256,1024]{1,0:T(8,128)(2,1)S(1)}, u32[]{:S(2)}, u32[]{:S(2)}) %collective-permute-start.11) | collective-permute-done | bytes 524320 | tf_op jit(solution)/shard_map/ppermute | solution.py:38
  60.4 2.4 %collective-permute-start.12 = (bf16[512,1024]{1,0:T(8,128)(2,1)S(1)}, bf16[512,1024]{1,0:T(8,128)(2,1)S(1)}, u32[]{:S(2)}, u32[]{:S(2)}) collective-permute-start(bf16[512,1024]{1,0:T(8,128)(2,1)S(1)} %constant_dynamic-update-slice_fusion.1.refs_0_), channel_id=1, source_target_pairs={{0,1},{1,0},{2,3},{3,2},{4,5},{5,4},{6,7},{7,6},{8,9},{9,8},{10,11... | collective-permute-start | bytes 3145736 | tf_op jit(solution)/shard_map/ppermute | solution.py:38
  62.8 0.0 collective-permute-done.4
  62.8 1.9 %collective-permute-start.10 = (bf16[256,1024]{1,0:T(8,128)(2,1)S(1)}, bf16[256,1024]{1,0:T(8,128)(2,1)S(1)}, u32[]{:S(2)}, u32[]{:S(2)}) collective-permute-start(bf16[256,1024]{1,0:T(8,128)(2,1)S(1)} %collective-permute-done.4), channel_id=1, source_target_pairs={{0,2},{1,3},{2,0},{3,1},{4,6},{5,7},{6,4},{7,5},{8,10},{9,11},{10,... | collective-permute-start | bytes 1572872 | tf_op jit(solution)/shard_map/ppermute | solution.py:38
  64.8 0.0 collective-permute-done.6
  64.8 0.0 collective-permute-done.7
  64.8 0.0 collective-permute-done.8
  64.9 2.0 %collective-permute-start.13 = (bf16[128,1024]{1,0:T(8,128)(2,1)S(1)}, bf16[128,1024]{1,0:T(8,128)(2,1)S(1)}, u32[]{:S(2)}, u32[]{:S(2)}) collective-permute-start(bf16[128,1024]{1,0:T(8,128)(2,1)S(1)} %pad_maximum_fusion.2), channel_id=1, source_target_pairs={{0,4},{1,5},{2,6},{3,7},{4,0},{5,1},{6,2},{7,3},{8,12},{9,13},{10,... | collective-permute-start | bytes 786440 | tf_op jit(solution)/shard_map/ppermute | solution.py:38
  66.9 3.0 %collective-permute-start.9 = (bf16[384,1024]{1,0:T(8,128)(2,1)S(1)}, bf16[384,1024]{1,0:T(8,128)(2,1)S(1)}, u32[]{:S(2)}, u32[]{:S(2)}) collective-permute-start(bf16[384,1024]{1,0:T(8,128)(2,1)S(1)} %get-tuple-element.62.refs_0_), channel_id=1, source_target_pairs={{0,1},{1,0},{2,3},{3,2},{4,5},{5,4},{6,7},{7,6},{8,9},{9,8},{10,11... | collective-permute-start | bytes 2359304 | tf_op jit(solution)/shard_map/ppermute | solution.py:38
  70.0 11.9 %collective-permute-done.13 = bf16[128,1024]{1,0:T(8,128)(2,1)S(1)} collective-permute-done((bf16[128,1024]{1,0:T(8,128)(2,1)S(1)}, bf16[128,1024]{1,0:T(8,128)(2,1)S(1)}, u32[]{:S(2)}, u32[]{:S(2)}) %collective-permute-start.13) | collective-permute-done | bytes 262176 | tf_op jit(solution)/shard_map/ppermute | solution.py:38
  81.9 2.3 %collective-permute-start.14 = (bf16[256,1024]{1,0:T(8,128)(2,1)S(1)}, bf16[256,1024]{1,0:T(8,128)(2,1)S(1)}, u32[]{:S(2)}, u32[]{:S(2)}) collective-permute-start(bf16[256,1024]{1,0:T(8,128)(2,1)S(1)} %constant_dynamic-update-slice_fusion.6), channel_id=1, source_target_pairs={{0,2},{1,3},{2,0},{3,1},{4,6},{5,7},{6,4},{7,5},{8,10},{9,11},{10,... | collective-permute-start | bytes 1572872 | tf_op jit(solution)/shard_map/ppermute | solution.py:38
  84.2 0.0 collective-permute-done.10.refs_2_
  84.2 3.3 %collective-permute-start.15 = (bf16[256,1024]{1,0:T(8,128)(2,1)S(1)}, bf16[256,1024]{1,0:T(8,128)(2,1)S(1)}, u32[]{:S(2)}, u32[]{:S(2)}) collective-permute-start(bf16[256,1024]{1,0:T(8,128)(2,1)S(1)} %collective-permute-done.10.refs_2_), channel_id=1, source_target_pairs={{0,1},{1,0},{2,3},{3,2},{4,5},{5,4},{6,7},{7,6},{8,9},{9,8},{10,11... | collective-permute-start | bytes 1572872 | tf_op jit(solution)/shard_map/ppermute | solution.py:38
  87.5 0.0 collective-permute-done.12.refs_1_
  87.5 2.0 %shard_map.40.refs_3_ = f32[2,1024,256]{2,1,0:T(8,128)S(1)} custom-call(bf16[512,1024]{1,0:T(8,128)(2,1)S(1)} %constant_dynamic-update-slice_fusion.1.refs_0_, bf16[512,1024]{1,0:T(8,128)(2,1)S(1)} %collective-permute-done.12.refs_1_), custom_call_target="tpu_custom_call" | custom-call | flops 1073741824 | bytes 4194304 | tf_op jit(solution)/shard_map/pallas_call | solution.py:173
  89.6 0.0 collective-permute-done.9.refs_1_
  89.6 2.5 %shard_map.41.refs_3_ = f32[2,1024,256]{2,1,0:T(8,128)S(1)} custom-call(bf16[384,1024]{1,0:T(8,128)(2,1)S(1)} %get-tuple-element.62.refs_0_, bf16[384,1024]{1,0:T(8,128)(2,1)S(1)} %collective-permute-done.9.refs_1_, bf16[256,1024]{1,0:T(8,128)(2,1)S(1)} %collective-permute-done.10.refs_2_, f32[2,1024,256]{2,1,0:T(8,128)S(1)} %shard_map.40.refs_3_), custom_call_target="tpu_custom_call" | custom-call | flops 1073741824 | bytes 4194304 | tf_op jit(solution)/shard_map/pallas_call | solution.py:173
  92.0 4.6 %collective-permute-done.14 = bf16[256,1024]{1,0:T(8,128)(2,1)S(1)} collective-permute-done((bf16[256,1024]{1,0:T(8,128)(2,1)S(1)}, bf16[256,1024]{1,0:T(8,128)(2,1)S(1)}, u32[]{:S(2)}, u32[]{:S(2)}) %collective-permute-start.14) | collective-permute-done | bytes 524320 | tf_op jit(solution)/shard_map/ppermute | solution.py:38
  96.7 0.0 collective-permute-done.15.refs_0_
  96.8 3.4 %collective-permute-start.16 = (bf16[384,1024]{1,0:T(8,128)(2,1)S(1)}, bf16[384,1024]{1,0:T(8,128)(2,1)S(1)}, u32[]{:S(2)}, u32[]{:S(2)}) collective-permute-start(bf16[384,1024]{1,0:T(8,128)(2,1)S(1)} %constant_dynamic-update-slice_fusion.7.refs_1_), channel_id=1, source_target_pairs={{0,1},{1,0},{2,3},{3,2},{4,5},{5,4},{6,7},{7,6},{8,9},{9,8},{10,11... | collective-permute-start | bytes 2359304 | tf_op jit(solution)/shard_map/ppermute | solution.py:38
  100.1 1.9 %collective-permute-done.16.refs_2_ = bf16[384,1024]{1,0:T(8,128)(2,1)S(1)} collective-permute-done((bf16[384,1024]{1,0:T(8,128)(2,1)S(1)}, bf16[384,1024]{1,0:T(8,128)(2,1)S(1)}, u32[]{:S(2)}, u32[]{:S(2)}) %collective-permute-start.16) | collective-permute-done | bytes 786464 | tf_op jit(solution)/shard_map/ppermute | solution.py:38
  102.0 3.3 %shard_map.42 = f32[2,1024,256]{2,1,0:T(8,128)} custom-call(bf16[256,1024]{1,0:T(8,128)(2,1)S(1)} %collective-permute-done.15.refs_0_, bf16[384,1024]{1,0:T(8,128)(2,1)S(1)} %constant_dynamic-update-slice_fusion.7.refs_1_, bf16[384,1024]{1,0:T(8,128)(2,1)S(1)} %collective-permute-done.16.refs_2_, f32[2,1024,256]{2,1,0:T(8,128)S(1)} %shard_map.41.refs_3_), custom_call_target="tpu_custom_call" | custom-call | flops 1073741824 | bytes 4194304 | tf_op jit(solution)/shard_map/pallas_call | solution.py:173
  (16 shorter events, 0.4 us)
Async XLA Ops:
  0.0 7.8 %copy-start.2 = (f32[256]{0:T(256)S(1)}, f32[256]{0:T(256)}, u32[]{:S(2)}) copy-start(f32[256]{0:T(256)} %param.4) | copy-start | bytes 3076
  0.0 1.9 %copy-start = (bf16[768,2,1,1024]{3,1,2,0:T(2,128)(2,1)S(1)}, bf16[768,2,1,1024]{3,1,2,0:T(2,128)(2,1)}, u32[]{:S(2)}) copy-start(bf16[768,2,1,1024]{3,1,2,0:T(2,128)(2,1)} %param.3) | copy-start | bytes 9437188
  1.9 5.9 %copy-start.1 = (bf16[768,2,1,1024]{3,1,2,0:T(2,128)(2,1)S(1)}, bf16[768,2,1,1024]{3,1,2,0:T(2,128)(2,1)}, u32[]{:S(2)}) copy-start(bf16[768,2,1,1024]{3,1,2,0:T(2,128)(2,1)} %param.3) | copy-start | bytes 9437188
  1.9 5.9 %copy-start.3 = (f32[16,1024]{1,0:T(8,128)S(1)}, f32[16,1024]{1,0:T(8,128)}, u32[]{:S(2)}) copy-start(f32[16,1024]{1,0:T(8,128)} %constant.2.clone.trig_ref) | copy-start | bytes 196612
  2.2 25.8 %collective-permute-start = (bf16[240,2,1024]{2,1,0:T(2,128)(2,1)S(1)}, bf16[240,2,1024]{2,1,0:T(2,128)(2,1)S(1)}, u32[]{:S(2)}, u32[]{:S(2)}) collective-permute-start(bf16[240,2,1024]{2,1,0:T(2,128)(2,1)S(1)} %shard_map.37), channel_id=1, source_target_pairs={{0,1},{1,2},{2,3},{3,4},{4,5},{5,6},{6,7},{8,9},{9,10},{10,11},{11... | collective-permute-start | bytes 2949128 | tf_op jit(solution)/shard_map/ppermute | solution.py:62
  9.5 11.3 %collective-permute-start.1 = (bf16[128,1024]{1,0:T(8,128)(2,1)S(1)}, bf16[128,1024]{1,0:T(8,128)(2,1)S(1)}, u32[]{:S(2)}, u32[]{:S(2)}) collective-permute-start(bf16[128,1024]{1,0:T(8,128)(2,1)S(1)} %get-tuple-element.23), channel_id=1, source_target_pairs={{0,8},{1,9},{2,10},{3,11},{4,12},{5,13},{6,14},{7,15},{8,16},{9,17... | collective-permute-start | bytes 786440 | tf_op jit(solution)/shard_map/ppermute | solution.py:38
  12.7 12.7 %collective-permute-start.2 = (bf16[128,1024]{1,0:T(8,128)(2,1)S(1)}, bf16[128,1024]{1,0:T(8,128)(2,1)S(1)}, u32[]{:S(2)}, u32[]{:S(2)}) collective-permute-start(bf16[128,1024]{1,0:T(8,128)(2,1)S(1)} %get-tuple-element.24), channel_id=1, source_target_pairs={{0,16},{1,17},{2,18},{3,19},{4,20},{5,21},{6,22},{7,23},{8,24},{9,... | collective-permute-start | bytes 786440 | tf_op jit(solution)/shard_map/ppermute | solution.py:38
  17.0 11.0 %collective-permute-start.3 = (bf16[128,1024]{1,0:T(8,128)(2,1)S(1)}, bf16[128,1024]{1,0:T(8,128)(2,1)S(1)}, u32[]{:S(2)}, u32[]{:S(2)}) collective-permute-start(bf16[128,1024]{1,0:T(8,128)(2,1)S(1)} %get-tuple-element.25), channel_id=1, source_target_pairs={{0,24},{1,25},{2,26},{3,27},{4,28},{5,29},{6,30},{7,31},{8,0},{9,1... | collective-permute-start | bytes 786440 | tf_op jit(solution)/shard_map/ppermute | solution.py:38
  20.1 15.4 %collective-permute-start.5 = (bf16[240,2,1024]{2,1,0:T(2,128)(2,1)S(1)}, bf16[240,2,1024]{2,1,0:T(2,128)(2,1)S(1)}, u32[]{:S(2)}, u32[]{:S(2)}) collective-permute-start(bf16[240,2,1024]{2,1,0:T(2,128)(2,1)S(1)} %shard_map.37), channel_id=1, source_target_pairs={{7,8},{15,16},{23,24},{39,40},{47,48},{55,56},{71,72},{79,80},{87,... | collective-permute-start | bytes 2949128 | tf_op jit(solution)/shard_map/ppermute | solution.py:62
  28.3 32.0 %collective-permute-start.11 = (bf16[256,1024]{1,0:T(8,128)(2,1)S(1)}, bf16[256,1024]{1,0:T(8,128)(2,1)S(1)}, u32[]{:S(2)}, u32[]{:S(2)}) collective-permute-start(bf16[256,1024]{1,0:T(8,128)(2,1)S(1)} %pad_maximum_fusion.1), channel_id=1, source_target_pairs={{0,2},{1,3},{2,0},{3,1},{4,6},{5,7},{6,4},{7,5},{8,10},{9,11},{10,... | collective-permute-start | bytes 1572872 | tf_op jit(solution)/shard_map/ppermute | solution.py:38
  31.8 31.0 %collective-permute-start.4 = (bf16[256,1024]{1,0:T(8,128)(2,1)S(1)}, bf16[256,1024]{1,0:T(8,128)(2,1)S(1)}, u32[]{:S(2)}, u32[]{:S(2)}) collective-permute-start(bf16[256,1024]{1,0:T(8,128)(2,1)S(1)} %pad_maximum_fusion), channel_id=1, source_target_pairs={{0,4},{1,5},{2,6},{3,7},{4,0},{5,1},{6,2},{7,3},{8,12},{9,13},{10,... | collective-permute-start | bytes 1572872 | tf_op jit(solution)/shard_map/ppermute | solution.py:38
  36.4 28.4 %collective-permute-start.6 = (bf16[64,1024]{1,0:T(8,128)(2,1)S(1)}, bf16[64,1024]{1,0:T(8,128)(2,1)S(1)}, u32[]{:S(2)}, u32[]{:S(2)}) collective-permute-start(bf16[64,1024]{1,0:T(8,128)(2,1)S(1)} %get-tuple-element.33), channel_id=1, source_target_pairs={{0,8},{1,9},{2,10},{3,11},{4,12},{5,13},{6,14},{7,15},{8,16},{9,17... | collective-permute-start | bytes 393224 | tf_op jit(solution)/shard_map/ppermute | solution.py:38
  40.8 24.0 %collective-permute-start.7 = (bf16[64,1024]{1,0:T(8,128)(2,1)S(1)}, bf16[64,1024]{1,0:T(8,128)(2,1)S(1)}, u32[]{:S(2)}, u32[]{:S(2)}) collective-permute-start(bf16[64,1024]{1,0:T(8,128)(2,1)S(1)} %get-tuple-element.34), channel_id=1, source_target_pairs={{0,16},{1,17},{2,18},{3,19},{4,20},{5,21},{6,22},{7,23},{8,24},{9,... | collective-permute-start | bytes 393224 | tf_op jit(solution)/shard_map/ppermute | solution.py:38
  43.8 21.1 %collective-permute-start.8 = (bf16[64,1024]{1,0:T(8,128)(2,1)S(1)}, bf16[64,1024]{1,0:T(8,128)(2,1)S(1)}, u32[]{:S(2)}, u32[]{:S(2)}) collective-permute-start(bf16[64,1024]{1,0:T(8,128)(2,1)S(1)} %get-tuple-element.35), channel_id=1, source_target_pairs={{0,24},{1,25},{2,26},{3,27},{4,28},{5,29},{6,30},{7,31},{8,0},{9,1... | collective-permute-start | bytes 393224 | tf_op jit(solution)/shard_map/ppermute | solution.py:38
  60.4 27.1 %collective-permute-start.12 = (bf16[512,1024]{1,0:T(8,128)(2,1)S(1)}, bf16[512,1024]{1,0:T(8,128)(2,1)S(1)}, u32[]{:S(2)}, u32[]{:S(2)}) collective-permute-start(bf16[512,1024]{1,0:T(8,128)(2,1)S(1)} %constant_dynamic-update-slice_fusion.1.refs_0_), channel_id=1, source_target_pairs={{0,1},{1,0},{2,3},{3,2},{4,5},{5,4},{6,7},{7,6},{8,9},{9,8},{10,11... | collective-permute-start | bytes 3145736 | tf_op jit(solution)/shard_map/ppermute | solution.py:38
  62.8 21.4 %collective-permute-start.10 = (bf16[256,1024]{1,0:T(8,128)(2,1)S(1)}, bf16[256,1024]{1,0:T(8,128)(2,1)S(1)}, u32[]{:S(2)}, u32[]{:S(2)}) collective-permute-start(bf16[256,1024]{1,0:T(8,128)(2,1)S(1)} %collective-permute-done.4), channel_id=1, source_target_pairs={{0,2},{1,3},{2,0},{3,1},{4,6},{5,7},{6,4},{7,5},{8,10},{9,11},{10,... | collective-permute-start | bytes 1572872 | tf_op jit(solution)/shard_map/ppermute | solution.py:38
  64.9 17.0 %collective-permute-start.13 = (bf16[128,1024]{1,0:T(8,128)(2,1)S(1)}, bf16[128,1024]{1,0:T(8,128)(2,1)S(1)}, u32[]{:S(2)}, u32[]{:S(2)}) collective-permute-start(bf16[128,1024]{1,0:T(8,128)(2,1)S(1)} %pad_maximum_fusion.2), channel_id=1, source_target_pairs={{0,4},{1,5},{2,6},{3,7},{4,0},{5,1},{6,2},{7,3},{8,12},{9,13},{10,... | collective-permute-start | bytes 786440 | tf_op jit(solution)/shard_map/ppermute | solution.py:38
  66.9 22.6 %collective-permute-start.9 = (bf16[384,1024]{1,0:T(8,128)(2,1)S(1)}, bf16[384,1024]{1,0:T(8,128)(2,1)S(1)}, u32[]{:S(2)}, u32[]{:S(2)}) collective-permute-start(bf16[384,1024]{1,0:T(8,128)(2,1)S(1)} %get-tuple-element.62.refs_0_), channel_id=1, source_target_pairs={{0,1},{1,0},{2,3},{3,2},{4,5},{5,4},{6,7},{7,6},{8,9},{9,8},{10,11... | collective-permute-start | bytes 2359304 | tf_op jit(solution)/shard_map/ppermute | solution.py:38
  81.9 14.8 %collective-permute-start.14 = (bf16[256,1024]{1,0:T(8,128)(2,1)S(1)}, bf16[256,1024]{1,0:T(8,128)(2,1)S(1)}, u32[]{:S(2)}, u32[]{:S(2)}) collective-permute-start(bf16[256,1024]{1,0:T(8,128)(2,1)S(1)} %constant_dynamic-update-slice_fusion.6), channel_id=1, source_target_pairs={{0,2},{1,3},{2,0},{3,1},{4,6},{5,7},{6,4},{7,5},{8,10},{9,11},{10,... | collective-permute-start | bytes 1572872 | tf_op jit(solution)/shard_map/ppermute | solution.py:38
  84.2 12.5 %collective-permute-start.15 = (bf16[256,1024]{1,0:T(8,128)(2,1)S(1)}, bf16[256,1024]{1,0:T(8,128)(2,1)S(1)}, u32[]{:S(2)}, u32[]{:S(2)}) collective-permute-start(bf16[256,1024]{1,0:T(8,128)(2,1)S(1)} %collective-permute-done.10.refs_2_), channel_id=1, source_target_pairs={{0,1},{1,0},{2,3},{3,2},{4,5},{5,4},{6,7},{7,6},{8,9},{9,8},{10,11... | collective-permute-start | bytes 1572872 | tf_op jit(solution)/shard_map/ppermute | solution.py:38
  96.8 5.3 %collective-permute-start.16 = (bf16[384,1024]{1,0:T(8,128)(2,1)S(1)}, bf16[384,1024]{1,0:T(8,128)(2,1)S(1)}, u32[]{:S(2)}, u32[]{:S(2)}) collective-permute-start(bf16[384,1024]{1,0:T(8,128)(2,1)S(1)} %constant_dynamic-update-slice_fusion.7.refs_1_), channel_id=1, source_target_pairs={{0,1},{1,0},{2,3},{3,2},{4,5},{5,4},{6,7},{7,6},{8,9},{9,8},{10,11... | collective-permute-start | bytes 2359304 | tf_op jit(solution)/shard_map/ppermute | solution.py:38

commit v9 on v8

--- a/solution.py
+++ b/solution.py
@@ -234,10 +234,9 @@
     acc = correlate([ma, move(ma, other_core)], None)
     own = jnp.concatenate([ta, mb], 0)
     acc = correlate([own, move(own, other_core), ta_near], acc)
-    ta_core = move(ta_near, other_core)
-    acc, b_near, ta_core = lax.optimization_barrier((acc, b_near, ta_core))
-    last = jnp.concatenate([b_near, tb], 0)
-    pieces = [ta_core, last, move(last, other_core)]
+    ta_core, tb_core = move(ta_near, other_core), move(tb, other_core)
+    acc, b_near, ta_core, tb_core = lax.optimization_barrier((acc, b_near, ta_core, tb_core))
+    pieces = [ta_core, tb, tb_core, b_near, move(b_near, other_core)]
     frames = samples_here // FINE * XS * ZS * CORES
     return correlate(pieces, acc, 1.0 / frames)[None]
 

time: 106 us -> 106 us (level)
  waiting for transfers between devices: 39 us -> 37.3 us
  starting transfers between devices: 52.9 us -> 54.2 us
    ppermute x15 -> x16, waiting for transfers between devices: 39 us -> 37.3 us  [move(): return lax.ppermute(array, 'tm', moves(rule))]
    ppermute x15 -> x16, starting transfers between devices: 46.7 us -> 48 us  [move(): return lax.ppermute(array, 'tm', moves(rule))]
  transfers between devices with their start and end apart: 17 -> 18, of which waited for: 6 -> 6; matrix products, arithmetic and copies ran while one was open for 0% -> 0% of each run, Pallas kernels for 7% -> 7%
where the time goes in v9:
time: 106 us; the launch traced here: 105 us
  starting transfers between devices  54.2 us (51%)
  waiting for transfers between devices  37.3 us (35%)
  Pallas kernels  10.7 us (10%)
  local copies, waits for them, and re-layouts  2.18 us (2%)
    ppermute x16, starting transfers between devices, move(): return lax.ppermute(array, 'tm', moves(rule))  48 us
    ppermute x16, waiting for transfers between devices, move(): return lax.ppermute(array, 'tm', moves(rule))  37.3 us
    pallas_call x3, Pallas kernels, correlate(): pl.pallas_call(functools.partial(products, len(pieces), scale), grid=(4,)...  7.8 us
    ppermute x2, starting transfers between devices, halo_of(): return (lax.ppermute(tail, 'tm', inside), lax.ppermute(tail, 'tm', across))  6.25 us
  transfers between devices with their start and end apart: 18, of which 6 were waited for; matrix products, arithmetic and copies ran while one was open for 0% of the time, Pallas kernels for 7%

profile of v9, /device:TPU:1, one launch (start us, length us, event | category | flops | bytes accessed | tf_op | source)
XLA Modules:
  0.0 104.9 jit_solution(13446117300994520327)
XLA Ops:
  0.0 0.0 copy-start.2
  0.0 0.0 copy-start
  0.0 1.9 %copy-done = bf16[768,2,1,1024]{3,1,2,0:T(2,128)(2,1)S(1)} copy-done((bf16[768,2,1,1024]{3,1,2,0:T(2,128)(2,1)S(1)}, bf16[768,2,1,1024]{3,1,2,0:T(2,128)(2,1)}, u32[]{:S(2)}) %copy-start) | copy-done | bytes 3145752
  1.9 0.3 shard_map.37
  2.2 5.5 %collective-permute-start = (bf16[240,2,1024]{2,1,0:T(2,128)(2,1)S(1)}, bf16[240,2,1024]{2,1,0:T(2,128)(2,1)S(1)}, u32[]{:S(2)}, u32[]{:S(2)}) collective-permute-start(bf16[240,2,1024]{2,1,0:T(2,128)(2,1)S(1)} %shard_map.37), channel_id=1, source_target_pairs={{0,1},{1,2},{2,3},{3,4},{4,5},{5,6},{6,7},{8,9},{9,10},{10,11},{11... | collective-permute-start | bytes 2949128 | tf_op jit(solution)/shard_map/ppermute | solution.py:62
  7.8 0.0 copy-done.2
  7.8 0.0 copy-done.1
  7.8 0.0 copy-done.3
  7.8 1.7 %shard_map.38 = (bf16[256,1024]{1,0:T(8,128)(2,1)S(1)}, bf16[128,1024]{1,0:T(8,128)(2,1)S(1)}, bf16[128,1024]{1,0:T(8,128)(2,1)S(1)}, bf16[128,1024]{1,0:T(8,128)(2,1)S(1)}, bf16[128,1024]{1,0:T(8,128)(2,1)S(1)}) custom-call(f32[1,256]{1,0:T(1,128)S(1)} %bitcast.6, f32[16,1024]{1,0:T(8,128)S(1)} %copy-done.3, bf16[768,2,1024]{2,1,0:T(2,128)(2,1)S(1)} %bitcast.4), custom_call_target="tpu_custom_call" | custom-call | flops 1073741824 | bytes 6291456 | tf_op jit(solution)/shard_map/pallas_call | solution.py:207
  9.5 3.1 %collective-permute-start.1 = (bf16[128,1024]{1,0:T(8,128)(2,1)S(1)}, bf16[128,1024]{1,0:T(8,128)(2,1)S(1)}, u32[]{:S(2)}, u32[]{:S(2)}) collective-permute-start(bf16[128,1024]{1,0:T(8,128)(2,1)S(1)} %get-tuple-element.24), channel_id=1, source_target_pairs={{0,8},{1,9},{2,10},{3,11},{4,12},{5,13},{6,14},{7,15},{8,16},{9,17... | collective-permute-start | bytes 786440 | tf_op jit(solution)/shard_map/ppermute | solution.py:38
  12.7 4.4 %collective-permute-start.2 = (bf16[128,1024]{1,0:T(8,128)(2,1)S(1)}, bf16[128,1024]{1,0:T(8,128)(2,1)S(1)}, u32[]{:S(2)}, u32[]{:S(2)}) collective-permute-start(bf16[128,1024]{1,0:T(8,128)(2,1)S(1)} %get-tuple-element.25), channel_id=1, source_target_pairs={{0,16},{1,17},{2,18},{3,19},{4,20},{5,21},{6,22},{7,23},{8,24},{9,... | collective-permute-start | bytes 786440 | tf_op jit(solution)/shard_map/ppermute | solution.py:38
  17.0 3.1 %collective-permute-start.3 = (bf16[128,1024]{1,0:T(8,128)(2,1)S(1)}, bf16[128,1024]{1,0:T(8,128)(2,1)S(1)}, u32[]{:S(2)}, u32[]{:S(2)}) collective-permute-start(bf16[128,1024]{1,0:T(8,128)(2,1)S(1)} %get-tuple-element.26), channel_id=1, source_target_pairs={{0,24},{1,25},{2,26},{3,27},{4,28},{5,29},{6,30},{7,31},{8,0},{9,1... | collective-permute-start | bytes 786440 | tf_op jit(solution)/shard_map/ppermute | solution.py:38
  20.1 0.7 collective-permute-start.5
  20.8 0.0 collective-permute-done.1
  20.8 4.5 %collective-permute-done.2 = bf16[128,1024]{1,0:T(8,128)(2,1)S(1)} collective-permute-done((bf16[128,1024]{1,0:T(8,128)(2,1)S(1)}, bf16[128,1024]{1,0:T(8,128)(2,1)S(1)}, u32[]{:S(2)}, u32[]{:S(2)}) %collective-permute-start.2) | collective-permute-done | bytes 262176 | tf_op jit(solution)/shard_map/ppermute | solution.py:38
  25.3 2.7 %collective-permute-done.3 = bf16[128,1024]{1,0:T(8,128)(2,1)S(1)} collective-permute-done((bf16[128,1024]{1,0:T(8,128)(2,1)S(1)}, bf16[128,1024]{1,0:T(8,128)(2,1)S(1)}, u32[]{:S(2)}, u32[]{:S(2)}) %collective-permute-start.3) | collective-permute-done | bytes 262176 | tf_op jit(solution)/shard_map/ppermute | solution.py:38
  28.1 0.0 collective-permute-done.halo_ref
  28.3 3.5 %collective-permute-start.11 = (bf16[256,1024]{1,0:T(8,128)(2,1)S(1)}, bf16[256,1024]{1,0:T(8,128)(2,1)S(1)}, u32[]{:S(2)}, u32[]{:S(2)}) collective-permute-start(bf16[256,1024]{1,0:T(8,128)(2,1)S(1)} %pad_maximum_fusion.1), channel_id=1, source_target_pairs={{0,2},{1,3},{2,0},{3,1},{4,6},{5,7},{6,4},{7,5},{8,10},{9,11},{10,... | collective-permute-start | bytes 1572872 | tf_op jit(solution)/shard_map/ppermute | solution.py:38
  31.8 3.7 %collective-permute-start.4 = (bf16[256,1024]{1,0:T(8,128)(2,1)S(1)}, bf16[256,1024]{1,0:T(8,128)(2,1)S(1)}, u32[]{:S(2)}, u32[]{:S(2)}) collective-permute-start(bf16[256,1024]{1,0:T(8,128)(2,1)S(1)} %pad_maximum_fusion), channel_id=1, source_target_pairs={{0,4},{1,5},{2,6},{3,7},{4,0},{5,1},{6,2},{7,3},{8,12},{9,13},{10,... | collective-permute-start | bytes 1572872 | tf_op jit(solution)/shard_map/ppermute | solution.py:38
  35.5 0.0 collective-permute-done.5.wrap_ref
  35.5 0.8 shard_map.39
  36.4 4.3 %collective-permute-start.8 = (bf16[64,1024]{1,0:T(8,128)(2,1)S(1)}, bf16[64,1024]{1,0:T(8,128)(2,1)S(1)}, u32[]{:S(2)}, u32[]{:S(2)}) collective-permute-start(bf16[64,1024]{1,0:T(8,128)(2,1)S(1)} %get-tuple-element.36), channel_id=1, source_target_pairs={{0,24},{1,25},{2,26},{3,27},{4,28},{5,29},{6,30},{7,31},{8,0},{9,1... | collective-permute-start | bytes 393224 | tf_op jit(solution)/shard_map/ppermute | solution.py:38
  40.7 3.8 %collective-permute-start.7 = (bf16[64,1024]{1,0:T(8,128)(2,1)S(1)}, bf16[64,1024]{1,0:T(8,128)(2,1)S(1)}, u32[]{:S(2)}, u32[]{:S(2)}) collective-permute-start(bf16[64,1024]{1,0:T(8,128)(2,1)S(1)} %get-tuple-element.35), channel_id=1, source_target_pairs={{0,16},{1,17},{2,18},{3,19},{4,20},{5,21},{6,22},{7,23},{8,24},{9,... | collective-permute-start | bytes 393224 | tf_op jit(solution)/shard_map/ppermute | solution.py:38
  44.5 1.9 %collective-permute-start.6 = (bf16[64,1024]{1,0:T(8,128)(2,1)S(1)}, bf16[64,1024]{1,0:T(8,128)(2,1)S(1)}, u32[]{:S(2)}, u32[]{:S(2)}) collective-permute-start(bf16[64,1024]{1,0:T(8,128)(2,1)S(1)} %get-tuple-element.34), channel_id=1, source_target_pairs={{0,8},{1,9},{2,10},{3,11},{4,12},{5,13},{6,14},{7,15},{8,16},{9,17... | collective-permute-start | bytes 393224 | tf_op jit(solution)/shard_map/ppermute | solution.py:38
  46.4 13.9 %collective-permute-done.11 = bf16[256,1024]{1,0:T(8,128)(2,1)S(1)} collective-permute-done((bf16[256,1024]{1,0:T(8,128)(2,1)S(1)}, bf16[256,1024]{1,0:T(8,128)(2,1)S(1)}, u32[]{:S(2)}, u32[]{:S(2)}) %collective-permute-start.11) | collective-permute-done | bytes 524320 | tf_op jit(solution)/shard_map/ppermute | solution.py:38
  60.4 2.4 %collective-permute-start.12 = (bf16[512,1024]{1,0:T(8,128)(2,1)S(1)}, bf16[512,1024]{1,0:T(8,128)(2,1)S(1)}, u32[]{:S(2)}, u32[]{:S(2)}) collective-permute-start(bf16[512,1024]{1,0:T(8,128)(2,1)S(1)} %constant_dynamic-update-slice_fusion.1.refs_0_), channel_id=1, source_target_pairs={{0,1},{1,0},{2,3},{3,2},{4,5},{5,4},{6,7},{7,6},{8,9},{9,8},{10,11... | collective-permute-start | bytes 3145736 | tf_op jit(solution)/shard_map/ppermute | solution.py:38
  62.8 0.0 collective-permute-done.4
  62.8 1.9 %collective-permute-start.10 = (bf16[256,1024]{1,0:T(8,128)(2,1)S(1)}, bf16[256,1024]{1,0:T(8,128)(2,1)S(1)}, u32[]{:S(2)}, u32[]{:S(2)}) collective-permute-start(bf16[256,1024]{1,0:T(8,128)(2,1)S(1)} %collective-permute-done.4), channel_id=1, source_target_pairs={{0,2},{1,3},{2,0},{3,1},{4,6},{5,7},{6,4},{7,5},{8,10},{9,11},{10,... | collective-permute-start | bytes 1572872 | tf_op jit(solution)/shard_map/ppermute | solution.py:38
  64.8 0.0 collective-permute-done.6
  64.8 0.0 collective-permute-done.7
  64.8 0.0 collective-permute-done.8
  64.9 2.0 %collective-permute-start.13 = (bf16[128,1024]{1,0:T(8,128)(2,1)S(1)}, bf16[128,1024]{1,0:T(8,128)(2,1)S(1)}, u32[]{:S(2)}, u32[]{:S(2)}) collective-permute-start(bf16[128,1024]{1,0:T(8,128)(2,1)S(1)} %pad_maximum_fusion.2), channel_id=1, source_target_pairs={{0,4},{1,5},{2,6},{3,7},{4,0},{5,1},{6,2},{7,3},{8,12},{9,13},{10,... | collective-permute-start | bytes 786440 | tf_op jit(solution)/shard_map/ppermute | solution.py:38
  66.9 3.0 %collective-permute-start.9 = (bf16[384,1024]{1,0:T(8,128)(2,1)S(1)}, bf16[384,1024]{1,0:T(8,128)(2,1)S(1)}, u32[]{:S(2)}, u32[]{:S(2)}) collective-permute-start(bf16[384,1024]{1,0:T(8,128)(2,1)S(1)} %get-tuple-element.64.refs_0_), channel_id=1, source_target_pairs={{0,1},{1,0},{2,3},{3,2},{4,5},{5,4},{6,7},{7,6},{8,9},{9,8},{10,11... | collective-permute-start | bytes 2359304 | tf_op jit(solution)/shard_map/ppermute | solution.py:38
  70.0 11.9 %collective-permute-done.13.refs_1_ = bf16[128,1024]{1,0:T(8,128)(2,1)S(1)} collective-permute-done((bf16[128,1024]{1,0:T(8,128)(2,1)S(1)}, bf16[128,1024]{1,0:T(8,128)(2,1)S(1)}, u32[]{:S(2)}, u32[]{:S(2)}) %collective-permute-start.13) | collective-permute-done | bytes 262176 | tf_op jit(solution)/shard_map/ppermute | solution.py:38
  81.9 2.3 %collective-permute-start.14 = (bf16[256,1024]{1,0:T(8,128)(2,1)S(1)}, bf16[256,1024]{1,0:T(8,128)(2,1)S(1)}, u32[]{:S(2)}, u32[]{:S(2)}) collective-permute-start(bf16[256,1024]{1,0:T(8,128)(2,1)S(1)} %constant_dynamic-update-slice_fusion.6), channel_id=1, source_target_pairs={{0,2},{1,3},{2,0},{3,1},{4,6},{5,7},{6,4},{7,5},{8,10},{9,11},{10,... | collective-permute-start | bytes 1572872 | tf_op jit(solution)/shard_map/ppermute | solution.py:38
  84.2 0.0 collective-permute-done.10.refs_2_
  84.2 3.3 %collective-permute-start.15 = (bf16[256,1024]{1,0:T(8,128)(2,1)S(1)}, bf16[256,1024]{1,0:T(8,128)(2,1)S(1)}, u32[]{:S(2)}, u32[]{:S(2)}) collective-permute-start(bf16[256,1024]{1,0:T(8,128)(2,1)S(1)} %collective-permute-done.10.refs_2_), channel_id=1, source_target_pairs={{0,1},{1,0},{2,3},{3,2},{4,5},{5,4},{6,7},{7,6},{8,9},{9,8},{10,11... | collective-permute-start | bytes 1572872 | tf_op jit(solution)/shard_map/ppermute | solution.py:38
  87.5 1.9 %collective-permute-start.16 = (bf16[128,1024]{1,0:T(8,128)(2,1)S(1)}, bf16[128,1024]{1,0:T(8,128)(2,1)S(1)}, u32[]{:S(2)}, u32[]{:S(2)}) collective-permute-start(bf16[128,1024]{1,0:T(8,128)(2,1)S(1)} %collective-permute-done.13.refs_1_), channel_id=1, source_target_pairs={{0,1},{1,0},{2,3},{3,2},{4,5},{5,4},{6,7},{7,6},{8,9},{9,8},{10,11... | collective-permute-start | bytes 786440 | tf_op jit(solution)/shard_map/ppermute | solution.py:38
  89.4 0.0 collective-permute-done.12.refs_1_
  89.4 2.0 %shard_map.40.refs_3_ = f32[2,1024,256]{2,1,0:T(8,128)S(1)} custom-call(bf16[512,1024]{1,0:T(8,128)(2,1)S(1)} %constant_dynamic-update-slice_fusion.1.refs_0_, bf16[512,1024]{1,0:T(8,128)(2,1)S(1)} %collective-permute-done.12.refs_1_), custom_call_target="tpu_custom_call" | custom-call | flops 1073741824 | bytes 4194304 | tf_op jit(solution)/shard_map/pallas_call | solution.py:173
  91.5 0.0 collective-permute-done.9.refs_1_
  91.5 2.5 %shard_map.41.refs_5_ = f32[2,1024,256]{2,1,0:T(8,128)S(1)} custom-call(bf16[384,1024]{1,0:T(8,128)(2,1)S(1)} %get-tuple-element.64.refs_0_, bf16[384,1024]{1,0:T(8,128)(2,1)S(1)} %collective-permute-done.9.refs_1_, bf16[256,1024]{1,0:T(8,128)(2,1)S(1)} %collective-permute-done.10.refs_2_, f32[2,1024,256]{2,1,0:T(8,128)S(1)} %shard_map.40.refs_3_), custom_call_target="tpu_custom_call" | custom-call | flops 1073741824 | bytes 4194304 | tf_op jit(solution)/shard_map/pallas_call | solution.py:173
  94.0 0.0 collective-permute-done.16.refs_2_
  94.0 2.7 %collective-permute-done.14.refs_3_ = bf16[256,1024]{1,0:T(8,128)(2,1)S(1)} collective-permute-done((bf16[256,1024]{1,0:T(8,128)(2,1)S(1)}, bf16[256,1024]{1,0:T(8,128)(2,1)S(1)}, u32[]{:S(2)}, u32[]{:S(2)}) %collective-permute-start.14) | collective-permute-done | bytes 524320 | tf_op jit(solution)/shard_map/ppermute | solution.py:38
  96.7 0.0 collective-permute-done.15.refs_0_
  96.7 3.4 %collective-permute-start.17 = (bf16[256,1024]{1,0:T(8,128)(2,1)S(1)}, bf16[256,1024]{1,0:T(8,128)(2,1)S(1)}, u32[]{:S(2)}, u32[]{:S(2)}) collective-permute-start(bf16[256,1024]{1,0:T(8,128)(2,1)S(1)} %collective-permute-done.14.refs_3_), channel_id=1, source_target_pairs={{0,1},{1,0},{2,3},{3,2},{4,5},{5,4},{6,7},{7,6},{8,9},{9,8},{10,11... | collective-permute-start | bytes 1572872 | tf_op jit(solution)/shard_map/ppermute | solution.py:38
  100.0 1.5 %collective-permute-done.17.refs_4_ = bf16[256,1024]{1,0:T(8,128)(2,1)S(1)} collective-permute-done((bf16[256,1024]{1,0:T(8,128)(2,1)S(1)}, bf16[256,1024]{1,0:T(8,128)(2,1)S(1)}, u32[]{:S(2)}, u32[]{:S(2)}) %collective-permute-start.17) | collective-permute-done | bytes 524320 | tf_op jit(solution)/shard_map/ppermute | solution.py:38
  101.6 3.3 %shard_map.42 = f32[2,1024,256]{2,1,0:T(8,128)} custom-call(bf16[256,1024]{1,0:T(8,128)(2,1)S(1)} %collective-permute-done.15.refs_0_, bf16[128,1024]{1,0:T(8,128)(2,1)S(1)} %collective-permute-done.13.refs_1_, bf16[128,1024]{1,0:T(8,128)(2,1)S(1)} %collective-permute-done.16.refs_2_, bf16[256,1024]{1,0:T(8,128)(2,1)S(1)} %collective-permute-done.14.refs_3_, ...), custom_call_target="tpu_custom_call" | custom-call | flops 1073741824 | bytes 4194304 | tf_op jit(solution)/shard_map/pallas_call | solution.py:173
  (16 shorter events, 0.4 us)
Async XLA Ops:
  0.0 7.8 %copy-start.2 = (f32[256]{0:T(256)S(1)}, f32[256]{0:T(256)}, u32[]{:S(2)}) copy-start(f32[256]{0:T(256)} %param.4) | copy-start | bytes 3076
  0.0 1.9 %copy-start = (bf16[768,2,1,1024]{3,1,2,0:T(2,128)(2,1)S(1)}, bf16[768,2,1,1024]{3,1,2,0:T(2,128)(2,1)}, u32[]{:S(2)}) copy-start(bf16[768,2,1,1024]{3,1,2,0:T(2,128)(2,1)} %param.3) | copy-start | bytes 9437188
  1.9 5.9 %copy-start.1 = (bf16[768,2,1,1024]{3,1,2,0:T(2,128)(2,1)S(1)}, bf16[768,2,1,1024]{3,1,2,0:T(2,128)(2,1)}, u32[]{:S(2)}) copy-start(bf16[768,2,1,1024]{3,1,2,0:T(2,128)(2,1)} %param.3) | copy-start | bytes 9437188
  1.9 5.9 %copy-start.3 = (f32[16,1024]{1,0:T(8,128)S(1)}, f32[16,1024]{1,0:T(8,128)}, u32[]{:S(2)}) copy-start(f32[16,1024]{1,0:T(8,128)} %constant.2.clone.trig_ref) | copy-start | bytes 196612
  2.2 25.8 %collective-permute-start = (bf16[240,2,1024]{2,1,0:T(2,128)(2,1)S(1)}, bf16[240,2,1024]{2,1,0:T(2,128)(2,1)S(1)}, u32[]{:S(2)}, u32[]{:S(2)}) collective-permute-start(bf16[240,2,1024]{2,1,0:T(2,128)(2,1)S(1)} %shard_map.37), channel_id=1, source_target_pairs={{0,1},{1,2},{2,3},{3,4},{4,5},{5,6},{6,7},{8,9},{9,10},{10,11},{11... | collective-permute-start | bytes 2949128 | tf_op jit(solution)/shard_map/ppermute | solution.py:62
  9.5 11.3 %collective-permute-start.1 = (bf16[128,1024]{1,0:T(8,128)(2,1)S(1)}, bf16[128,1024]{1,0:T(8,128)(2,1)S(1)}, u32[]{:S(2)}, u32[]{:S(2)}) collective-permute-start(bf16[128,1024]{1,0:T(8,128)(2,1)S(1)} %get-tuple-element.24), channel_id=1, source_target_pairs={{0,8},{1,9},{2,10},{3,11},{4,12},{5,13},{6,14},{7,15},{8,16},{9,17... | collective-permute-start | bytes 786440 | tf_op jit(solution)/shard_map/ppermute | solution.py:38
  12.7 12.7 %collective-permute-start.2 = (bf16[128,1024]{1,0:T(8,128)(2,1)S(1)}, bf16[128,1024]{1,0:T(8,128)(2,1)S(1)}, u32[]{:S(2)}, u32[]{:S(2)}) collective-permute-start(bf16[128,1024]{1,0:T(8,128)(2,1)S(1)} %get-tuple-element.25), channel_id=1, source_target_pairs={{0,16},{1,17},{2,18},{3,19},{4,20},{5,21},{6,22},{7,23},{8,24},{9,... | collective-permute-start | bytes 786440 | tf_op jit(solution)/shard_map/ppermute | solution.py:38
  17.0 11.0 %collective-permute-start.3 = (bf16[128,1024]{1,0:T(8,128)(2,1)S(1)}, bf16[128,1024]{1,0:T(8,128)(2,1)S(1)}, u32[]{:S(2)}, u32[]{:S(2)}) collective-permute-start(bf16[128,1024]{1,0:T(8,128)(2,1)S(1)} %get-tuple-element.26), channel_id=1, source_target_pairs={{0,24},{1,25},{2,26},{3,27},{4,28},{5,29},{6,30},{7,31},{8,0},{9,1... | collective-permute-start | bytes 786440 | tf_op jit(solution)/shard_map/ppermute | solution.py:38
  20.1 15.4 %collective-permute-start.5 = (bf16[240,2,1024]{2,1,0:T(2,128)(2,1)S(1)}, bf16[240,2,1024]{2,1,0:T(2,128)(2,1)S(1)}, u32[]{:S(2)}, u32[]{:S(2)}) collective-permute-start(bf16[240,2,1024]{2,1,0:T(2,128)(2,1)S(1)} %shard_map.37), channel_id=1, source_target_pairs={{7,8},{15,16},{23,24},{39,40},{47,48},{55,56},{71,72},{79,80},{87,... | collective-permute-start | bytes 2949128 | tf_op jit(solution)/shard_map/ppermute | solution.py:62
  28.3 32.0 %collective-permute-start.11 = (bf16[256,1024]{1,0:T(8,128)(2,1)S(1)}, bf16[256,1024]{1,0:T(8,128)(2,1)S(1)}, u32[]{:S(2)}, u32[]{:S(2)}) collective-permute-start(bf16[256,1024]{1,0:T(8,128)(2,1)S(1)} %pad_maximum_fusion.1), channel_id=1, source_target_pairs={{0,2},{1,3},{2,0},{3,1},{4,6},{5,7},{6,4},{7,5},{8,10},{9,11},{10,... | collective-permute-start | bytes 1572872 | tf_op jit(solution)/shard_map/ppermute | solution.py:38
  31.8 31.0 %collective-permute-start.4 = (bf16[256,1024]{1,0:T(8,128)(2,1)S(1)}, bf16[256,1024]{1,0:T(8,128)(2,1)S(1)}, u32[]{:S(2)}, u32[]{:S(2)}) collective-permute-start(bf16[256,1024]{1,0:T(8,128)(2,1)S(1)} %pad_maximum_fusion), channel_id=1, source_target_pairs={{0,4},{1,5},{2,6},{3,7},{4,0},{5,1},{6,2},{7,3},{8,12},{9,13},{10,... | collective-permute-start | bytes 1572872 | tf_op jit(solution)/shard_map/ppermute | solution.py:38
  36.4 28.5 %collective-permute-start.8 = (bf16[64,1024]{1,0:T(8,128)(2,1)S(1)}, bf16[64,1024]{1,0:T(8,128)(2,1)S(1)}, u32[]{:S(2)}, u32[]{:S(2)}) collective-permute-start(bf16[64,1024]{1,0:T(8,128)(2,1)S(1)} %get-tuple-element.36), channel_id=1, source_target_pairs={{0,24},{1,25},{2,26},{3,27},{4,28},{5,29},{6,30},{7,31},{8,0},{9,1... | collective-permute-start | bytes 393224 | tf_op jit(solution)/shard_map/ppermute | solution.py:38
  40.7 24.1 %collective-permute-start.7 = (bf16[64,1024]{1,0:T(8,128)(2,1)S(1)}, bf16[64,1024]{1,0:T(8,128)(2,1)S(1)}, u32[]{:S(2)}, u32[]{:S(2)}) collective-permute-start(bf16[64,1024]{1,0:T(8,128)(2,1)S(1)} %get-tuple-element.35), channel_id=1, source_target_pairs={{0,16},{1,17},{2,18},{3,19},{4,20},{5,21},{6,22},{7,23},{8,24},{9,... | collective-permute-start | bytes 393224 | tf_op jit(solution)/shard_map/ppermute | solution.py:38
  44.5 20.3 %collective-permute-start.6 = (bf16[64,1024]{1,0:T(8,128)(2,1)S(1)}, bf16[64,1024]{1,0:T(8,128)(2,1)S(1)}, u32[]{:S(2)}, u32[]{:S(2)}) collective-permute-start(bf16[64,1024]{1,0:T(8,128)(2,1)S(1)} %get-tuple-element.34), channel_id=1, source_target_pairs={{0,8},{1,9},{2,10},{3,11},{4,12},{5,13},{6,14},{7,15},{8,16},{9,17... | collective-permute-start | bytes 393224 | tf_op jit(solution)/shard_map/ppermute | solution.py:38
  60.4 29.1 %collective-permute-start.12 = (bf16[512,1024]{1,0:T(8,128)(2,1)S(1)}, bf16[512,1024]{1,0:T(8,128)(2,1)S(1)}, u32[]{:S(2)}, u32[]{:S(2)}) collective-permute-start(bf16[512,1024]{1,0:T(8,128)(2,1)S(1)} %constant_dynamic-update-slice_fusion.1.refs_0_), channel_id=1, source_target_pairs={{0,1},{1,0},{2,3},{3,2},{4,5},{5,4},{6,7},{7,6},{8,9},{9,8},{10,11... | collective-permute-start | bytes 3145736 | tf_op jit(solution)/shard_map/ppermute | solution.py:38
  62.8 21.4 %collective-permute-start.10 = (bf16[256,1024]{1,0:T(8,128)(2,1)S(1)}, bf16[256,1024]{1,0:T(8,128)(2,1)S(1)}, u32[]{:S(2)}, u32[]{:S(2)}) collective-permute-start(bf16[256,1024]{1,0:T(8,128)(2,1)S(1)} %collective-permute-done.4), channel_id=1, source_target_pairs={{0,2},{1,3},{2,0},{3,1},{4,6},{5,7},{6,4},{7,5},{8,10},{9,11},{10,... | collective-permute-start | bytes 1572872 | tf_op jit(solution)/shard_map/ppermute | solution.py:38
  64.9 17.0 %collective-permute-start.13 = (bf16[128,1024]{1,0:T(8,128)(2,1)S(1)}, bf16[128,1024]{1,0:T(8,128)(2,1)S(1)}, u32[]{:S(2)}, u32[]{:S(2)}) collective-permute-start(bf16[128,1024]{1,0:T(8,128)(2,1)S(1)} %pad_maximum_fusion.2), channel_id=1, source_target_pairs={{0,4},{1,5},{2,6},{3,7},{4,0},{5,1},{6,2},{7,3},{8,12},{9,13},{10,... | collective-permute-start | bytes 786440 | tf_op jit(solution)/shard_map/ppermute | solution.py:38
  66.9 24.5 %collective-permute-start.9 = (bf16[384,1024]{1,0:T(8,128)(2,1)S(1)}, bf16[384,1024]{1,0:T(8,128)(2,1)S(1)}, u32[]{:S(2)}, u32[]{:S(2)}) collective-permute-start(bf16[384,1024]{1,0:T(8,128)(2,1)S(1)} %get-tuple-element.64.refs_0_), channel_id=1, source_target_pairs={{0,1},{1,0},{2,3},{3,2},{4,5},{5,4},{6,7},{7,6},{8,9},{9,8},{10,11... | collective-permute-start | bytes 2359304 | tf_op jit(solution)/shard_map/ppermute | solution.py:38
  81.9 14.8 %collective-permute-start.14 = (bf16[256,1024]{1,0:T(8,128)(2,1)S(1)}, bf16[256,1024]{1,0:T(8,128)(2,1)S(1)}, u32[]{:S(2)}, u32[]{:S(2)}) collective-permute-start(bf16[256,1024]{1,0:T(8,128)(2,1)S(1)} %constant_dynamic-update-slice_fusion.6), channel_id=1, source_target_pairs={{0,2},{1,3},{2,0},{3,1},{4,6},{5,7},{6,4},{7,5},{8,10},{9,11},{10,... | collective-permute-start | bytes 1572872 | tf_op jit(solution)/shard_map/ppermute | solution.py:38
  84.2 12.5 %collective-permute-start.15 = (bf16[256,1024]{1,0:T(8,128)(2,1)S(1)}, bf16[256,1024]{1,0:T(8,128)(2,1)S(1)}, u32[]{:S(2)}, u32[]{:S(2)}) collective-permute-start(bf16[256,1024]{1,0:T(8,128)(2,1)S(1)} %collective-permute-done.10.refs_2_), channel_id=1, source_target_pairs={{0,1},{1,0},{2,3},{3,2},{4,5},{5,4},{6,7},{7,6},{8,9},{9,8},{10,11... | collective-permute-start | bytes 1572872 | tf_op jit(solution)/shard_map/ppermute | solution.py:38
  87.5 6.5 %collective-permute-start.16 = (bf16[128,1024]{1,0:T(8,128)(2,1)S(1)}, bf16[128,1024]{1,0:T(8,128)(2,1)S(1)}, u32[]{:S(2)}, u32[]{:S(2)}) collective-permute-start(bf16[128,1024]{1,0:T(8,128)(2,1)S(1)} %collective-permute-done.13.refs_1_), channel_id=1, source_target_pairs={{0,1},{1,0},{2,3},{3,2},{4,5},{5,4},{6,7},{7,6},{8,9},{9,8},{10,11... | collective-permute-start | bytes 786440 | tf_op jit(solution)/shard_map/ppermute | solution.py:38
  96.7 4.9 %collective-permute-start.17 = (bf16[256,1024]{1,0:T(8,128)(2,1)S(1)}, bf16[256,1024]{1,0:T(8,128)(2,1)S(1)}, u32[]{:S(2)}, u32[]{:S(2)}) collective-permute-start(bf16[256,1024]{1,0:T(8,128)(2,1)S(1)} %collective-permute-done.14.refs_3_), channel_id=1, source_target_pairs={{0,1},{1,0},{2,3},{3,2},{4,5},{5,4},{6,7},{7,6},{8,9},{9,8},{10,11... | collective-permute-start | bytes 1572872 | tf_op jit(solution)/shard_map/ppermute | solution.py:38

commit v10 on v4

--- a/solution.py
+++ b/solution.py
@@ -111,16 +111,16 @@
     copy.wait()
 
 
-def filter_late(taps_ref, trig_ref, volt_ref, m0, m1, m2, m3, t_ref, band_ref):
+def filter_late(taps_ref, trig_ref, volt_ref, t0, t1, t2, t3, m_ref, band_ref):
     band_matrix(taps_ref, trig_ref, band_ref)
     for i in range(2):
         start = i * BLOCK * FINE
         window = volt_ref[start : start + WINDOW].reshape(2 * WINDOW, S)
         out = jnp.dot(band_ref[...], window, preferred_element_type=F32).astype(BF16)
         rows = slice(i * ROWS, (i + 1) * ROWS)
-        for d, m_ref in enumerate((m0, m1, m2, m3)):
-            m_ref[rows, :] = out[2 * d * ROWS : (2 * d + 1) * ROWS]
-            t_ref[d, rows, :] = out[(2 * d + 1) * ROWS : (2 * d + 2) * ROWS]
+        for d, t_ref in enumerate((t0, t1, t2, t3)):
+            m_ref[d, rows, :] = out[2 * d * ROWS : (2 * d + 1) * ROWS]
+            t_ref[rows, :] = out[(2 * d + 1) * ROWS : (2 * d + 2) * ROWS]
 
 
 def filter_first(halo_ref, volt_ref, band_ref, m_ref, t_ref):
@@ -164,7 +164,7 @@
     out_ref[1] = imag
 
 
-def correlate(pieces, acc, scale=None):
+def correlate(pieces, acc, scale=None, weight=1):
     frames = sum(p.shape[0] for p in pieces)
     block = pl.BlockSpec((2, 256, 256), lambda j: (0, j, 0))
     more = [] if acc is None else [acc]
@@ -176,7 +176,7 @@
         + [block] * len(more),
         out_specs=block,
         compiler_params=pltpu.CompilerParams(vmem_limit_bytes=40 << 20),
-        cost_estimate=pl.CostEstimate(flops=16 * frames * S * 512, bytes_accessed=4 << 20, transcendentals=0),
+        cost_estimate=pl.CostEstimate(flops=2 * weight * frames * S * 512, bytes_accessed=4 << 20, transcendentals=0),
     )(*pieces, *more)
 
 
@@ -205,11 +205,11 @@
         compiler_params=params,
         cost_estimate=pl.CostEstimate(flops=2 << 29, bytes_accessed=6 << 20, transcendentals=0),
     )(taps.reshape(1, -1), jnp.asarray(trig_table()), volt)
-    ma = spread(late_out[:XS])
-    halo, *ma = lax.optimization_barrier((halo, *ma))
-    ma = jnp.concatenate(ma, 0)
-    ma_near, ma_near2 = move(ma[:ROWS], near_z), move(ma[ROWS:], near_z)
-    ta = move(late_out[XS], far_z)
+    ma = late_out[XS]
+    ma_near = move(ma, near_z)
+    ta = spread(late_out[:XS])
+    halo, *ta = lax.optimization_barrier((halo, *ta))
+    ta = move(jnp.concatenate(ta, 0), far_z)
     first_out = pl.pallas_call(
         filter_first,
         out_shape=[shape(XS, ROWS, S)] * 2,
@@ -219,21 +219,18 @@
         cost_estimate=pl.CostEstimate(flops=1 << 29, bytes_accessed=3 << 20, transcendentals=0),
     )(halo, volt, band)
     mb, tb = first_out
-    mb_near = move(mb, near_z)
-    tb = move(tb, far_z)
-    ta, ma_near = lax.optimization_barrier((ta, ma_near))
-    second = spread([jnp.concatenate([ta[d], mb[d]], 0) for d in range(XS)])
-    tb, mb_near, ma_near2, *second = lax.optimization_barrier((tb, mb_near, ma_near2, *second))
-    ta = jnp.concatenate([slab[: 2 * ROWS] for slab in second], 0)
+    round_b = spread([jnp.concatenate([tb[d], mb[d], ma[d], ma_near[d]], 0) for d in range(XS)])
+    tb = move(jnp.concatenate([slab[:ROWS] for slab in round_b], 0), far_z)
+    mb = jnp.concatenate([slab[ROWS : 2 * ROWS] for slab in round_b], 0)
+    mine = jnp.concatenate([slab[ROWS:] for slab in round_b], 0)
     ta_near = move(ta, near_z)
-    third = spread([jnp.concatenate([tb[d], mb_near[d]], 0) for d in range(XS)])
-    tb_near = move(jnp.concatenate([slab[:ROWS] for slab in third], 0), near_z)
-    second, third = jnp.concatenate(second, 0), jnp.concatenate(third, 0)
-    ma = jnp.concatenate([ma, ma_near, ma_near2, second], 0)
-    acc = correlate([ma, move(ma, other_core), ta_near], None)
-    acc, ta_near, tb_near = lax.optimization_barrier((acc, ta_near, tb_near))
-    last = jnp.concatenate([tb_near, third], 0)
-    pieces = [last, move(jnp.concatenate([last, ta_near], 0), other_core)]
+    b_near = move(jnp.concatenate([mb, tb], 0), near_z)
+    acc = correlate([ta, move(ta, other_core), ta_near], None, weight=64)
+    acc = correlate([mine, move(mine, other_core)], acc)
+    ta_core = move(ta_near, other_core)
+    acc, b_near, ta_core = lax.optimization_barrier((acc, b_near, ta_core))
+    last = jnp.concatenate([b_near, tb], 0)
+    pieces = [ta_core, last, move(last, other_core)]
     frames = samples_here // FINE * XS * ZS * CORES
     return correlate(pieces, acc, 1.0 / frames)[None]
 

time: 110 us -> 107 us (0.973)
  the two profiles are of different devices: /device:TPU:1 before, /device:TPU:11 now
where the time goes in v10:
time: 107 us; the launch traced here: 106 us
  starting transfers between devices  51 us (48%)
  waiting for transfers between devices  42 us (39%)
  Pallas kernels  10.6 us (10%)
  local copies, waits for them, and re-layouts  2.19 us (2%)
    ppermute x15, starting transfers between devices, move(): return lax.ppermute(array, 'tm', moves(rule))  46.3 us
    ppermute x15, waiting for transfers between devices, move(): return lax.ppermute(array, 'tm', moves(rule))  42 us
    pallas_call x3, Pallas kernels, correlate(): pl.pallas_call(functools.partial(products, len(pieces), scale), grid=(4,)...  7.78 us
    ppermute x1, starting transfers between devices, halo_of(): return lax.ppermute(tail, 'tm', pairs)  4.69 us
  transfers between devices with their start and end apart: 16, of which 8 were waited for; matrix products, arithmetic and copies ran while one was open for 0% of the time, Pallas kernels for 6%

profile of v10, /device:TPU:11, one launch (start us, length us, event | category | flops | bytes accessed | tf_op | source)
XLA Modules:
  0.0 106.3 jit_solution(10131586155399616345)
XLA Ops:
  0.0 0.0 copy-start
  0.0 1.9 %copy-done = bf16[768,2,1,1024]{3,1,2,0:T(2,128)(2,1)S(1)} copy-done((bf16[768,2,1,1024]{3,1,2,0:T(2,128)(2,1)S(1)}, bf16[768,2,1,1024]{3,1,2,0:T(2,128)(2,1)}, u32[]{:S(2)}) %copy-start) | copy-done | bytes 3145752
  1.9 0.0 copy-start.1
  1.9 0.0 copy-start.2
  1.9 0.0 copy-start.3
  1.9 0.3 shard_map.37
  2.2 4.7 %collective-permute-start = (bf16[240,2,1024]{2,1,0:T(2,128)(2,1)S(1)}, bf16[240,2,1024]{2,1,0:T(2,128)(2,1)S(1)}, u32[]{:S(2)}, u32[]{:S(2)}) collective-permute-start(bf16[240,2,1024]{2,1,0:T(2,128)(2,1)S(1)} %shard_map.37), channel_id=1, source_target_pairs={{0,1},{1,2},{2,3},{3,4},{4,5},{5,6},{6,7},{7,8},{8,9},{9,10},{10,1... | collective-permute-start | bytes 2949128 | tf_op jit(solution)/shard_map/ppermute | solution.py:59
  6.9 0.0 copy-done.1
  6.9 0.0 copy-done.2
  6.9 0.0 copy-done.3
  6.9 1.7 %shard_map.38 = (bf16[64,1024]{1,0:T(8,128)(2,1)S(1)}, bf16[64,1024]{1,0:T(8,128)(2,1)S(1)}, bf16[64,1024]{1,0:T(8,128)(2,1)S(1)}, bf16[64,1024]{1,0:T(8,128)(2,...) custom-call(f32[1,256]{1,0:T(1,128)S(1)} %bitcast.41, f32[16,1024]{1,0:T(8,128)S(1)} %copy-done.3, ...), custom_call_target="tpu_custom_call" | custom-call | flops 1073741824 | bytes 6291456 | tf_op jit(solution)/shard_map/pallas_call | solution.py:200
  8.7 4.0 %collective-permute-start.4 = (bf16[4,64,1024]{2,1,0:T(8,128)(2,1)S(1)}, bf16[4,64,1024]{2,1,0:T(8,128)(2,1)S(1)}, u32[]{:S(2)}, u32[]{:S(2)}) collective-permute-start(bf16[4,64,1024]{2,1,0:T(8,128)(2,1)S(1)} %get-tuple-element.28), channel_id=1, source_target_pairs={{0,2},{1,3},{2,0},{3,1},{4,6},{5,7},{6,4},{7,5},{8,10},{9,11},{10,... | collective-permute-start | bytes 1572872 | tf_op jit(solution)/shard_map/ppermute | solution.py:38
  12.7 3.1 %collective-permute-start.1 = (bf16[64,1024]{1,0:T(8,128)(2,1)S(1)}, bf16[64,1024]{1,0:T(8,128)(2,1)S(1)}, u32[]{:S(2)}, u32[]{:S(2)}) collective-permute-start(bf16[64,1024]{1,0:T(8,128)(2,1)S(1)} %get-tuple-element.22), channel_id=1, source_target_pairs={{0,8},{1,9},{2,10},{3,11},{4,12},{5,13},{6,14},{7,15},{8,16},{9,17... | collective-permute-start | bytes 393224 | tf_op jit(solution)/shard_map/ppermute | solution.py:38
  15.8 2.7 %collective-permute-start.2 = (bf16[64,1024]{1,0:T(8,128)(2,1)S(1)}, bf16[64,1024]{1,0:T(8,128)(2,1)S(1)}, u32[]{:S(2)}, u32[]{:S(2)}) collective-permute-start(bf16[64,1024]{1,0:T(8,128)(2,1)S(1)} %get-tuple-element.23), channel_id=1, source_target_pairs={{0,16},{1,17},{2,18},{3,19},{4,20},{5,21},{6,22},{7,23},{8,24},{9,... | collective-permute-start | bytes 393224 | tf_op jit(solution)/shard_map/ppermute | solution.py:38
  18.6 3.8 %collective-permute-start.3 = (bf16[64,1024]{1,0:T(8,128)(2,1)S(1)}, bf16[64,1024]{1,0:T(8,128)(2,1)S(1)}, u32[]{:S(2)}, u32[]{:S(2)}) collective-permute-start(bf16[64,1024]{1,0:T(8,128)(2,1)S(1)} %get-tuple-element.24), channel_id=1, source_target_pairs={{0,24},{1,25},{2,26},{3,27},{4,28},{5,29},{6,30},{7,31},{8,0},{9,1... | collective-permute-start | bytes 393224 | tf_op jit(solution)/shard_map/ppermute | solution.py:38
  22.4 10.5 %collective-permute-done.4 = bf16[4,64,1024]{2,1,0:T(8,128)(2,1)S(1)} collective-permute-done((bf16[4,64,1024]{2,1,0:T(8,128)(2,1)S(1)}, bf16[4,64,1024]{2,1,0:T(8,128)(2,1)S(1)}, u32[]{:S(2)}, u32[]{:S(2)}) %collective-permute-start.4) | collective-permute-done | bytes 524320 | tf_op jit(solution)/shard_map/ppermute | solution.py:38
  32.9 0.0 collective-permute-done.1
  32.9 0.0 collective-permute-done.2
  32.9 0.0 collective-permute-done.3
  32.9 0.0 collective-permute-done.halo_ref
  32.9 0.8 shard_map.39
  33.8 2.1 %collective-permute-start.9 = (bf16[256,1024]{1,0:T(8,128)(2,1)S(1)}, bf16[256,1024]{1,0:T(8,128)(2,1)S(1)}, u32[]{:S(2)}, u32[]{:S(2)}) collective-permute-start(bf16[256,1024]{1,0:T(8,128)(2,1)S(1)} %pad_maximum_fusion), channel_id=1, source_target_pairs={{0,4},{1,5},{2,6},{3,7},{4,0},{5,1},{6,2},{7,3},{8,12},{9,13},{10,... | collective-permute-start | bytes 1572872 | tf_op jit(solution)/shard_map/ppermute | solution.py:38
  36.0 3.1 %collective-permute-start.5 = (bf16[192,1024]{1,0:T(8,128)(2,1)S(1)}, bf16[192,1024]{1,0:T(8,128)(2,1)S(1)}, u32[]{:S(2)}, u32[]{:S(2)}) collective-permute-start(bf16[192,1024]{1,0:T(8,128)(2,1)S(1)} %pad_maximum_fusion.1), channel_id=1, source_target_pairs={{0,8},{1,9},{2,10},{3,11},{4,12},{5,13},{6,14},{7,15},{8,16},{9,17... | collective-permute-start | bytes 1179656 | tf_op jit(solution)/shard_map/ppermute | solution.py:38
  39.1 2.7 %collective-permute-start.6 = (bf16[192,1024]{1,0:T(8,128)(2,1)S(1)}, bf16[192,1024]{1,0:T(8,128)(2,1)S(1)}, u32[]{:S(2)}, u32[]{:S(2)}) collective-permute-start(bf16[192,1024]{1,0:T(8,128)(2,1)S(1)} %pad_maximum_fusion.2), channel_id=1, source_target_pairs={{0,16},{1,17},{2,18},{3,19},{4,20},{5,21},{6,22},{7,23},{8,24},{9,... | collective-permute-start | bytes 1179656 | tf_op jit(solution)/shard_map/ppermute | solution.py:38
  41.9 3.8 %collective-permute-start.7 = (bf16[192,1024]{1,0:T(8,128)(2,1)S(1)}, bf16[192,1024]{1,0:T(8,128)(2,1)S(1)}, u32[]{:S(2)}, u32[]{:S(2)}) collective-permute-start(bf16[192,1024]{1,0:T(8,128)(2,1)S(1)} %pad_maximum_fusion.3), channel_id=1, source_target_pairs={{0,24},{1,25},{2,26},{3,27},{4,28},{5,29},{6,30},{7,31},{8,0},{9,1... | collective-permute-start | bytes 1179656 | tf_op jit(solution)/shard_map/ppermute | solution.py:38
  45.7 2.6 %collective-permute-done.5 = bf16[192,1024]{1,0:T(8,128)(2,1)S(1)} collective-permute-done((bf16[192,1024]{1,0:T(8,128)(2,1)S(1)}, bf16[192,1024]{1,0:T(8,128)(2,1)S(1)}, u32[]{:S(2)}, u32[]{:S(2)}) %collective-permute-start.5) | collective-permute-done | bytes 393248 | tf_op jit(solution)/shard_map/ppermute | solution.py:38
  48.4 4.4 %collective-permute-done.6 = bf16[192,1024]{1,0:T(8,128)(2,1)S(1)} collective-permute-done((bf16[192,1024]{1,0:T(8,128)(2,1)S(1)}, bf16[192,1024]{1,0:T(8,128)(2,1)S(1)}, u32[]{:S(2)}, u32[]{:S(2)}) %collective-permute-start.6) | collective-permute-done | bytes 393248 | tf_op jit(solution)/shard_map/ppermute | solution.py:38
  52.8 9.2 %collective-permute-done.7 = bf16[192,1024]{1,0:T(8,128)(2,1)S(1)} collective-permute-done((bf16[192,1024]{1,0:T(8,128)(2,1)S(1)}, bf16[192,1024]{1,0:T(8,128)(2,1)S(1)}, u32[]{:S(2)}, u32[]{:S(2)}) %collective-permute-start.7) | collective-permute-done | bytes 393248 | tf_op jit(solution)/shard_map/ppermute | solution.py:38
  62.0 4.1 %collective-permute-start.12 = (bf16[128,1024]{1,0:T(8,128)(2,1)S(1)}, bf16[128,1024]{1,0:T(8,128)(2,1)S(1)}, u32[]{:S(2)}, u32[]{:S(2)}) collective-permute-start(bf16[128,1024]{1,0:T(8,128)(2,1)S(1)} %pad_maximum_fusion.4), channel_id=1, source_target_pairs={{0,4},{1,5},{2,6},{3,7},{4,0},{5,1},{6,2},{7,3},{8,12},{9,13},{10,... | collective-permute-start | bytes 786440 | tf_op jit(solution)/shard_map/ppermute | solution.py:38
  66.2 0.0 collective-permute-done.9.refs_0_
  66.2 1.9 %collective-permute-start.11 = (bf16[256,1024]{1,0:T(8,128)(2,1)S(1)}, bf16[256,1024]{1,0:T(8,128)(2,1)S(1)}, u32[]{:S(2)}, u32[]{:S(2)}) collective-permute-start(bf16[256,1024]{1,0:T(8,128)(2,1)S(1)} %collective-permute-done.9.refs_0_), channel_id=1, source_target_pairs={{0,2},{1,3},{2,0},{3,1},{4,6},{5,7},{6,4},{7,5},{8,10},{9,11},{10,... | collective-permute-start | bytes 1572872 | tf_op jit(solution)/shard_map/ppermute | solution.py:38
  68.1 2.7 %collective-permute-start.10 = (bf16[256,1024]{1,0:T(8,128)(2,1)S(1)}, bf16[256,1024]{1,0:T(8,128)(2,1)S(1)}, u32[]{:S(2)}, u32[]{:S(2)}) collective-permute-start(bf16[256,1024]{1,0:T(8,128)(2,1)S(1)} %collective-permute-done.9.refs_0_), channel_id=1, source_target_pairs={{0,1},{1,0},{2,3},{3,2},{4,5},{5,4},{6,7},{7,6},{8,9},{9,8},{10,11... | collective-permute-start | bytes 1572872 | tf_op jit(solution)/shard_map/ppermute | solution.py:38
  70.9 1.9 %collective-permute-start.8 = (bf16[640,1024]{1,0:T(8,128)(2,1)S(1)}, bf16[640,1024]{1,0:T(8,128)(2,1)S(1)}, u32[]{:S(2)}, u32[]{:S(2)}) collective-permute-start(bf16[640,1024]{1,0:T(8,128)(2,1)S(1)} %slice_dynamic-update-slice_fusion.refs_0_), channel_id=1, source_target_pairs={{0,1},{1,0},{2,3},{3,2},{4,5},{5,4},{6,7},{7,6},{8,9},{9,8},{10,11... | collective-permute-start | bytes 3932168 | tf_op jit(solution)/shard_map/ppermute | solution.py:38
  72.8 5.9 %collective-permute-done.12 = bf16[128,1024]{1,0:T(8,128)(2,1)S(1)} collective-permute-done((bf16[128,1024]{1,0:T(8,128)(2,1)S(1)}, bf16[128,1024]{1,0:T(8,128)(2,1)S(1)}, u32[]{:S(2)}, u32[]{:S(2)}) %collective-permute-start.12) | collective-permute-done | bytes 262176 | tf_op jit(solution)/shard_map/ppermute | solution.py:38
  78.7 1.9 %collective-permute-start.13 = (bf16[256,1024]{1,0:T(8,128)(2,1)S(1)}, bf16[256,1024]{1,0:T(8,128)(2,1)S(1)}, u32[]{:S(2)}, u32[]{:S(2)}) collective-permute-start(bf16[256,1024]{1,0:T(8,128)(2,1)S(1)} %constant_dynamic-update-slice_fusion), channel_id=1, source_target_pairs={{0,2},{1,3},{2,0},{3,1},{4,6},{5,7},{6,4},{7,5},{8,10},{9,11},{10,... | collective-permute-start | bytes 1572872 | tf_op jit(solution)/shard_map/ppermute | solution.py:38
  80.6 5.6 %collective-permute-done.11.refs_2_ = bf16[256,1024]{1,0:T(8,128)(2,1)S(1)} collective-permute-done((bf16[256,1024]{1,0:T(8,128)(2,1)S(1)}, bf16[256,1024]{1,0:T(8,128)(2,1)S(1)}, u32[]{:S(2)}, u32[]{:S(2)}) %collective-permute-start.11) | collective-permute-done | bytes 524320 | tf_op jit(solution)/shard_map/ppermute | solution.py:38
  86.3 4.8 %collective-permute-start.14 = (bf16[256,1024]{1,0:T(8,128)(2,1)S(1)}, bf16[256,1024]{1,0:T(8,128)(2,1)S(1)}, u32[]{:S(2)}, u32[]{:S(2)}) collective-permute-start(bf16[256,1024]{1,0:T(8,128)(2,1)S(1)} %collective-permute-done.11.refs_2_), channel_id=1, source_target_pairs={{0,1},{1,0},{2,3},{3,2},{4,5},{5,4},{6,7},{7,6},{8,9},{9,8},{10,11... | collective-permute-start | bytes 1572872 | tf_op jit(solution)/shard_map/ppermute | solution.py:38
  91.1 0.0 collective-permute-done.10.refs_1_
  91.1 1.7 %shard_map.40.refs_2_ = f32[2,1024,256]{2,1,0:T(8,128)S(1)} custom-call(bf16[256,1024]{1,0:T(8,128)(2,1)S(1)} %collective-permute-done.9.refs_0_, bf16[256,1024]{1,0:T(8,128)(2,1)S(1)} %collective-permute-done.10.refs_1_, bf16[256,1024]{1,0:T(8,128)(2,1)S(1)} %collective-permute-done.11.refs_2_), custom_call_target="tpu_custom_call" | custom-call | flops 51539607552 | bytes 4194304 | tf_op jit(solution)/shard_map/pallas_call | solution.py:171
  92.8 0.0 collective-permute-done.8.refs_1_
  92.9 2.7 %shard_map.41.refs_3_ = f32[2,1024,256]{2,1,0:T(8,128)S(1)} custom-call(bf16[640,1024]{1,0:T(8,128)(2,1)S(1)} %slice_dynamic-update-slice_fusion.refs_0_, bf16[640,1024]{1,0:T(8,128)(2,1)S(1)} %collective-permute-done.8.refs_1_, f32[2,1024,256]{2,1,0:T(8,128)S(1)} %shard_map.40.refs_2_), custom_call_target="tpu_custom_call" | custom-call | flops 1342177280 | bytes 4194304 | tf_op jit(solution)/shard_map/pallas_call | solution.py:171
  95.6 1.9 %collective-permute-done.13 = bf16[256,1024]{1,0:T(8,128)(2,1)S(1)} collective-permute-done((bf16[256,1024]{1,0:T(8,128)(2,1)S(1)}, bf16[256,1024]{1,0:T(8,128)(2,1)S(1)}, u32[]{:S(2)}, u32[]{:S(2)}) %collective-permute-start.13) | collective-permute-done | bytes 524320 | tf_op jit(solution)/shard_map/ppermute | solution.py:38
  97.5 0.0 collective-permute-done.14.refs_0_
  97.6 3.6 %collective-permute-start.15 = (bf16[384,1024]{1,0:T(8,128)(2,1)S(1)}, bf16[384,1024]{1,0:T(8,128)(2,1)S(1)}, u32[]{:S(2)}, u32[]{:S(2)}) collective-permute-start(bf16[384,1024]{1,0:T(8,128)(2,1)S(1)} %constant_dynamic-update-slice_fusion.1.refs_1_), channel_id=1, source_target_pairs={{0,1},{1,0},{2,3},{3,2},{4,5},{5,4},{6,7},{7,6},{8,9},{9,8},{10,11... | collective-permute-start | bytes 2359304 | tf_op jit(solution)/shard_map/ppermute | solution.py:38
  101.1 1.9 %collective-permute-done.15.refs_2_ = bf16[384,1024]{1,0:T(8,128)(2,1)S(1)} collective-permute-done((bf16[384,1024]{1,0:T(8,128)(2,1)S(1)}, bf16[384,1024]{1,0:T(8,128)(2,1)S(1)}, u32[]{:S(2)}, u32[]{:S(2)}) %collective-permute-start.15) | collective-permute-done | bytes 786464 | tf_op jit(solution)/shard_map/ppermute | solution.py:38
  103.0 3.3 %shard_map.42 = f32[2,1024,256]{2,1,0:T(8,128)} custom-call(bf16[256,1024]{1,0:T(8,128)(2,1)S(1)} %collective-permute-done.14.refs_0_, bf16[384,1024]{1,0:T(8,128)(2,1)S(1)} %constant_dynamic-update-slice_fusion.1.refs_1_, bf16[384,1024]{1,0:T(8,128)(2,1)S(1)} %collective-permute-done.15.refs_2_, f32[2,1024,256]{2,1,0:T(8,128)S(1)} %shard_map.41.refs_3_), custom_call_target="tpu_custom_call" | custom-call | flops 1073741824 | bytes 4194304 | tf_op jit(solution)/shard_map/pallas_call | solution.py:171
  (20 shorter events, 0.4 us)
Async XLA Ops:
  0.0 1.9 %copy-start = (bf16[768,2,1,1024]{3,1,2,0:T(2,128)(2,1)S(1)}, bf16[768,2,1,1024]{3,1,2,0:T(2,128)(2,1)}, u32[]{:S(2)}) copy-start(bf16[768,2,1,1024]{3,1,2,0:T(2,128)(2,1)} %param.3) | copy-start | bytes 9437188
  1.9 5.0 %copy-start.1 = (bf16[768,2,1,1024]{3,1,2,0:T(2,128)(2,1)S(1)}, bf16[768,2,1,1024]{3,1,2,0:T(2,128)(2,1)}, u32[]{:S(2)}) copy-start(bf16[768,2,1,1024]{3,1,2,0:T(2,128)(2,1)} %param.3) | copy-start | bytes 9437188
  1.9 5.0 %copy-start.2 = (f32[256]{0:T(256)S(1)}, f32[256]{0:T(256)}, u32[]{:S(2)}) copy-start(f32[256]{0:T(256)} %param.4) | copy-start | bytes 3076
  1.9 5.0 %copy-start.3 = (f32[16,1024]{1,0:T(8,128)S(1)}, f32[16,1024]{1,0:T(8,128)}, u32[]{:S(2)}) copy-start(f32[16,1024]{1,0:T(8,128)} %constant.2.clone.trig_ref) | copy-start | bytes 196612
  2.2 30.7 %collective-permute-start = (bf16[240,2,1024]{2,1,0:T(2,128)(2,1)S(1)}, bf16[240,2,1024]{2,1,0:T(2,128)(2,1)S(1)}, u32[]{:S(2)}, u32[]{:S(2)}) collective-permute-start(bf16[240,2,1024]{2,1,0:T(2,128)(2,1)S(1)} %shard_map.37), channel_id=1, source_target_pairs={{0,1},{1,2},{2,3},{3,4},{4,5},{5,6},{6,7},{7,8},{8,9},{9,10},{10,1... | collective-permute-start | bytes 2949128 | tf_op jit(solution)/shard_map/ppermute | solution.py:59
  8.7 24.2 %collective-permute-start.4 = (bf16[4,64,1024]{2,1,0:T(8,128)(2,1)S(1)}, bf16[4,64,1024]{2,1,0:T(8,128)(2,1)S(1)}, u32[]{:S(2)}, u32[]{:S(2)}) collective-permute-start(bf16[4,64,1024]{2,1,0:T(8,128)(2,1)S(1)} %get-tuple-element.28), channel_id=1, source_target_pairs={{0,2},{1,3},{2,0},{3,1},{4,6},{5,7},{6,4},{7,5},{8,10},{9,11},{10,... | collective-permute-start | bytes 1572872 | tf_op jit(solution)/shard_map/ppermute | solution.py:38
  12.7 20.2 %collective-permute-start.1 = (bf16[64,1024]{1,0:T(8,128)(2,1)S(1)}, bf16[64,1024]{1,0:T(8,128)(2,1)S(1)}, u32[]{:S(2)}, u32[]{:S(2)}) collective-permute-start(bf16[64,1024]{1,0:T(8,128)(2,1)S(1)} %get-tuple-element.22), channel_id=1, source_target_pairs={{0,8},{1,9},{2,10},{3,11},{4,12},{5,13},{6,14},{7,15},{8,16},{9,17... | collective-permute-start | bytes 393224 | tf_op jit(solution)/shard_map/ppermute | solution.py:38
  15.8 17.1 %collective-permute-start.2 = (bf16[64,1024]{1,0:T(8,128)(2,1)S(1)}, bf16[64,1024]{1,0:T(8,128)(2,1)S(1)}, u32[]{:S(2)}, u32[]{:S(2)}) collective-permute-start(bf16[64,1024]{1,0:T(8,128)(2,1)S(1)} %get-tuple-element.23), channel_id=1, source_target_pairs={{0,16},{1,17},{2,18},{3,19},{4,20},{5,21},{6,22},{7,23},{8,24},{9,... | collective-permute-start | bytes 393224 | tf_op jit(solution)/shard_map/ppermute | solution.py:38
  18.6 14.3 %collective-permute-start.3 = (bf16[64,1024]{1,0:T(8,128)(2,1)S(1)}, bf16[64,1024]{1,0:T(8,128)(2,1)S(1)}, u32[]{:S(2)}, u32[]{:S(2)}) collective-permute-start(bf16[64,1024]{1,0:T(8,128)(2,1)S(1)} %get-tuple-element.24), channel_id=1, source_target_pairs={{0,24},{1,25},{2,26},{3,27},{4,28},{5,29},{6,30},{7,31},{8,0},{9,1... | collective-permute-start | bytes 393224 | tf_op jit(solution)/shard_map/ppermute | solution.py:38
  33.8 32.3 %collective-permute-start.9 = (bf16[256,1024]{1,0:T(8,128)(2,1)S(1)}, bf16[256,1024]{1,0:T(8,128)(2,1)S(1)}, u32[]{:S(2)}, u32[]{:S(2)}) collective-permute-start(bf16[256,1024]{1,0:T(8,128)(2,1)S(1)} %pad_maximum_fusion), channel_id=1, source_target_pairs={{0,4},{1,5},{2,6},{3,7},{4,0},{5,1},{6,2},{7,3},{8,12},{9,13},{10,... | collective-permute-start | bytes 1572872 | tf_op jit(solution)/shard_map/ppermute | solution.py:38
  36.0 12.4 %collective-permute-start.5 = (bf16[192,1024]{1,0:T(8,128)(2,1)S(1)}, bf16[192,1024]{1,0:T(8,128)(2,1)S(1)}, u32[]{:S(2)}, u32[]{:S(2)}) collective-permute-start(bf16[192,1024]{1,0:T(8,128)(2,1)S(1)} %pad_maximum_fusion.1), channel_id=1, source_target_pairs={{0,8},{1,9},{2,10},{3,11},{4,12},{5,13},{6,14},{7,15},{8,16},{9,17... | collective-permute-start | bytes 1179656 | tf_op jit(solution)/shard_map/ppermute | solution.py:38
  39.1 13.6 %collective-permute-start.6 = (bf16[192,1024]{1,0:T(8,128)(2,1)S(1)}, bf16[192,1024]{1,0:T(8,128)(2,1)S(1)}, u32[]{:S(2)}, u32[]{:S(2)}) collective-permute-start(bf16[192,1024]{1,0:T(8,128)(2,1)S(1)} %pad_maximum_fusion.2), channel_id=1, source_target_pairs={{0,16},{1,17},{2,18},{3,19},{4,20},{5,21},{6,22},{7,23},{8,24},{9,... | collective-permute-start | bytes 1179656 | tf_op jit(solution)/shard_map/ppermute | solution.py:38
  41.9 20.1 %collective-permute-start.7 = (bf16[192,1024]{1,0:T(8,128)(2,1)S(1)}, bf16[192,1024]{1,0:T(8,128)(2,1)S(1)}, u32[]{:S(2)}, u32[]{:S(2)}) collective-permute-start(bf16[192,1024]{1,0:T(8,128)(2,1)S(1)} %pad_maximum_fusion.3), channel_id=1, source_target_pairs={{0,24},{1,25},{2,26},{3,27},{4,28},{5,29},{6,30},{7,31},{8,0},{9,1... | collective-permute-start | bytes 1179656 | tf_op jit(solution)/shard_map/ppermute | solution.py:38
  62.0 16.6 %collective-permute-start.12 = (bf16[128,1024]{1,0:T(8,128)(2,1)S(1)}, bf16[128,1024]{1,0:T(8,128)(2,1)S(1)}, u32[]{:S(2)}, u32[]{:S(2)}) collective-permute-start(bf16[128,1024]{1,0:T(8,128)(2,1)S(1)} %pad_maximum_fusion.4), channel_id=1, source_target_pairs={{0,4},{1,5},{2,6},{3,7},{4,0},{5,1},{6,2},{7,3},{8,12},{9,13},{10,... | collective-permute-start | bytes 786440 | tf_op jit(solution)/shard_map/ppermute | solution.py:38
  66.2 20.1 %collective-permute-start.11 = (bf16[256,1024]{1,0:T(8,128)(2,1)S(1)}, bf16[256,1024]{1,0:T(8,128)(2,1)S(1)}, u32[]{:S(2)}, u32[]{:S(2)}) collective-permute-start(bf16[256,1024]{1,0:T(8,128)(2,1)S(1)} %collective-permute-done.9.refs_0_), channel_id=1, source_target_pairs={{0,2},{1,3},{2,0},{3,1},{4,6},{5,7},{6,4},{7,5},{8,10},{9,11},{10,... | collective-permute-start | bytes 1572872 | tf_op jit(solution)/shard_map/ppermute | solution.py:38
  68.1 23.0 %collective-permute-start.10 = (bf16[256,1024]{1,0:T(8,128)(2,1)S(1)}, bf16[256,1024]{1,0:T(8,128)(2,1)S(1)}, u32[]{:S(2)}, u32[]{:S(2)}) collective-permute-start(bf16[256,1024]{1,0:T(8,128)(2,1)S(1)} %collective-permute-done.9.refs_0_), channel_id=1, source_target_pairs={{0,1},{1,0},{2,3},{3,2},{4,5},{5,4},{6,7},{7,6},{8,9},{9,8},{10,11... | collective-permute-start | bytes 1572872 | tf_op jit(solution)/shard_map/ppermute | solution.py:38
  70.9 22.0 %collective-permute-start.8 = (bf16[640,1024]{1,0:T(8,128)(2,1)S(1)}, bf16[640,1024]{1,0:T(8,128)(2,1)S(1)}, u32[]{:S(2)}, u32[]{:S(2)}) collective-permute-start(bf16[640,1024]{1,0:T(8,128)(2,1)S(1)} %slice_dynamic-update-slice_fusion.refs_0_), channel_id=1, source_target_pairs={{0,1},{1,0},{2,3},{3,2},{4,5},{5,4},{6,7},{7,6},{8,9},{9,8},{10,11... | collective-permute-start | bytes 3932168 | tf_op jit(solution)/shard_map/ppermute | solution.py:38
  78.7 18.8 %collective-permute-start.13 = (bf16[256,1024]{1,0:T(8,128)(2,1)S(1)}, bf16[256,1024]{1,0:T(8,128)(2,1)S(1)}, u32[]{:S(2)}, u32[]{:S(2)}) collective-permute-start(bf16[256,1024]{1,0:T(8,128)(2,1)S(1)} %constant_dynamic-update-slice_fusion), channel_id=1, source_target_pairs={{0,2},{1,3},{2,0},{3,1},{4,6},{5,7},{6,4},{7,5},{8,10},{9,11},{10,... | collective-permute-start | bytes 1572872 | tf_op jit(solution)/shard_map/ppermute | solution.py:38
  86.3 11.2 %collective-permute-start.14 = (bf16[256,1024]{1,0:T(8,128)(2,1)S(1)}, bf16[256,1024]{1,0:T(8,128)(2,1)S(1)}, u32[]{:S(2)}, u32[]{:S(2)}) collective-permute-start(bf16[256,1024]{1,0:T(8,128)(2,1)S(1)} %collective-permute-done.11.refs_2_), channel_id=1, source_target_pairs={{0,1},{1,0},{2,3},{3,2},{4,5},{5,4},{6,7},{7,6},{8,9},{9,8},{10,11... | collective-permute-start | bytes 1572872 | tf_op jit(solution)/shard_map/ppermute | solution.py:38
  97.6 5.5 %collective-permute-start.15 = (bf16[384,1024]{1,0:T(8,128)(2,1)S(1)}, bf16[384,1024]{1,0:T(8,128)(2,1)S(1)}, u32[]{:S(2)}, u32[]{:S(2)}) collective-permute-start(bf16[384,1024]{1,0:T(8,128)(2,1)S(1)} %constant_dynamic-update-slice_fusion.1.refs_1_), channel_id=1, source_target_pairs={{0,1},{1,0},{2,3},{3,2},{4,5},{5,4},{6,7},{7,6},{8,9},{9,8},{10,11... | collective-permute-start | bytes 2359304 | tf_op jit(solution)/shard_map/ppermute | solution.py:38
